TPU v7x, 128 devices: a whole 4x4x4 slice. The times are simulated.
128 devices in a mesh: sample: 16 (over z_lo, y, core), token: 8 (over x, z_hi).
Axes of the slice: x: 4, y: 4, z: 4 (z_hi: 2, z_lo: 2; z = z_hi * 2 + z_lo), core: 2. Of those that a mesh axis runs over, the one named last changes fastest.
Arguments:
- activations: bfloat16 [32, 1024, 768], P('sample', 'token'), may hold values from -100 to 100
- levels: int32 [32], P('sample'), may hold values from 0 to 199
- ada_table: bfloat16 [200, 1536], replicated, may hold values from -1.796875 to 1.796875
- input_weight: bfloat16 [768, 3072], replicated, may hold values from -0.21875 to 0.21875
- output_matrix: bfloat16 [768, 768], replicated, may hold values from -0.21875 to 0.21875
- pair_feats: bfloat16 [1024, 1024, 128], P('token', 'sample'), may hold values from -51 to 51
- pair_weight: bfloat16 [128, 16], replicated, as said below
- cross_bias: float32 [16], replicated, may hold values from -2 to 2
- chains: int32 [1024], replicated, may hold values from 0 to 7, never falling along the last dimension, each value on 1 to 512 neighbouring positions
- cotangent: bfloat16 [32, 1024, 768], P('sample', 'token'), may hold values from -6 to 6
Outputs:
- updated: bfloat16 [32, 1024, 768], P('sample', 'token')
- grad_tokens: bfloat16 [32, 1024, 768], P('sample', 'token')
- grad_pair: bfloat16 [1024, 1024, 128], P('token', 'sample')
- input_weight_grad: float32 [768, 3072], replicated
- output_weight_grad: float32 [768, 768], replicated
- grad_pair_weight: float32 [128, 16], replicated
- grad_cross: float32 [16], replicated
- grad_table: float32 [200, 1536], replicated
Inputs may be any that keep to these rules, and one draw needn't show every extreme that they name: `chains`: chain ids never fall along the tokens. `pair_weight`: entries lie within 4 / sqrt(128) of zero.
All inputs are finite; a program needn't handle non-finite values.
Results may differ from a plain program's by a relative error of at most 0.035.
Values may be sent and summed in bfloat16 or wider, within the bound.
No kernel may reach another device: no remote copies, remote signals or barrier semaphores. Data moves between devices by JAX's collectives and lax.ppermute only.
A program may use at most 192 MiB of HBM per device.

v0:
```python
import math

import jax
import jax.numpy as jnp
from jax import lax
from jax.sharding import PartitionSpec as P

norm_epsilon = 1e-05
highest = lax.Precision.HIGHEST


def attend_sample(query_heads, key_heads, value_heads, grad_heads, fixed_bias):
    logits = (
        jnp.einsum("jhd,ihd->hji", key_heads, query_heads, preferred_element_type=jnp.float32)
        + fixed_bias
    )
    row_peak = jnp.max(logits, axis=1, keepdims=True)
    exp_terms = jnp.exp(logits - row_peak)
    weights_full = exp_terms / jnp.sum(exp_terms, axis=1, keepdims=True)
    weights_half = weights_full.astype(jnp.bfloat16)
    attended = jnp.einsum(
        "hji,jhd->ihd", weights_half, value_heads, preferred_element_type=jnp.float32
    )
    delta_sum = jnp.sum(grad_heads.astype(jnp.float32) * attended, axis=2)
    grad_weights = jnp.einsum(
        "ihd,jhd->hji", grad_heads, value_heads, preferred_element_type=jnp.float32
    )
    grad_logits = (weights_full * (grad_weights - jnp.transpose(delta_sum)[:, None, :])).astype(
        jnp.bfloat16
    )
    query_rows_grad = jnp.einsum(
        "hji,jhd->ihd", grad_logits, key_heads, preferred_element_type=jnp.float32
    )
    key_rows_grad = jnp.einsum(
        "hji,ihd->jhd", grad_logits, query_heads, preferred_element_type=jnp.float32
    )
    value_rows_grad = jnp.einsum(
        "hji,ihd->jhd", weights_half, grad_heads, preferred_element_type=jnp.float32
    )
    return (attended, query_rows_grad, key_rows_grad, value_rows_grad, grad_logits)


def shards(
    activations,
    levels,
    ada_table,
    input_weight,
    output_matrix,
    pair_feats,
    pair_weight,
    cross_bias,
    chains,
    cotangent,
):
    sample_count, row_count, feature_width = activations.shape
    head_count = pair_weight.shape[1]
    head_size = feature_width // head_count
    col_count = pair_feats.shape[1]
    key_count = row_count * lax.axis_size("token")
    level_count = ada_table.shape[0]
    factor = 1.0 / math.sqrt(head_size)
    onehot = (
        levels[:, None] == lax.broadcasted_iota(jnp.int32, (sample_count, level_count), 1)
    ).astype(jnp.float32)
    modulation = jnp.dot(onehot, ada_table.astype(jnp.float32), precision=highest)
    ada_scale = 1.0 + modulation[:, None, :feature_width]
    ada_shift = modulation[:, None, feature_width:]
    input_broadcast = activations.astype(jnp.float32)
    row_mean = jnp.mean(input_broadcast, axis=2, keepdims=True)
    centred = input_broadcast - row_mean
    inv_std = lax.rsqrt(jnp.mean(centred * centred, axis=2, keepdims=True) + norm_epsilon)
    whitened = centred * inv_std
    layer_normalized = (whitened * ada_scale + ada_shift).astype(jnp.bfloat16)
    pair_part = jnp.einsum(
        "ijc,ch->hji", pair_feats, pair_weight, preferred_element_type=jnp.float32
    )
    pair_bias = lax.all_gather(pair_part, "sample", axis=1, tiled=True)
    own_chain = lax.dynamic_slice_in_dim(chains, lax.axis_index("token") * row_count, row_count)
    query_weight = input_weight[:, :feature_width]
    key_value_weight = input_weight[:, feature_width : 3 * feature_width]
    gate_weight = input_weight[:, 3 * feature_width :]
    key_value_full = key_value_weight.astype(jnp.float32)
    query = (
        jnp.einsum(
            "sqd,de->sqe", layer_normalized, query_weight, preferred_element_type=jnp.float32
        )
        * factor
    ).astype(jnp.bfloat16)
    gate_open = jax.nn.sigmoid(
        jnp.einsum("sqd,de->sqe", layer_normalized, gate_weight, preferred_element_type=jnp.float32)
    )
    grad_gate_applied = jnp.einsum(
        "sqe,de->sqd", cotangent, output_matrix, preferred_element_type=jnp.float32
    )
    grad_attend = (grad_gate_applied * gate_open).astype(jnp.bfloat16)
    differ = (chains[:, None] != own_chain[None, :]).astype(jnp.float32)
    fixed_bias = pair_bias + cross_bias[:, None, None] * differ[None]
    key_value_own = jnp.einsum(
        "sqd,de->sqe", layer_normalized, key_value_weight, preferred_element_type=jnp.float32
    ).astype(jnp.bfloat16)
    key_value = lax.all_gather(key_value_own, "token", axis=1, tiled=True)
    query_heads = query.reshape(sample_count, row_count, head_count, head_size)
    grad_heads = grad_attend.reshape(sample_count, row_count, head_count, head_size)
    key_heads = key_value[..., :feature_width].reshape(
        sample_count, key_count, head_count, head_size
    )
    value_heads = key_value[..., feature_width:].reshape(
        sample_count, key_count, head_count, head_size
    )
    attended_list = []
    query_grad_list = []
    key_grad_list = []
    value_grad_list = []
    bias_term = jnp.zeros(fixed_bias.shape, jnp.float32)
    for sample in range(sample_count):
        attended, query_rows_grad, key_rows_grad, value_rows_grad, grad_logits = attend_sample(
            query_heads[sample],
            key_heads[sample],
            value_heads[sample],
            grad_heads[sample],
            fixed_bias,
        )
        attended_list.append(attended)
        query_grad_list.append(query_rows_grad)
        key_grad_list.append(key_rows_grad)
        value_grad_list.append(value_rows_grad)
        bias_term = bias_term + grad_logits.astype(jnp.float32)
    attended_all = jnp.stack(attended_list).reshape(sample_count, row_count, feature_width)
    grad_query_all = (
        (jnp.stack(query_grad_list) * factor)
        .astype(jnp.bfloat16)
        .reshape(sample_count, row_count, feature_width)
    )
    grad_key_value = jnp.concatenate(
        [
            jnp.stack(key_grad_list).reshape(sample_count, key_count, feature_width),
            jnp.stack(value_grad_list).reshape(sample_count, key_count, feature_width),
        ],
        axis=2,
    )
    grad_bias = lax.psum_scatter(bias_term, "sample", scatter_dimension=1, tiled=True)
    grad_key_value_own = lax.psum_scatter(grad_key_value, "token", scatter_dimension=1, tiled=True)
    grad_normed_keys = jnp.einsum(
        "sqe,de->sqd", grad_key_value_own, key_value_full, precision=highest
    )
    grad_kv_weight = jnp.einsum(
        "sqd,sqe->de", layer_normalized.astype(jnp.float32), grad_key_value_own, precision=highest
    )
    gate_applied = (gate_open * attended_all).astype(jnp.bfloat16)
    updated = (
        input_broadcast
        + jnp.einsum("sqd,de->sqe", gate_applied, output_matrix, preferred_element_type=jnp.float32)
    ).astype(jnp.bfloat16)
    grad_out_part = jnp.einsum(
        "sqd,sqe->de", gate_applied, cotangent, preferred_element_type=jnp.float32
    )
    grad_gate_logits = (grad_gate_applied * attended_all * gate_open * (1.0 - gate_open)).astype(
        jnp.bfloat16
    )
    normalized_grad = grad_normed_keys + jnp.einsum(
        "sqe,de->sqd", grad_query_all, query_weight, preferred_element_type=jnp.float32
    )
    normalized_grad = normalized_grad + jnp.einsum(
        "sqe,de->sqd", grad_gate_logits, gate_weight, preferred_element_type=jnp.float32
    )
    grad_query_weight = jnp.einsum(
        "sqd,sqe->de", layer_normalized, grad_query_all, preferred_element_type=jnp.float32
    )
    grad_gate_weight = jnp.einsum(
        "sqd,sqe->de", layer_normalized, grad_gate_logits, preferred_element_type=jnp.float32
    )
    grad_input_part = jnp.concatenate([grad_query_weight, grad_kv_weight, grad_gate_weight], axis=1)
    grad_whitened = normalized_grad * ada_scale
    grad_scale = jnp.sum(normalized_grad * whitened, axis=1)
    grad_shift = jnp.sum(normalized_grad, axis=1)
    grad_table_part = jnp.dot(
        jnp.transpose(onehot), jnp.concatenate([grad_scale, grad_shift], axis=1), precision=highest
    )
    grad_tokens = (
        cotangent.astype(jnp.float32)
        + inv_std
        * (
            grad_whitened
            - jnp.mean(grad_whitened, axis=2, keepdims=True)
            - whitened * jnp.mean(grad_whitened * whitened, axis=2, keepdims=True)
        )
    ).astype(jnp.bfloat16)
    grad_bias_half = grad_bias.astype(jnp.bfloat16)
    grad_pair = jnp.einsum(
        "hji,ch->ijc", grad_bias_half, pair_weight, preferred_element_type=jnp.float32
    ).astype(jnp.bfloat16)
    grad_pair_part = jnp.einsum(
        "ijc,hji->ch", pair_feats, grad_bias_half, preferred_element_type=jnp.float32
    )
    col_chain = lax.dynamic_slice_in_dim(chains, lax.axis_index("sample") * col_count, col_count)
    differ_own = (col_chain[:, None] != own_chain[None, :]).astype(jnp.float32)
    grad_cross_part = jnp.sum(grad_bias * differ_own[None], axis=(1, 2))
    totals = lax.psum(
        (grad_input_part, grad_out_part, grad_pair_part, grad_cross_part, grad_table_part),
        ("sample", "token"),
    )
    return (updated, grad_tokens, grad_pair, totals[0], totals[1], totals[2], totals[3], totals[4])


def solution(mesh):
    placed = (
        P("sample", "token", None),
        P("sample"),
        P(),
        P(),
        P(),
        P("token", "sample", None),
        P(),
        P(),
        P(),
        P("sample", "token", None),
    )
    return jax.shard_map(
        shards,
        mesh=mesh,
        in_specs=placed,
        out_specs=(
            P("sample", "token", None),
            P("sample", "token", None),
            P("token", "sample", None),
            P(),
            P(),
            P(),
            P(),
            P(),
        ),
        check_vma=False,
    )
```

profile of v0, /device:TPU:1, one launch (start us, length us, event | category | flops | bytes accessed | tf_op | source)
XLA Modules:
  0.0 685.4 jit_solution(10881732611625712524)
XLA Ops:
  11.1 3.6 convolution_convert_fusion
  23.0 84.3 %all-gather.3.cloned.1.call-done = bf16[2,1024,1536]{2,1,0:T(8,128)(2,1)} async-done(((bf16[2,128,1536]{2,1,0:T(8,128)(2,1)}), bf16[2,1024,1536]{2,1,0:T(8,128)(2,1)}) %all-gather.3.cloned.1.call-update) | async-done | bytes 6291472 | tf_op jit(solution)/shard_map/all_gather | solution.py:101
  107.3 5.7 fusion.78
  123.7 36.0 %all-gather.5.cloned.1.call-done = f32[16,1024,128]{2,1,0:T(8,128)} async-done(((f32[16,64,128]{2,1,0:T(8,128)}), f32[16,1024,128]{2,1,0:T(8,128)}) %all-gather.5.cloned.1.call-update) | async-done | bytes 8388624 | tf_op jit(solution)/shard_map/all_gather | solution.py:77
  159.7 10.8 %fusion.81 = (f32[16,128]{1,0:T(8,128)S(1)}, f32[16,1024,128]{2,1,0:T(8,128)}) fusion(f32[16,1024,128]{2,1,0:T(8,128)} %all-gather.5.cloned.1.call-done, f32[1024,128]{1,0:T(8,128)S(1)} %compare_convert_fusion, f32[16]{0:T(128)S(1)} %copy-done.27, bf16[1024,16,48]{0,2,1:T(8,128)(2,1)} %bitcast.127, bf16[128,16,48]{0,2,1:T(8,128)(2,1)S(1)} %bitcast.142), kind=kOutput, calls=%fused_computation.109 | convolution fusion | flops 211813376 | bytes 19079232 | tf_op jit(solution)/shard_map/sub | solution.py:18
  170.6 4.5 fusion.5
  178.8 10.8 %fusion.82 = (f32[16,128]{1,0:T(8,128)S(1)}, f32[16,1024,128]{2,1,0:T(8,128)}) fusion(f32[16,1024,128]{2,1,0:T(8,128)} %all-gather.5.cloned.1.call-done, f32[1024,128]{1,0:T(8,128)S(1)} %compare_convert_fusion, f32[16]{0:T(128)S(1)} %copy-done.27, bf16[1024,16,48]{0,2,1:T(8,128)(2,1)} %bitcast.129, bf16[128,16,48]{0,2,1:T(8,128)(2,1)} %bitcast.144), kind=kOutput, calls=%fused_computation.110 | convolution fusion | flops 211813376 | bytes 19079232 | tf_op jit(solution)/shard_map/sub | solution.py:18
  189.5 4.5 fusion.4
  198.5 3.0 multiply_convert_fusion.3
  204.4 5.6 fusion.88
  213.0 5.7 fusion.87
  218.8 5.4 multiply_convert_fusion.1
  224.2 3.2 fusion.85
  227.4 6.0 convert_add_fusion
  233.5 3.6 copy.71
  237.1 3.6 copy.70
  240.6 5.4 fusion.86
  246.0 3.6 copy.69
  249.6 3.6 copy.68
  253.3 10.3 %maximum_maximum_fusion = f32[2,1024,1536]{2,1,0:T(8,128)} fusion(f32[1,1024,768]{2,1,0:T(8,128)} %copy.71, f32[1,1024,768]{2,1,0:T(8,128)} %copy.70, f32[1,1024,768]{2,1,0:T(8,128)} %copy.69, f32[1,1024,768]{2,1,0:T(8,128)} %copy.68), kind=kLoop, calls=%fused_computation.2 | loop fusion | flops 9437184 | bytes 25165824 | tf_op jit(solution)/shard_map/concatenate | solution.py:134
  264.7 4.2 fusion.90
  270.8 4.2 fusion.89
  278.9 3.1 convolution_bitcast_fusion.2
  289.5 125.9 %reduce-scatter.3.cloned.1.call-done = f32[2,128,1536]{2,1,0:T(8,128)} async-done(((f32[2,1024,1536]{2,1,0:T(8,128)}), f32[2,128,1536]{2,1,0:T(8,128)}) %reduce-scatter.3.cloned.1.call-update) | async-done | bytes 1572880 | tf_op jit(solution)/shard_map/reduce_scatter | solution.py:142
  415.4 6.0 convolution_bitcast_fusion
  421.4 4.9 fusion.50
  428.1 9.0 %pad_maximum_fusion = f32[768,3072]{1,0:T(8,128)} fusion(f32[768,768]{1,0:T(8,128)} %convolution_bitcast_fusion.2, f32[768,1536]{1,0:T(8,128)} %convolution_bitcast_fusion, f32[768,768]{1,0:T(8,128)} %convolution_bitcast_fusion.3), kind=kLoop, calls=%fused_computation.3 | loop fusion | flops 4718592 | bytes 18874368 | tf_op jit(solution)/shard_map/concatenate | solution.py:172
  439.8 47.5 %reduce-scatter.5.cloned.1.call-done = f32[16,64,128]{2,1,0:T(8,128)} async-done(((f32[16,1024,128]{2,1,0:T(8,128)}), f32[16,64,128]{2,1,0:T(8,128)}) %reduce-scatter.5.cloned.1.call-update) | async-done | bytes 524304 | tf_op jit(solution)/shard_map/reduce_scatter | solution.py:141
  490.7 2.8 copy.83
  494.0 68.7 %all-reduce = (f32[128,16]{0,1:T(8,128)}, f32[16]{0:T(128)}) all-reduce(f32[128,16]{0,1:T(8,128)S(1)} %convolution_bitcast_fusion.4, f32[16]{0:T(128)S(1)} %get-tuple-element.40), channel_id=1, replica_groups=mesh['sample'=16,'token'=8] {'sample','token'}, use_global_device_ids=true, to_apply=%region_14.0 | all-reduce | flops 2064 | bytes 16512 | tf_op jit(solution)/shard_map/psum | solution.py:198
  564.9 101.9 %all-reduce.4.cloned.1.call-done = (f32[768,3072]{1,0:T(8,128)}, f32[768,768]{1,0:T(8,128)}, f32[200,1536]{1,0:T(8,128)}) async-done(((f32[768,3072]{1,0:T(8,128)}, f32[768,768]{1,0:T(8,128)}, f32[200,1536]{1,0:T(8,128)}), (f32[768,3072]{1,0:T(8,128)}, f32[768,768]{1,0:T(8,128)}, f32[200,1536]{1,0:T(8,128)})) %all-reduce.4.cloned.1.call-update) | async-done | bytes 13025296 | tf_op jit(solution)/shard_map/psum | solution.py:198
  666.8 8.8 %copy.104 = f32[768,3072]{1,0:T(8,128)} copy(f32[768,3072]{1,0:T(8,128)} %get-tuple-element.60) | data formatting | bytes 18874368
  (119 shorter events, 64.9 us)
Async XLA Ops:
  7.2 7.6 %copy-start = (bf16[128,64,128]{2,1,0:T(8,128)(2,1)S(1)}, bf16[128,64,128]{2,1,0:T(8,128)(2,1)}, u32[]{:S(2)}) copy-start(bf16[128,64,128]{2,1,0:T(8,128)(2,1)} %param.15) | copy-start | bytes 6291460
  7.2 7.6 %copy-start.25 = (bf16[128,16]{0,1:T(8,128)(2,1)S(1)}, bf16[128,16]{0,1:T(8,128)(2,1)}, u32[]{:S(2)}) copy-start(bf16[128,16]{0,1:T(8,128)(2,1)} %param.16) | copy-start | bytes 12292
  7.2 100.1 %all-gather.3.cloned.1.call-start = ((), (), s32[]{:S(2)}) async-start(), calls=%async_computation.2 | async-start | bytes 7077888 | tf_op jit(solution)/shard_map/all_gather | solution.py:101
  11.1 6.0 copy-start.3
  14.7 5.2 copy-start.26
  14.7 145.0 %all-gather.5.cloned.1.call-start = ((), (), s32[]{:S(2)}) async-start(), calls=%async_computation.3 | async-start | bytes 8912896 | tf_op jit(solution)/shard_map/all_gather | solution.py:77
  17.0 398.4 %reduce-scatter.3.cloned.1.call-start = ((), (), s32[]{:S(2)}) async-start(), calls=%async_computation.4 | async-start | bytes 14155776 | tf_op jit(solution)/shard_map/reduce_scatter | solution.py:142
  19.1 140.6 %copy-start.17 = (bf16[1,128,768]{1,2,0:T(8,128)(2,1)}, bf16[1,128,768]{1,2,0:T(8,128)(2,1)S(1)}, u32[]{:S(2)}) copy-start(bf16[1,128,768]{1,2,0:T(8,128)(2,1)S(1)} %copy.63) | copy-start | bytes 589828
  115.6 44.1 %copy-start.27 = (f32[16]{0:T(128)S(1)}, f32[16]{0:T(128)}, u32[]{:S(2)}) copy-start(f32[16]{0:T(128)} %param.17) | copy-start | bytes 196
  170.6 6.5 copy-start.5
  177.8 11.7 %copy-start.11 = (f32[16,48,128]{2,1,0:T(8,128)}, f32[16,48,128]{2,1,0:T(8,128)S(1)}, u32[]{:S(2)}) copy-start(f32[16,48,128]{2,1,0:T(8,128)S(1)} %fusion.84) | copy-start | bytes 1179652
  189.5 6.5 copy-start.7
  194.1 4.4 copy-start.10
  211.8 7.0 %copy-start.8 = (bf16[1,1024,768]{1,2,0:T(8,128)(2,1)S(1)}, bf16[1,1024,768]{1,2,0:T(8,128)(2,1)}, u32[]{:S(2)}) copy-start(bf16[1,1024,768]{1,2,0:T(8,128)(2,1)} %copy.56) | copy-start | bytes 4718596
  211.8 7.0 %copy-start.20 = (bf16[1,128,768]{1,2,0:T(8,128)(2,1)S(1)}, bf16[1,128,768]{1,2,0:T(8,128)(2,1)}, u32[]{:S(2)}) copy-start(bf16[1,128,768]{1,2,0:T(8,128)(2,1)} %copy.66) | copy-start | bytes 589828
  213.0 14.4 %slice-start = ((s8[8388608]{0:T(1024)(128)(4,1)}), s8[4194304]{0:T(1024)(128)(4,1)S(1)}, s32[]{:S(2)}) async-start(s8[8388608]{0:T(1024)(128)(4,1)} %bitcast.125), calls=%async_computation.7 | async-start | bytes 8388608
  218.7 5.5 copy-start.19
  218.8 8.7 %slice-start.1 = ((s8[8388608]{0:T(1024)(128)(4,1)}), s8[4194304]{0:T(1024)(128)(4,1)S(1)}, s32[]{:S(2)}) async-start(s8[8388608]{0:T(1024)(128)(4,1)} %bitcast.125), calls=%async_computation.8 | async-start | bytes 8388608
  224.2 9.2 %copy-start.4 = (bf16[16,1024,128]{2,1,0:T(8,128)(2,1)}, bf16[16,1024,128]{2,1,0:T(8,128)(2,1)S(1)}, u32[]{:S(2)}) copy-start(bf16[16,1024,128]{2,1,0:T(8,128)(2,1)S(1)} %multiply_convert_fusion.1) | copy-start | bytes 12582916
  224.2 3.2 copy-start.6
  237.0 3.6 copy-start.18
  263.6 223.7 %reduce-scatter.5.cloned.1.call-start = ((), (), s32[]{:S(2)}) async-start(), calls=%async_computation.5 | async-start | bytes 8912896 | tf_op jit(solution)/shard_map/reduce_scatter | solution.py:141
  264.2 402.6 %all-reduce.4.cloned.1.call-start = ((), (), s32[]{:S(2)}) async-start(), calls=%async_computation.6 | async-start | bytes 26050560 | tf_op jit(solution)/shard_map/psum | solution.py:198
  276.9 5.1 copy-start.21
  276.9 5.1 copy-start.22
  278.9 8.0 %copy-start.13 = (bf16[2,128,768]{2,1,0:T(8,128)(2,1)S(1)}, bf16[2,128,768]{2,1,0:T(8,128)(2,1)}, u32[]{:S(2)}) copy-start(bf16[2,128,768]{2,1,0:T(8,128)(2,1)} %get-tuple-element.38) | copy-start | bytes 1179652
  415.4 6.0 copy-start.9
  415.4 6.0 copy-start.14
  415.4 6.0 copy-start.24
  421.4 4.9 copy-start.28
  490.0 3.6 copy-start.16
  666.8 8.8 %copy-start.15 = (f32[768,768]{1,0:T(8,128)S(1)}, f32[768,768]{1,0:T(8,128)}, u32[]{:S(2)}) copy-start(f32[768,768]{1,0:T(8,128)} %get-tuple-element.61) | copy-start | bytes 7077892
  (4 other events, 6.8 us)
Sparse Core Ops, SparseCore 0:
  14.8 92.4 all-gather.2
  109.0 50.7 all-gather.4
  263.8 151.5 reduce-scatter.2
  417.8 69.5 reduce-scatter.4
  494.2 172.5 all-reduce.3
where the time goes:
time: 691 us; the launch traced here: 685 us
  waiting for transfers between devices  396 us (57%)
  matrix products  106 us (15%)
  blocking collectives  68.7 us (10%)
  local copies, waits for them, and re-layouts  62.8 us (9%)
  other arithmetic  37 us (5%)
  between operations  14.3 us (2%)
    reduce_scatter x1, waiting for transfers between devices, shards(): lax.psum_scatter(grad_key_value, 'token', scatter_dimension=1, tiled=True)  126 us
    psum x1, waiting for transfers between devices, shards(): lax.psum((grad_input_part, grad_out_part, grad_pair_part, grad_cross_part...  102 us
    all_gather x1, waiting for transfers between devices, shards(): key_value = lax.all_gather(key_value_own, 'token', axis=1, tiled=True)  84.3 us
    psum x1, blocking collectives, shards(): lax.psum((grad_input_part, grad_out_part, grad_pair_part, grad_cross_part...  68.7 us
    reduce_scatter x1, waiting for transfers between devices, shards(): lax.psum_scatter(bias_term, 'sample', scatter_dimension=1, tiled=True)  47.5 us
    all_gather x1, waiting for transfers between devices, shards(): pair_bias = lax.all_gather(pair_part, 'sample', axis=1, tiled=True)  36 us
    sub x2, matrix products, attend_sample(): exp_terms = jnp.exp(logits - row_peak)  21.6 us
    unnamed x66, local copies, waits for them, and re-layouts  19.5 us
  transfers between devices with their start and end apart: 5, of which 5 were waited for; matrix products, arithmetic and copies ran while one was open for 12% of the time, Pallas kernels for 0%

commit v1 on v0

v1 whole, which is shorter than its diff:
```python
import functools
import math

import jax
import jax.numpy as jnp
from jax import lax
from jax.experimental import pallas as pl
from jax.experimental.pallas import tpu as pltpu
from jax.sharding import Mesh, PartitionSpec as P

norm_epsilon = 1e-05
bf16 = jnp.bfloat16
f32 = jnp.float32
token_axes = ("x", "z_hi")
head_axes = ("core", "x", "z_hi")
column_axes = ("z_lo", "y")
chip_axes = ("z_lo", "y", "x", "z_hi")


def dot(a, b, dims):
    return lax.dot_general(a, b, (dims, ((), ())), preferred_element_type=f32)


def attend_kernel(
    factor,
    cross_ref,
    chain_col_ref,
    chain_row_ref,
    rows_ref,
    bias_ref,
    out_ref,
    grad_bias_ref,
    bias_full,
    logits,
    exp_half,
    grad_half,
    grad_sum,
):
    blocks, width, lanes = rows_ref.shape
    size = width // 4
    count = blocks * lanes
    chunk = 128
    step = pl.program_id(0)

    @pl.when(step == 0)
    def _():
        cross = cross_ref[0]
        part = bias_ref.shape[3]
        for p in range(count // part):
            at = pl.ds(part * p, part)
            block = jnp.concatenate(
                [bias_ref[p // 2, p % 2, t] for t in range(blocks)], axis=1
            )
            differ = chain_col_ref[at, 0:1] != chain_row_ref[0:1, :]
            bias_full[at, :] = block + jnp.where(differ, cross, 0.0)
            grad_sum[at, :] = jnp.zeros((part, count), f32)

    def take(index):
        return jnp.concatenate(
            [rows_ref[t, index * size : (index + 1) * size, :] for t in range(blocks)], axis=1
        )

    query_t, key_t, value_t, grad_t = take(0), take(1), take(2), take(3)
    key = key_t.T
    value = value_t.T
    peak = jnp.full((1, count), -jnp.inf, f32)
    for p in range(count // chunk):
        at = pl.ds(chunk * p, chunk)
        part = dot(key[chunk * p : chunk * (p + 1)], query_t, ((1,), (0,))) + bias_full[at, :]
        logits[at, :] = part
        peak = jnp.maximum(peak, jnp.max(part, axis=0, keepdims=True))
    for p in range(count // chunk):
        at = pl.ds(chunk * p, chunk)
        exp_half[at, :] = jnp.exp(logits[at, :] - peak).astype(bf16)
    value_ones = jnp.concatenate([value_t, jnp.ones((16, count), bf16)], axis=0)
    summed = dot(value_ones, exp_half[...], ((1,), (0,)))
    inverse = 1.0 / summed[size : size + 1]
    attended_t = summed[:size] * inverse
    scaled_t = (grad_t.astype(f32) * inverse).astype(bf16)
    delta = jnp.sum(scaled_t.astype(f32) * attended_t, axis=0, keepdims=True)
    key_grad = []
    value_grad = []
    for p in range(count // chunk):
        at = pl.ds(chunk * p, chunk)
        weights = dot(value[chunk * p : chunk * (p + 1)], scaled_t, ((1,), (0,)))
        terms = exp_half[at, :]
        grad = terms.astype(f32) * (weights - delta)
        half = grad.astype(bf16)
        grad_half[at, :] = half
        grad_sum[at, :] += grad
        key_grad.append(dot(half, query_t, ((1,), (1,))))
        value_grad.append(dot(terms, scaled_t, ((1,), (1,))))
    query_grad_t = dot(key_t, grad_half[...], ((1,), (0,))) * factor
    key_grad_t = jnp.concatenate(key_grad, axis=0).T
    value_grad_t = jnp.concatenate(value_grad, axis=0).T
    for index, array in enumerate((attended_t, query_grad_t, key_grad_t, value_grad_t)):
        array = array.astype(bf16)
        for t in range(blocks):
            out_ref[t, index * size : (index + 1) * size, :] = array[:, t * lanes : (t + 1) * lanes]

    @pl.when(step == pl.num_programs(0) - 1)
    def _():
        part = grad_bias_ref.shape[3]
        for p in range(count // part):
            for t in range(blocks):
                grad_bias_ref[p // 2, p % 2, t] = grad_sum[
                    pl.ds(part * p, part), t * lanes : (t + 1) * lanes
                ].astype(bf16)


def attend(rows, bias, cross, chains, factor):
    blocks, width, total = rows.shape
    lanes = 128
    samples = total // lanes
    count = blocks * lanes
    chain_col = jnp.broadcast_to(chains[:, None], (count, 128))
    chain_row = jnp.broadcast_to(chains[None, :], (8, count))
    whole = lambda shape: pl.BlockSpec(shape, lambda s: (0,) * len(shape))
    return pl.pallas_call(
        functools.partial(attend_kernel, factor),
        grid=(samples,),
        in_specs=[
            pl.BlockSpec(memory_space=pltpu.SMEM),
            whole(chain_col.shape),
            whole(chain_row.shape),
            pl.BlockSpec((blocks, width, lanes), lambda s: (0, 0, s)),
            whole(bias.shape),
        ],
        out_specs=[
            pl.BlockSpec((blocks, width, lanes), lambda s: (0, 0, s)),
            whole(bias.shape),
        ],
        out_shape=[
            jax.ShapeDtypeStruct(rows.shape, bf16),
            jax.ShapeDtypeStruct(bias.shape, bf16),
        ],
        scratch_shapes=[
            pltpu.VMEM((count, count), f32),
            pltpu.VMEM((count, count), f32),
            pltpu.VMEM((count, count), bf16),
            pltpu.VMEM((count, count), bf16),
            pltpu.VMEM((count, count), f32),
        ],
        compiler_params=pltpu.CompilerParams(vmem_limit_bytes=52 * 1024 * 1024),
        cost_estimate=pl.CostEstimate(
            flops=12 * samples * count * count * 48,
            bytes_accessed=16 * 1024 * 1024,
            transcendentals=samples * count * count,
        ),
    )(cross, chain_col, chain_row, rows, bias)


def swap(array):
    return lax.ppermute(array, "core", [(0, 1), (1, 0)])


def exchange(array, axes):
    return lax.all_to_all(array, axes, 0, 0, tiled=True)


def spread(array, axes, count):
    return exchange(jnp.broadcast_to(array[None], (count,) + array.shape), axes)


def shards(
    activations,
    levels,
    ada_table,
    input_weight,
    output_matrix,
    pair_feats,
    pair_weight,
    cross_bias,
    chains,
    cotangent,
):
    own_samples, row_count, width = activations.shape
    heads = pair_weight.shape[1]
    size = width // heads
    col_count = pair_feats.shape[1]
    level_count = ada_table.shape[0]
    factor = 1.0 / math.sqrt(size)
    core = lax.axis_index("core")
    blocks = lax.axis_size("x") * lax.axis_size("z_hi")
    zy_count = lax.axis_size("z_lo") * lax.axis_size("y")
    chip_count = blocks * zy_count
    token = lax.axis_index(token_axes)
    zy = lax.axis_index(column_axes)
    half = width // 2

    pair_part = jnp.einsum("ijc,ch->hji", pair_feats, pair_weight, preferred_element_type=f32)
    bias_own = exchange(pair_part.astype(jnp.float16), head_axes)
    bias = spread(bias_own, column_axes, zy_count).astype(f32)
    bias = bias.reshape(zy_count, 2, blocks, col_count, row_count)

    rows = own_samples * 2 * row_count
    acts = jnp.concatenate([activations, swap(activations)], axis=0)
    cots = jnp.concatenate([cotangent, swap(cotangent)], axis=0).reshape(rows, width)
    chip_levels = jnp.concatenate([levels, swap(levels)], axis=0)
    onehot = (
        chip_levels[:, None]
        == lax.broadcasted_iota(jnp.int32, (2 * own_samples, level_count), 1)
    ).astype(bf16)
    modulation = jnp.dot(onehot, ada_table, preferred_element_type=f32)
    ada_scale = 1.0 + modulation[:, None, :width]
    ada_shift = modulation[:, None, width:]
    wide = acts.astype(f32)
    row_mean = jnp.mean(wide, axis=2, keepdims=True)
    centred = wide - row_mean
    inv_std = lax.rsqrt(jnp.mean(centred * centred, axis=2, keepdims=True) + norm_epsilon)
    normed = (centred * inv_std * ada_scale + ada_shift).astype(bf16).reshape(rows, width)

    weight = lax.dynamic_slice_in_dim(
        input_weight.reshape(width, 4, 2, half), core, 1, axis=2
    ).reshape(width, 4 * half)
    out_weight = lax.dynamic_slice_in_dim(output_matrix, core * half, half, axis=0)
    projected = dot(weight, normed, ((0,), (1,)))
    query = (projected[:half] * factor).astype(bf16)
    key = projected[half : 2 * half].astype(bf16)
    value = projected[2 * half : 3 * half].astype(bf16)
    gate_open = jax.nn.sigmoid(projected[3 * half :])
    grad_gated = dot(out_weight, cots, ((1,), (1,)))
    grad_attend = (grad_gated * gate_open).astype(bf16)
    by_head = lambda a: a.reshape(blocks, size, rows)
    sent = jnp.concatenate([by_head(a) for a in (query, key, value, grad_attend)], axis=1)
    head_rows = exchange(sent, token_axes)
    own_cross = lax.dynamic_slice_in_dim(cross_bias, core * blocks + token, 1)

    head_grads, grad_bias = attend(head_rows, bias, own_cross, chains, factor)

    back = exchange(head_grads, token_axes).reshape(blocks, 4, size, rows)
    attended = back[:, 0].reshape(half, rows).astype(f32)
    gated = (gate_open * attended).astype(bf16)
    grad_gate = (grad_gated * attended * gate_open * (1.0 - gate_open)).astype(bf16)
    grads = jnp.concatenate(
        [back[:, index].reshape(half, rows) for index in (1, 2, 3)] + [grad_gate], axis=0
    )
    normed_part = dot(grads, weight, ((0,), (1,)))
    updated_part = dot(gated, out_weight, ((0,), (0,)))
    own = rows // 2
    grad_normed = normed_part[:own] + swap(normed_part[own:].astype(bf16)).astype(f32)
    output = updated_part[:own] + swap(updated_part[own:].astype(bf16)).astype(f32)
    own_shape = (own_samples, row_count, width)
    grad_normed = grad_normed.reshape(own_shape)
    updated = (activations.astype(f32) + output.reshape(own_shape)).astype(bf16)

    whitened = centred[:own_samples] * inv_std[:own_samples]
    grad_whitened = grad_normed * ada_scale[:own_samples]
    grad_scale = jnp.sum(grad_normed * whitened, axis=1)
    grad_shift = jnp.sum(grad_normed, axis=1)
    grad_tokens = (
        cotangent.astype(f32)
        + inv_std[:own_samples]
        * (
            grad_whitened
            - jnp.mean(grad_whitened, axis=2, keepdims=True)
            - whitened * jnp.mean(grad_whitened * whitened, axis=2, keepdims=True)
        )
    ).astype(bf16)

    bias_parts = exchange(grad_bias, column_axes)
    bias_sum = jnp.sum(bias_parts.astype(f32), axis=0).astype(bf16)
    grad_bias_half = exchange(bias_sum.reshape(heads, col_count, row_count), head_axes)
    grad_pair = jnp.einsum(
        "hji,ch->ijc", grad_bias_half, pair_weight, preferred_element_type=f32
    ).astype(bf16)
    grad_pair_part = jnp.einsum(
        "ijc,hji->ch", pair_feats, grad_bias_half, preferred_element_type=f32
    )
    col_at = (zy * 2 + core) * col_count
    col_chain = lax.dynamic_slice_in_dim(chains, col_at, col_count)
    row_chain = lax.dynamic_slice_in_dim(chains, token * row_count, row_count)
    differ = col_chain[:, None] != row_chain[None, :]
    grad_cross_part = jnp.sum(
        jnp.where(differ[None], grad_bias_half.astype(f32), 0.0), axis=(1, 2)
    )

    line = 2 * width
    weight_part = dot(normed, grads, ((0,), (1,))).astype(bf16)
    out_part = dot(gated, cots, ((1,), (0,))).astype(bf16)
    at_own = (jnp.arange(zy_count) == zy).astype(f32)[:, None]
    at_first = (jnp.arange(zy_count) == 0).astype(f32)[:, None]
    table_rows = jnp.concatenate([grad_scale, grad_shift], axis=1)
    level_row = jnp.pad(
        levels.astype(f32) * (token == 0).astype(f32), (0, line - own_samples)
    )
    pair_rows = jnp.pad(
        jnp.concatenate([grad_pair_part.reshape(-1), grad_cross_part]),
        (0, 2 * line - grad_pair_part.size - heads),
    ).reshape(2, line)
    small = jnp.stack(
        [
            at_own * table_rows[0],
            at_own * table_rows[1],
            at_first * pair_rows[0],
            at_first * pair_rows[1],
            at_own * level_row,
        ]
        + [jnp.zeros((zy_count, line), f32)] * (blocks - 5),
        axis=1,
    ).reshape(chip_count, 1, line)
    payload = jnp.concatenate(
        [
            weight_part.reshape(chip_count, -1, line),
            out_part.reshape(chip_count, -1, line),
            small.astype(bf16),
        ],
        axis=1,
    )
    parts = exchange(payload, chip_axes)
    summed = jnp.sum(parts.astype(f32), axis=0).astype(bf16)
    gathered = spread(summed, chip_axes, chip_count)
    other = swap(gathered)
    pair_of = jnp.where(core == 0, jnp.stack([gathered, other]), jnp.stack([other, gathered]))
    depth = width // chip_count
    input_weight_grad = (
        pair_of[:, :, :depth]
        .reshape(2, width, 4, half)
        .transpose(1, 2, 0, 3)
        .reshape(width, 4 * width)
        .astype(f32)
    )
    output_weight_grad = pair_of[:, :, depth : depth + depth // 4].reshape(width, width).astype(f32)
    small_all = pair_of[:, :, -1].reshape(2, zy_count, blocks, line).astype(f32)
    table_all = small_all[:, :, :2].transpose(1, 0, 2, 3).reshape(-1, line)
    level_all = small_all[:, :, 4, :own_samples].transpose(1, 0, 2).reshape(-1)
    onehot_all = (
        level_all[None, :] == jnp.arange(level_count, dtype=f32)[:, None]
    ).astype(f32)
    grad_table = jnp.dot(onehot_all, table_all, precision=lax.Precision.HIGHEST)
    pair_flat = jnp.sum(small_all[:, 0, 2:4], axis=0).reshape(-1)
    pair_size = pair_weight.shape[0] * heads
    grad_pair_weight = pair_flat[:pair_size].reshape(pair_weight.shape)
    grad_cross = pair_flat[pair_size : pair_size + heads]
    return (
        updated,
        grad_tokens,
        grad_pair,
        input_weight_grad,
        output_weight_grad,
        grad_pair_weight,
        grad_cross,
        grad_table,
    )


def solution(mesh):
    fine = Mesh(mesh.devices.reshape(2, 4, 2, 4, 2), ("z_lo", "y", "core", "x", "z_hi"))
    sample = ("z_lo", "y", "core")
    token = ("x", "z_hi")
    placed = (
        P(sample, token, None),
        P(sample),
        P(),
        P(),
        P(),
        P(token, sample, None),
        P(),
        P(),
        P(),
        P(sample, token, None),
    )
    return jax.shard_map(
        shards,
        mesh=fine,
        in_specs=placed,
        out_specs=(
            P(sample, token, None),
            P(sample, token, None),
            P(token, sample, None),
            P(),
            P(),
            P(),
            P(),
            P(),
        ),
        check_vma=False,
    )
```

time: 691 us -> 408 us (0.59)
  waiting for transfers between devices: 396 us -> 71.5 us
  matrix products: 106 us -> 15.9 us
  starting transfers between devices: 0.61 us -> 42.3 us
  local copies, waits for them, and re-layouts: 62.8 us -> 101 us
  blocking collectives: 68.7 us -> 102 us
  Pallas kernels: 0 us -> 22.8 us
  between operations: 14.3 us -> 1.46 us
  other arithmetic: 37 us -> 45.4 us
    reduce_scatter x2 -> x0, waiting for transfers between devices: 173 us -> none  [the longest x1 126 us: shards(): lax.psum_scatter(grad_key_value, 'token', scatter_dimension=1, tiled=True)]
    all_gather x2 -> x0, waiting for transfers between devices: 120 us -> none  [the longest x1 84.3 us: shards(): key_value = lax.all_gather(key_value_own, 'token', axis=1, tiled=True)]
    psum x1 -> x0, waiting for transfers between devices: 102 us -> none  [shards(): lax.psum((grad_input_part, grad_out_part, grad_pair_part, grad_cross_part...]
    all_to_all x0 -> x2, blocking collectives: none -> 102 us  [exchange(): return lax.all_to_all(array, axes, 0, 0, tiled=True)]
    dot_general x24 -> x8, matrix products: 81.8 us -> 11.7 us  [the longest x6 10.2 us: dot(): return lax.dot_general(a, b, (dims, ((), ())), preferred_element_type=f32)]
    psum x1 -> x0, blocking collectives: 68.7 us -> none  [shards(): lax.psum((grad_input_part, grad_out_part, grad_pair_part, grad_cross_part...]
    all_to_all x0 -> x6, waiting for transfers between devices: none -> 66.5 us  [exchange(): return lax.all_to_all(array, axes, 0, 0, tiled=True)]
    convert_element_type x1 -> x7, local copies, waits for them, and re-layouts: 1.19 us -> 53.6 us  [the longest x3 43 us: shards(): input_weight_grad = pair_of[:, :, :depth].reshape(2, width, 4, half).tran...]
  transfers between devices with their start and end apart: 5 -> 12, of which waited for: 5 -> 6; matrix products, arithmetic and copies ran while one was open for 12% -> 15% of each run, Pallas kernels for 0% -> 0%
where the time goes in v1:
time: 408 us; the launch traced here: 402 us
  blocking collectives  102 us (25%)
  local copies, waits for them, and re-layouts  101 us (25%)
  waiting for transfers between devices  71.5 us (18%)
  other arithmetic  45.4 us (11%)
  starting transfers between devices  42.3 us (10%)
  Pallas kernels  22.8 us (6%)
  matrix products  15.9 us (4%)
    all_to_all x2, blocking collectives, exchange(): return lax.all_to_all(array, axes, 0, 0, tiled=True)  102 us
    all_to_all x6, waiting for transfers between devices, exchange(): return lax.all_to_all(array, axes, 0, 0, tiled=True)  66.5 us
    convert_element_type x3, local copies, waits for them, and re-layouts, shards(): input_weight_grad = pair_of[:, :, :depth].reshape(2, width, 4, half).tran...  43 us
    all_to_all x6, starting transfers between devices, exchange(): return lax.all_to_all(array, axes, 0, 0, tiled=True)  34.9 us
    pallas_call x1, Pallas kernels, attend(): pl.pallas_call(functools.partial(attend_kernel, factor), grid=(samples,),...  22.8 us
    unnamed x78, local copies, waits for them, and re-layouts  22.7 us
    dot_general x6, matrix products, dot(): return lax.dot_general(a, b, (dims, ((), ())), preferred_element_type=f32)  10.2 us
    convert_element_type x2, local copies, waits for them, and re-layouts, shards(): pair_of[:, :, depth:depth + depth // 4].reshape(width, width).astype(f32)  9.58 us
  transfers between devices with their start and end apart: 12, of which 6 were waited for; matrix products, arithmetic and copies ran while one was open for 15% of the time, Pallas kernels for 0%

profile of v1, /device:TPU:1, one launch (start us, length us, event | category | flops | bytes accessed | tf_op | source)
XLA Modules:
  0.0 402.2 jit_solution(2901299400004925636)
XLA Ops:
  5.0 9.1 %all-to-all-start.1 = ((f16[16,64,128]{2,1,0:T(8,128)(2,1)}), f16[16,64,128]{2,1,0:T(8,128)(2,1)S(1)}, u32[]{:S(2)}, u32[]{:S(2)}) async-start(f16[16,64,128]{2,1,0:T(8,128)(2,1)} %copy.75), calls=%async_computation.1 | async-start | bytes 524288 | tf_op jit(solution)/shard_map/all_to_all | solution.py:158
  14.7 6.6 %copy.73 = bf16[768,3072]{0,1:T(8,128)(2,1)} copy(bf16[768,3072]{1,0:T(8,128)(2,1)} %param.13) | data formatting | bytes 9437184 | tf_op args[3]
  21.3 3.3 constant_dynamic-slice_fusion
  27.4 4.7 %all-to-all-start.2 = ((f16[8,16,64,128]{3,2,1,0:T(8,128)(2,1)}), f16[8,16,64,128]{3,2,1,0:T(8,128)(2,1)}, u32[]{:S(2)}, u32[]{:S(2)}) async-start(f16[8,16,64,128]{3,2,1,0:T(8,128)(2,1)} %broadcast_in_dim.18), calls=%async_computation.2 | async-start | bytes 4194304 | tf_op jit(solution)/shard_map/all_to_all | solution.py:158
  40.2 19.1 %all-to-all-done.2 = f16[8,16,64,128]{3,2,1,0:T(8,128)(2,1)} async-done(((f16[8,16,64,128]{3,2,1,0:T(8,128)(2,1)}), f16[8,16,64,128]{3,2,1,0:T(8,128)(2,1)}, u32[]{:S(2)}, u32[]{:S(2)}) %all-to-all-start.2) | async-done | bytes 2097184 | tf_op jit(solution)/shard_map/all_to_all | solution.py:158
  59.3 7.1 %all-to-all-start = ((bf16[8,192,512]{2,1,0:T(8,128)(2,1)}), bf16[8,192,512]{2,1,0:T(8,128)(2,1)}, u32[]{:S(2)}, u32[]{:S(2)}) async-start(bf16[8,192,512]{2,1,0:T(8,128)(2,1)} %pad_maximum_fusion.1), calls=%async_computation | async-start | bytes 3145728 | tf_op jit(solution)/shard_map/all_to_all | solution.py:158
  67.0 4.1 %convert.47.bias_ref = f32[8,2,8,64,128]{4,3,2,1,0:T(8,128)} convert(f16[8,2,8,64,128]{4,3,2,1,0:T(8,128)(2,1)} %bitcast.41) | non-fusion elementwise | flops 1048576 | bytes 6291456 | tf_op jit(solution)/shard_map/reshape | solution.py:194
  71.1 18.3 %all-to-all-done.rows_ref = bf16[8,192,512]{2,1,0:T(8,128)(2,1)} async-done(((bf16[8,192,512]{2,1,0:T(8,128)(2,1)}), bf16[8,192,512]{2,1,0:T(8,128)(2,1)}, u32[]{:S(2)}, u32[]{:S(2)}) %all-to-all-start) | async-done | bytes 1572896 | tf_op jit(solution)/shard_map/all_to_all | solution.py:158
  89.6 22.8 %shard_map.161 = (bf16[8,192,512]{2,1,0:T(8,128)(2,1)}, bf16[8,2,8,64,128]{4,3,2,1,0:T(8,128)(2,1)}) custom-call(f32[1]{0:T(128)} %dynamic_slice.16.cross_ref, s32[1024,128]{1,0:T(8,128)S(1)} %broadcast_in_dim.16.chain_col_ref, s32[8,1024]{1,0:T(8,128)S(1)} %broadcast_in_dim.17.chain_row_ref, bf16[8,192,512]{2,1,0:T(8,128)(2,1)} %all-to-all-done.rows_ref, ...), custom_call_target="tpu_custom_call" | custom-call | flops 2415919104 | bytes 16777216 | tf_op jit(solution)/shard_map/pallas_call | solution.py:119
  112.4 4.5 %all-to-all-start.3 = ((bf16[8,192,512]{2,1,0:T(8,128)(2,1)}), bf16[8,192,512]{2,1,0:T(8,128)(2,1)}, u32[]{:S(2)}, u32[]{:S(2)}) async-start(bf16[8,192,512]{2,1,0:T(8,128)(2,1)} %get-tuple-element.10), calls=%async_computation.3 | async-start | bytes 3145728 | tf_op jit(solution)/shard_map/all_to_all | solution.py:158
  120.8 18.2 %all-to-all-done.3 = bf16[8,192,512]{2,1,0:T(8,128)(2,1)} async-done(((bf16[8,192,512]{2,1,0:T(8,128)(2,1)}), bf16[8,192,512]{2,1,0:T(8,128)(2,1)}, u32[]{:S(2)}, u32[]{:S(2)}) %all-to-all-start.3) | async-done | bytes 1572896 | tf_op jit(solution)/shard_map/all_to_all | solution.py:158
  139.0 4.3 %all-to-all-start.4 = ((bf16[8,2,8,64,128]{4,3,2,1,0:T(8,128)(2,1)}), bf16[8,2,8,64,128]{4,3,2,1,0:T(8,128)(2,1)}, u32[]{:S(2)}, u32[]{:S(2)}) async-start(bf16[8,2,8,64,128]{4,3,2,1,0:T(8,128)(2,1)} %get-tuple-element.11), calls=%async_computation.4 | async-start | bytes 4194304 | tf_op jit(solution)/shard_map/all_to_all | solution.py:158
  153.1 4.4 %convolution_convert_fusion = bf16[768,1536]{1,0:T(8,128)(2,1)} fusion(bf16[512,768]{1,0:T(8,128)(2,1)} %fusion.2, bf16[384,512]{1,0:T(8,128)(2,1)} %copy-done.22, bf16[384,512]{1,0:T(8,128)(2,1)} %bitcast.111, bf16[384,512]{1,0:T(8,128)(2,1)} %bitcast.113, bf16[384,512]{1,0:T(8,128)(2,1)} %bitcast.109), kind=kOutput, calls=%fused_computation.2 | convolution fusion | flops 1215430656 | bytes 4718592 | tf_op jit(solution)/shard_map/dot_general | solution.py:21
  157.5 4.8 %reshape.498 = bf16[64,12,1536]{2,1,0:T(8,128)(2,1)} reshape(bf16[768,1536]{1,0:T(8,128)(2,1)} %convolution_convert_fusion) | data formatting | bytes 4718592 | tf_op jit(solution)/shard_map/reshape | solution.py:304
  165.4 5.0 %all-to-all-done.4 = bf16[8,2,8,64,128]{4,3,2,1,0:T(8,128)(2,1)} async-done(((bf16[8,2,8,64,128]{4,3,2,1,0:T(8,128)(2,1)}), bf16[8,2,8,64,128]{4,3,2,1,0:T(8,128)(2,1)}, u32[]{:S(2)}, u32[]{:S(2)}) %all-to-all-start.4) | async-done | bytes 2097184 | tf_op jit(solution)/shard_map/all_to_all | solution.py:158
  173.1 5.1 %all-to-all-start.5 = ((bf16[16,64,128]{2,1,0:T(8,128)(2,1)}), bf16[16,64,128]{2,1,0:T(8,128)(2,1)S(1)}, u32[]{:S(2)}, u32[]{:S(2)}) async-start(bf16[16,64,128]{2,1,0:T(8,128)(2,1)} %bitcast.106), calls=%async_computation.5 | async-start | bytes 524288 | tf_op jit(solution)/shard_map/all_to_all | solution.py:158
  181.0 5.9 %all-to-all-done.5 = bf16[16,64,128]{2,1,0:T(8,128)(2,1)S(1)} async-done(((bf16[16,64,128]{2,1,0:T(8,128)(2,1)}), bf16[16,64,128]{2,1,0:T(8,128)(2,1)S(1)}, u32[]{:S(2)}, u32[]{:S(2)}) %all-to-all-start.5) | async-done | bytes 262176 | tf_op jit(solution)/shard_map/all_to_all | solution.py:158
  192.6 3.4 pad_maximum_fusion
  196.0 47.3 %all_to_all.40 = bf16[64,16,1536]{2,1,0:T(8,128)(2,1)} all-to-all(bf16[64,16,1536]{2,1,0:T(8,128)(2,1)S(1)} %pad_maximum_fusion), channel_id=1, replica_groups=mesh['z_lo'=2,'y'=4,'core'=2,'x'=4,'z_hi'=2] {'z_lo','y','x','z_hi'}, dimensions={0} | all-to-all | bytes 6291456 | tf_op jit(solution)/shard_map/all_to_all | solution.py:158
  246.0 54.5 %all_to_all.41 = bf16[64,16,1536]{2,1,0:T(8,128)(2,1)S(1)} all-to-all(bf16[64,16,1536]{2,1,0:T(8,128)(2,1)S(1)} %broadcast_in_dim.21), channel_id=1, replica_groups=mesh['z_lo'=2,'y'=4,'core'=2,'x'=4,'z_hi'=2] {'z_lo','y','x','z_hi'}, dimensions={0} | all-to-all | bytes 6291456 | tf_op jit(solution)/shard_map/all_to_all | solution.py:158
  300.5 3.4 copy.110
  303.9 3.2 collective-permute-start.5
  307.8 5.0 %collective-permute-done.3 = bf16[256,768]{1,0:T(8,128)(2,1)S(1)} collective-permute-done((bf16[256,768]{1,0:T(8,128)(2,1)S(1)}, bf16[256,768]{1,0:T(8,128)(2,1)S(1)}, u32[]{:S(2)}, u32[]{:S(2)}) %collective-permute-start.3) | collective-permute-done | bytes 393248 | tf_op jit(solution)/shard_map/ppermute | solution.py:154
  318.3 5.4 %maximum_select_fusion = bf16[2,64,16,1536]{3,1,0,2:T(8,128)(2,1)S(1)} fusion(bf16[1,64,16,1536]{3,1,0,2:T(8,128)(2,1)} %bitcast.33, bf16[1,64,16,1536]{3,1,0,2:T(8,128)(2,1)} %bitcast.92, pred[]{:T(512)S(6)} %eq.50), kind=kLoop, calls=%fused_computation | loop fusion | flops 9437184 | bytes 12582913 | tf_op jit(solution)/shard_map/jit(_where)/select_n | solution.py:314
  326.6 3.0 slice_convert_fusion.1
  329.6 7.4 %slice_convert_fusion = f32[2,64,12,1536]{3,1,0,2:T(8,128)} fusion(bf16[2,64,16,1536]{3,1,0,2:T(8,128)(2,1)} %copy-done.2), kind=kLoop, calls=%fused_computation.1 | loop fusion | flops 2359296 | bytes 14155776 | tf_op jit(solution)/shard_map/convert_element_type | solution.py:321
  338.5 4.9 %copy.90 = f32[2,64,3,1536]{3,2,1,0:T(4,128)} copy(f32[2,64,3,1536]{3,1,0,2:T(8,128)} %slice_convert_fusion.1) | data formatting | bytes 4718592 | tf_op jit(solution)/shard_map/convert_element_type | solution.py:323
  343.4 4.7 %reshape.508 = f32[768,768]{1,0:T(8,128)} reshape(f32[2,64,3,1536]{3,2,1,0:T(4,128)} %copy.90) | data formatting | bytes 4718592 | tf_op jit(solution)/shard_map/convert_element_type | solution.py:323
  348.0 17.1 %copy.88 = f32[2,64,12,1536]{3,0,2,1:T(2,128)} copy(f32[2,64,12,1536]{3,1,0,2:T(8,128)} %slice_convert_fusion) | data formatting | bytes 18874368 | tf_op jit(solution)/shard_map/convert_element_type | solution.py:321
  365.2 13.9 %reshape.509 = f32[2,768,4,384]{3,2,0,1:T(4,128)} reshape(f32[2,64,12,1536]{3,0,2,1:T(2,128)} %copy.88) | data formatting | bytes 18874368 | tf_op jit(solution)/shard_map/convert_element_type | solution.py:321
  379.1 11.9 %copy.89 = f32[768,4,2,384]{0,3,2,1:T(8,128)} copy(f32[768,4,2,384]{3,1,2,0:T(4,128)} %bitcast.94) | data formatting | bytes 18874368 | tf_op jit(solution)/shard_map/convert_element_type | solution.py:321
  391.0 9.7 %copy.95 = f32[768,3072]{1,0:T(8,128)} copy(f32[768,3072]{0,1:T(8,128)} %bitcast.95) | data formatting | bytes 18874368
  (169 shorter events, 58.6 us)
Async XLA Ops:
  0.6 13.5 %copy-start.14 = (bf16[2,128,768]{2,1,0:T(8,128)(2,1)S(1)}, bf16[2,128,768]{2,1,0:T(8,128)(2,1)}, u32[]{:S(2)}) copy-start(bf16[2,128,768]{2,1,0:T(8,128)(2,1)} %param.19) | copy-start | bytes 1179652
  0.7 13.6 %copy-start.6 = (bf16[2,128,768]{2,1,0:T(8,128)(2,1)S(1)}, bf16[2,128,768]{2,1,0:T(8,128)(2,1)}, u32[]{:S(2)}) copy-start(bf16[2,128,768]{2,1,0:T(8,128)(2,1)} %param.10) | copy-start | bytes 1179652
  0.7 23.9 %collective-permute-start.1 = (s32[2]{0:T(128)}, s32[2]{0:T(128)S(1)}, u32[]{:S(2)}, u32[]{:S(2)}) collective-permute-start(s32[2]{0:T(128)} %param.11), channel_id=1, source_target_pairs={{0,8},{8,0},{1,9},{9,1},{2,10},{10,2},{3,11},{11,3},{4,12},{12,4},... | collective-permute-start | bytes 32 | tf_op jit(solution)/shard_map/ppermute | solution.py:154
  5.0 20.6 %all-to-all-start.1 = ((f16[16,64,128]{2,1,0:T(8,128)(2,1)}), f16[16,64,128]{2,1,0:T(8,128)(2,1)S(1)}, u32[]{:S(2)}, u32[]{:S(2)}) async-start(f16[16,64,128]{2,1,0:T(8,128)(2,1)} %copy.75), calls=%async_computation.1 | async-start | bytes 524288 | tf_op jit(solution)/shard_map/all_to_all | solution.py:158
  14.1 18.1 %collective-permute-start.2 = (bf16[2,128,768]{2,1,0:T(8,128)(2,1)S(1)}, bf16[2,128,768]{2,1,0:T(8,128)(2,1)}, u32[]{:S(2)}, u32[]{:S(2)}) collective-permute-start(bf16[2,128,768]{2,1,0:T(8,128)(2,1)S(1)} %copy-done.14), channel_id=1, source_target_pairs={{0,8},{8,0},{1,9},{9,1},{2,10},{10,2},{3,11},{11,3},{4,12},{12,4},... | collective-permute-start | bytes 1179656 | tf_op jit(solution)/shard_map/ppermute | solution.py:154
  14.3 17.8 %collective-permute-start = (bf16[2,128,768]{2,1,0:T(8,128)(2,1)S(1)}, bf16[2,128,768]{2,1,0:T(8,128)(2,1)S(1)}, u32[]{:S(2)}, u32[]{:S(2)}) collective-permute-start(bf16[2,128,768]{2,1,0:T(8,128)(2,1)S(1)} %copy-done.6), channel_id=1, source_target_pairs={{0,8},{8,0},{1,9},{9,1},{2,10},{10,2},{3,11},{11,3},{4,12},{12,4},... | collective-permute-start | bytes 1179656 | tf_op jit(solution)/shard_map/ppermute | solution.py:154
  27.4 31.9 %all-to-all-start.2 = ((f16[8,16,64,128]{3,2,1,0:T(8,128)(2,1)}), f16[8,16,64,128]{3,2,1,0:T(8,128)(2,1)}, u32[]{:S(2)}, u32[]{:S(2)}) async-start(f16[8,16,64,128]{3,2,1,0:T(8,128)(2,1)} %broadcast_in_dim.18), calls=%async_computation.2 | async-start | bytes 4194304 | tf_op jit(solution)/shard_map/all_to_all | solution.py:158
  33.3 3.7 copy-start.11
  40.2 26.2 %copy-start.35 = (f32[16]{0:T(128)S(1)}, f32[16]{0:T(128)}, u32[]{:S(2)}) copy-start(f32[16]{0:T(128)} %param.17) | copy-start | bytes 196
  59.3 30.1 %all-to-all-start = ((bf16[8,192,512]{2,1,0:T(8,128)(2,1)}), bf16[8,192,512]{2,1,0:T(8,128)(2,1)}, u32[]{:S(2)}, u32[]{:S(2)}) async-start(bf16[8,192,512]{2,1,0:T(8,128)(2,1)} %pad_maximum_fusion.1), calls=%async_computation | async-start | bytes 3145728 | tf_op jit(solution)/shard_map/all_to_all | solution.py:158
  67.0 22.4 %copy-start.30 = (s32[1024]{0:T(1024)S(1)}, s32[1024]{0:T(1024)}, u32[]{:S(2)}) copy-start(s32[1024]{0:T(1024)} %param.18) | copy-start | bytes 12292
  112.4 26.6 %all-to-all-start.3 = ((bf16[8,192,512]{2,1,0:T(8,128)(2,1)}), bf16[8,192,512]{2,1,0:T(8,128)(2,1)}, u32[]{:S(2)}, u32[]{:S(2)}) async-start(bf16[8,192,512]{2,1,0:T(8,128)(2,1)} %get-tuple-element.10), calls=%async_computation.3 | async-start | bytes 3145728 | tf_op jit(solution)/shard_map/all_to_all | solution.py:158
  119.5 45.0 %copy-start.26 = (f32[2,768]{1,0:T(2,128)}, f32[2,768]{1,0:T(2,128)S(1)}, u32[]{:S(2)}) copy-start(f32[2,768]{1,0:T(2,128)S(1)} %slice.152) | copy-start | bytes 18436
  119.5 45.0 %copy-start.31 = (f32[2,128]{1,0:T(2,128)}, f32[2,128]{1,0:T(2,128)S(1)}, u32[]{:S(2)}) copy-start(f32[2,128]{1,0:T(2,128)S(1)} %slice.115) | copy-start | bytes 3076
  139.0 31.4 %all-to-all-start.4 = ((bf16[8,2,8,64,128]{4,3,2,1,0:T(8,128)(2,1)}), bf16[8,2,8,64,128]{4,3,2,1,0:T(8,128)(2,1)}, u32[]{:S(2)}, u32[]{:S(2)}) async-start(bf16[8,2,8,64,128]{4,3,2,1,0:T(8,128)(2,1)} %get-tuple-element.11), calls=%async_computation.4 | async-start | bytes 4194304 | tf_op jit(solution)/shard_map/all_to_all | solution.py:158
  143.3 3.6 copy-start.4
  146.9 4.5 %copy-start.9 = (bf16[384,512]{1,0:T(8,128)(2,1)}, bf16[384,512]{1,0:T(8,128)(2,1)S(1)}, u32[]{:S(2)}) copy-start(bf16[384,512]{1,0:T(8,128)(2,1)S(1)} %get-tuple-element.62) | copy-start | bytes 1179652
  147.0 4.5 %copy-start.12 = (bf16[4,128,768]{2,1,0:T(8,128)(2,1)S(1)}, bf16[4,128,768]{2,1,0:T(8,128)(2,1)}, u32[]{:S(2)}) copy-start(bf16[4,128,768]{2,1,0:T(8,128)(2,1)} %copy-done.11) | copy-start | bytes 2359300
  149.3 13.0 %collective-permute-start.4 = (bf16[256,768]{1,0:T(8,128)(2,1)}, bf16[256,768]{1,0:T(8,128)(2,1)}, u32[]{:S(2)}, u32[]{:S(2)}) collective-permute-start(bf16[256,768]{1,0:T(8,128)(2,1)} %slice.210), channel_id=1, source_target_pairs={{0,8},{8,0},{1,9},{9,1},{2,10},{10,2},{3,11},{11,3},{4,12},{12,4},... | collective-permute-start | bytes 1179656 | tf_op jit(solution)/shard_map/ppermute | solution.py:154
  173.1 13.8 %all-to-all-start.5 = ((bf16[16,64,128]{2,1,0:T(8,128)(2,1)}), bf16[16,64,128]{2,1,0:T(8,128)(2,1)S(1)}, u32[]{:S(2)}, u32[]{:S(2)}) async-start(bf16[16,64,128]{2,1,0:T(8,128)(2,1)} %bitcast.106), calls=%async_computation.5 | async-start | bytes 524288 | tf_op jit(solution)/shard_map/all_to_all | solution.py:158
  179.0 10.9 %copy-start.28 = (pred[64,128]{1,0:T(8,128)(4,1)S(1)}, pred[64,128]{1,0:T(8,128)(4,1)}, u32[]{:S(2)}) copy-start(pred[64,128]{1,0:T(8,128)(4,1)} %broadcast_compare_fusion) | copy-start | bytes 24580
  300.5 6.6 %copy-start.10 = (bf16[384,512]{1,0:T(8,128)(2,1)S(1)}, bf16[384,512]{1,0:T(8,128)(2,1)}, u32[]{:S(2)}) copy-start(bf16[384,512]{1,0:T(8,128)(2,1)} %copy-done.9) | copy-start | bytes 1179652
  300.5 6.6 %copy-start.24 = (bf16[768,768]{1,0:T(8,128)(2,1)S(1)}, bf16[768,768]{1,0:T(8,128)(2,1)}, u32[]{:S(2)}) copy-start(bf16[768,768]{1,0:T(8,128)(2,1)} %param.14) | copy-start | bytes 3538948
  303.9 3.9 copy-start.33
  303.9 4.0 copy-start.34
  303.9 14.4 %collective-permute-start.5 = (bf16[64,16,1536]{2,0,1:T(8,128)(2,1)}, bf16[64,16,1536]{2,0,1:T(8,128)(2,1)}, u32[]{:S(2)}, u32[]{:S(2)}) collective-permute-start(bf16[64,16,1536]{2,0,1:T(8,128)(2,1)} %copy.110), channel_id=1, source_target_pairs={{0,8},{8,0},{1,9},{9,1},{2,10},{10,2},{3,11},{11,3},{4,12},{12,4},... | collective-permute-start | bytes 9437192 | tf_op jit(solution)/shard_map/ppermute | solution.py:154
  307.6 6.1 %copy-start.8 = (f32[4,128,768]{2,1,0:T(8,128)S(1)}, f32[4,128,768]{2,1,0:T(8,128)}, u32[]{:S(2)}) copy-start(f32[4,128,768]{2,1,0:T(8,128)} %get-tuple-element.73) | copy-start | bytes 4718596
  307.6 6.1 %copy-start.15 = (bf16[2,128,768]{2,1,0:T(8,128)(2,1)S(1)}, bf16[2,128,768]{2,1,0:T(8,128)(2,1)}, u32[]{:S(2)}) copy-start(bf16[2,128,768]{2,1,0:T(8,128)(2,1)} %param.19) | copy-start | bytes 1179652
  307.6 6.1 %copy-start.27 = (f32[2,768]{1,0:T(2,128)S(1)}, f32[2,768]{1,0:T(2,128)}, u32[]{:S(2)}) copy-start(f32[2,768]{1,0:T(2,128)} %copy-done.26) | copy-start | bytes 18436
  307.6 6.1 %copy-start.32 = (f32[2,128]{1,0:T(2,128)S(1)}, f32[2,128]{1,0:T(2,128)}, u32[]{:S(2)}) copy-start(f32[2,128]{1,0:T(2,128)} %copy-done.31) | copy-start | bytes 3076
  307.7 5.2 %collective-permute-start.3 = (bf16[256,768]{1,0:T(8,128)(2,1)S(1)}, bf16[256,768]{1,0:T(8,128)(2,1)S(1)}, u32[]{:S(2)}, u32[]{:S(2)}) collective-permute-start(bf16[256,768]{1,0:T(8,128)(2,1)S(1)} %slice.211), channel_id=1, source_target_pairs={{0,8},{8,0},{1,9},{9,1},{2,10},{10,2},{3,11},{11,3},{4,12},{12,4},... | collective-permute-start | bytes 1179656 | tf_op jit(solution)/shard_map/ppermute | solution.py:154
  391.0 11.1 %copy-start.1 = (bf16[128,64,128]{2,1,0:T(8,128)(2,1)S(1)}, bf16[128,64,128]{2,1,0:T(8,128)(2,1)}, u32[]{:S(2)}) copy-start(bf16[128,64,128]{2,1,0:T(8,128)(2,1)} %param.15) | copy-start | bytes 6291460
  (17 other events, 41.8 us)

commit v2 on v1

--- a/solution.py
+++ b/solution.py
@@ -30,6 +30,7 @@
     bias_ref,
     out_ref,
     grad_bias_ref,
+    cross_sum_ref,
     bias_full,
     logits,
     exp_half,
@@ -101,11 +102,16 @@
     @pl.when(step == pl.num_programs(0) - 1)
     def _():
         part = grad_bias_ref.shape[3]
+        cross_sum = jnp.zeros((1, count), f32)
         for p in range(count // part):
+            at = pl.ds(part * p, part)
+            block = grad_sum[at, :]
+            differ = chain_col_ref[at, 0:1] != chain_row_ref[0:1, :]
+            cross_sum += jnp.sum(jnp.where(differ, block, 0.0), axis=0, keepdims=True)
+            half = block.astype(bf16)
             for t in range(blocks):
-                grad_bias_ref[p // 2, p % 2, t] = grad_sum[
-                    pl.ds(part * p, part), t * lanes : (t + 1) * lanes
-                ].astype(bf16)
+                grad_bias_ref[p // 2, p % 2, t] = half[:, t * lanes : (t + 1) * lanes]
+        cross_sum_ref[...] = jnp.broadcast_to(cross_sum, cross_sum_ref.shape)
 
 
 def attend(rows, bias, cross, chains, factor):
@@ -129,10 +135,12 @@
         out_specs=[
             pl.BlockSpec((blocks, width, lanes), lambda s: (0, 0, s)),
             whole(bias.shape),
+            whole((8, count)),
         ],
         out_shape=[
             jax.ShapeDtypeStruct(rows.shape, bf16),
             jax.ShapeDtypeStruct(bias.shape, bf16),
+            jax.ShapeDtypeStruct((8, count), f32),
         ],
         scratch_shapes=[
             pltpu.VMEM((count, count), f32),
@@ -148,6 +156,209 @@
             transcendentals=samples * count * count,
         ),
     )(cross, chain_col, chain_row, rows, bias)
+
+
+def before_kernel(factor, core_ref, acts_ref, cots_ref, mod_ref, *refs):
+    weight_refs = refs[:4]
+    out_weight_ref, sent_ref, gate_ref, grad_gated_ref, normed_ref = refs[4:]
+    rows, width = acts_ref.shape
+    heads, _, _ = sent_ref.shape
+    size = sent_ref.shape[1] // 4
+    samples = mod_ref.shape[0]
+    part = rows // samples
+    for s in range(samples):
+        at = slice(s * part, (s + 1) * part)
+        wide = acts_ref[at, :].astype(f32)
+        centred = wide - jnp.mean(wide, axis=1, keepdims=True)
+        inv_std = lax.rsqrt(jnp.mean(centred * centred, axis=1, keepdims=True) + norm_epsilon)
+        scale = 1.0 + mod_ref[s : s + 1, :width]
+        shift = mod_ref[s : s + 1, width:]
+        normed_ref[at, :] = (centred * inv_std * scale + shift).astype(bf16)
+    normed = normed_ref[...]
+
+    def put(index, array):
+        for h in range(heads):
+            sent_ref[h, index * size : (index + 1) * size, :] = array[h * size : (h + 1) * size]
+
+    for index in range(3):
+        projected = dot(normed, weight_refs[index][...], ((1,), (0,)))
+        if index == 0:
+            projected = projected * factor
+        put(index, projected.T.astype(bf16))
+    gate = jax.nn.sigmoid(dot(normed, weight_refs[3][...], ((1,), (0,)))).T
+    gate_ref[...] = gate
+    grad_gated = dot(cots_ref[...], out_weight_ref[...], ((1,), (1,))).T
+    grad_gated_ref[...] = grad_gated
+    put(3, (grad_gated * gate).astype(bf16))
+
+
+def weight_specs(width, half):
+    specs = [
+        pl.BlockSpec((width, half), functools.partial(lambda b, i, c: (0, 2 * b + c[0]), b))
+        for b in range(4)
+    ]
+    return specs + [pl.BlockSpec((half, width), lambda i, c: (c[0], 0))]
+
+
+def spec_of(shape):
+    return pl.BlockSpec(shape, lambda i, c: (0,) * len(shape))
+
+
+def before(core, acts, cots, modulation, input_weight, output_matrix, heads, factor):
+    rows, width = acts.shape
+    half = width // 2
+    size = half // heads
+    shapes = [
+        ((heads, 4 * size, rows), bf16),
+        ((half, rows), f32),
+        ((half, rows), f32),
+        ((rows, width), bf16),
+    ]
+    return pl.pallas_call(
+        functools.partial(before_kernel, factor),
+        grid_spec=pltpu.PrefetchScalarGridSpec(
+            num_scalar_prefetch=1,
+            grid=(1,),
+            in_specs=[spec_of(acts.shape), spec_of(cots.shape), spec_of(modulation.shape)]
+            + weight_specs(width, half),
+            out_specs=[spec_of(shape) for shape, _ in shapes],
+        ),
+        out_shape=[jax.ShapeDtypeStruct(shape, kind) for shape, kind in shapes],
+        compiler_params=pltpu.CompilerParams(vmem_limit_bytes=48 * 1024 * 1024),
+        cost_estimate=pl.CostEstimate(
+            flops=2 * rows * width * 5 * half,
+            bytes_accessed=8 * 1024 * 1024,
+            transcendentals=rows * half,
+        ),
+    )(core, acts, cots, modulation, *([input_weight] * 4), output_matrix)
+
+
+def after_kernel(core_ref, back_ref, gate_ref, grad_gated_ref, normed_ref, cots_ref, *refs):
+    weight_refs = refs[:4]
+    out_weight_ref, own_normed_ref, other_normed_ref, own_out_ref, other_out_ref = refs[4:9]
+    payload_ref = refs[9]
+    heads = back_ref.shape[0]
+    size = back_ref.shape[1] // 4
+    own = own_normed_ref.shape[0]
+    width = own_normed_ref.shape[1]
+    half = heads * size
+
+    def take(index):
+        return jnp.concatenate(
+            [back_ref[h, index * size : (index + 1) * size, :] for h in range(heads)], axis=0
+        )
+
+    attended = take(0).astype(f32)
+    gate = gate_ref[...]
+    gated_wide = gate * attended
+    gated = gated_wide.astype(bf16)
+    grad_gate = (grad_gated_ref[...] * gated_wide * (1.0 - gate)).astype(bf16)
+    normed_t = normed_ref[...].T
+    total = None
+    depth = 48
+    for index, grad_t in enumerate((take(1), take(2), take(3), grad_gate)):
+        grad = grad_t.T
+        part = dot(grad, weight_refs[index][...], ((1,), (1,)))
+        total = part if total is None else total + part
+        weight_grad = dot(normed_t, grad, ((1,), (0,))).astype(bf16)
+        for a in range(width // depth):
+            payload_ref[4 * a + index, :depth, :] = weight_grad[depth * a : depth * (a + 1)]
+    own_normed_ref[...] = total[:own]
+    other_normed_ref[...] = total[own:].astype(bf16)
+    output = dot(gated.T, out_weight_ref[...], ((1,), (0,)))
+    own_out_ref[...] = output[:own]
+    other_out_ref[...] = output[own:].astype(bf16)
+    out_grad = dot(gated, cots_ref[...], ((1,), (0,))).astype(bf16)
+    for d in range(payload_ref.shape[0]):
+        if d < half // 8:
+            block = out_grad[16 * (d // 2) : 16 * (d // 2 + 1), half * (d % 2) : half * (d % 2 + 1)]
+        else:
+            block = jnp.zeros((16, half), bf16)
+        payload_ref[d, depth:, :] = block
+
+
+def after(core, back, gate, grad_gated, normed, cots, input_weight, output_matrix):
+    rows, width = normed.shape
+    half = width // 2
+    own = rows // 2
+    shapes = [
+        ((own, width), f32),
+        ((own, width), bf16),
+        ((own, width), f32),
+        ((own, width), bf16),
+        ((64, 64, half), bf16),
+    ]
+    operands = (back, gate, grad_gated, normed, cots)
+    return pl.pallas_call(
+        after_kernel,
+        grid_spec=pltpu.PrefetchScalarGridSpec(
+            num_scalar_prefetch=1,
+            grid=(1,),
+            in_specs=[spec_of(a.shape) for a in operands] + weight_specs(width, half),
+            out_specs=[spec_of(shape) for shape, _ in shapes],
+        ),
+        out_shape=[jax.ShapeDtypeStruct(shape, kind) for shape, kind in shapes],
+        compiler_params=pltpu.CompilerParams(vmem_limit_bytes=48 * 1024 * 1024),
+        cost_estimate=pl.CostEstimate(
+            flops=4 * rows * width * 5 * half,
+            bytes_accessed=12 * 1024 * 1024,
+            transcendentals=0,
+        ),
+    )(core, *operands, *([input_weight] * 4), output_matrix)
+
+
+def assemble_kernel(core_ref, mine_ref, other_ref, input_ref, output_ref):
+    step = pl.program_id(0)
+    half = mine_ref.shape[2]
+    depth = input_ref.shape[0]
+
+    def write(position, ref):
+        for b in range(4):
+            at = (2 * b + position) * half
+            input_ref[:, at : at + half] = ref[b, :depth, :].astype(f32)
+
+        @pl.when(step < 12)
+        def _():
+            for b in range(4):
+                output_ref[
+                    position, 16 * (b // 2) : 16 * (b // 2 + 1), half * (b % 2) : half * (b % 2 + 1)
+                ] = ref[b, depth : depth + 16, :].astype(f32)
+
+    @pl.when(core_ref[0] == 0)
+    def _():
+        write(0, mine_ref)
+        write(1, other_ref)
+
+    @pl.when(core_ref[0] == 1)
+    def _():
+        write(1, mine_ref)
+        write(0, other_ref)
+
+
+def assemble(core, mine, other):
+    chips, depth, half = mine.shape
+    width = 2 * half
+    block = pl.BlockSpec((4, depth, half), lambda a, c: (a, 0, 0))
+    return pl.pallas_call(
+        assemble_kernel,
+        grid_spec=pltpu.PrefetchScalarGridSpec(
+            num_scalar_prefetch=1,
+            grid=(16,),
+            in_specs=[block, block],
+            out_specs=[
+                pl.BlockSpec((width // 16, 4 * width), lambda a, c: (a, 0)),
+                pl.BlockSpec((2, 32, width), lambda a, c: (0, jnp.minimum(a, 11), 0)),
+            ],
+        ),
+        out_shape=[
+            jax.ShapeDtypeStruct((width, 4 * width), f32),
+            jax.ShapeDtypeStruct((2, half, width), f32),
+        ],
+        compiler_params=pltpu.CompilerParams(vmem_limit_bytes=32 * 1024 * 1024),
+        cost_estimate=pl.CostEstimate(
+            flops=0, bytes_accessed=20 * 1024 * 1024, transcendentals=0
+        ),
+    )(core, mine, other)
 
 
 def swap(array):
@@ -185,7 +396,6 @@
     zy_count = lax.axis_size("z_lo") * lax.axis_size("y")
     chip_count = blocks * zy_count
     token = lax.axis_index(token_axes)
-    zy = lax.axis_index(column_axes)
     half = width // 2
 
     pair_part = jnp.einsum("ijc,ch->hji", pair_feats, pair_weight, preferred_element_type=f32)
@@ -194,7 +404,8 @@
     bias = bias.reshape(zy_count, 2, blocks, col_count, row_count)
 
     rows = own_samples * 2 * row_count
-    acts = jnp.concatenate([activations, swap(activations)], axis=0)
+    core_at = jnp.reshape(core, (1,)).astype(jnp.int32)
+    acts = jnp.concatenate([activations, swap(activations)], axis=0).reshape(rows, width)
     cots = jnp.concatenate([cotangent, swap(cotangent)], axis=0).reshape(rows, width)
     chip_levels = jnp.concatenate([levels, swap(levels)], axis=0)
     onehot = (
@@ -202,55 +413,31 @@
         == lax.broadcasted_iota(jnp.int32, (2 * own_samples, level_count), 1)
     ).astype(bf16)
     modulation = jnp.dot(onehot, ada_table, preferred_element_type=f32)
-    ada_scale = 1.0 + modulation[:, None, :width]
-    ada_shift = modulation[:, None, width:]
-    wide = acts.astype(f32)
-    row_mean = jnp.mean(wide, axis=2, keepdims=True)
-    centred = wide - row_mean
-    inv_std = lax.rsqrt(jnp.mean(centred * centred, axis=2, keepdims=True) + norm_epsilon)
-    normed = (centred * inv_std * ada_scale + ada_shift).astype(bf16).reshape(rows, width)
-
-    weight = lax.dynamic_slice_in_dim(
-        input_weight.reshape(width, 4, 2, half), core, 1, axis=2
-    ).reshape(width, 4 * half)
-    out_weight = lax.dynamic_slice_in_dim(output_matrix, core * half, half, axis=0)
-    projected = dot(weight, normed, ((0,), (1,)))
-    query = (projected[:half] * factor).astype(bf16)
-    key = projected[half : 2 * half].astype(bf16)
-    value = projected[2 * half : 3 * half].astype(bf16)
-    gate_open = jax.nn.sigmoid(projected[3 * half :])
-    grad_gated = dot(out_weight, cots, ((1,), (1,)))
-    grad_attend = (grad_gated * gate_open).astype(bf16)
-    by_head = lambda a: a.reshape(blocks, size, rows)
-    sent = jnp.concatenate([by_head(a) for a in (query, key, value, grad_attend)], axis=1)
+    sent, gate_open, grad_gated, normed = before(
+        core_at, acts, cots, modulation, input_weight, output_matrix, blocks, factor
+    )
     head_rows = exchange(sent, token_axes)
     own_cross = lax.dynamic_slice_in_dim(cross_bias, core * blocks + token, 1)
-
-    head_grads, grad_bias = attend(head_rows, bias, own_cross, chains, factor)
-
-    back = exchange(head_grads, token_axes).reshape(blocks, 4, size, rows)
-    attended = back[:, 0].reshape(half, rows).astype(f32)
-    gated = (gate_open * attended).astype(bf16)
-    grad_gate = (grad_gated * attended * gate_open * (1.0 - gate_open)).astype(bf16)
-    grads = jnp.concatenate(
-        [back[:, index].reshape(half, rows) for index in (1, 2, 3)] + [grad_gate], axis=0
-    )
-    normed_part = dot(grads, weight, ((0,), (1,)))
-    updated_part = dot(gated, out_weight, ((0,), (0,)))
-    own = rows // 2
-    grad_normed = normed_part[:own] + swap(normed_part[own:].astype(bf16)).astype(f32)
-    output = updated_part[:own] + swap(updated_part[own:].astype(bf16)).astype(f32)
+    head_grads, grad_bias, cross_sum = attend(head_rows, bias, own_cross, chains, factor)
+
+    back = exchange(head_grads, token_axes)
+    own_normed, other_normed, own_output, other_output, payload = after(
+        core_at, back, gate_open, grad_gated, normed, cots, input_weight, output_matrix
+    )
     own_shape = (own_samples, row_count, width)
-    grad_normed = grad_normed.reshape(own_shape)
-    updated = (activations.astype(f32) + output.reshape(own_shape)).astype(bf16)
-
-    whitened = centred[:own_samples] * inv_std[:own_samples]
-    grad_whitened = grad_normed * ada_scale[:own_samples]
+    grad_normed = (own_normed + swap(other_normed).astype(f32)).reshape(own_shape)
+    output = (own_output + swap(other_output).astype(f32)).reshape(own_shape)
+    wide = activations.astype(f32)
+    updated = (wide + output).astype(bf16)
+    centred = wide - jnp.mean(wide, axis=2, keepdims=True)
+    inv_std = lax.rsqrt(jnp.mean(centred * centred, axis=2, keepdims=True) + norm_epsilon)
+    whitened = centred * inv_std
+    grad_whitened = grad_normed * (1.0 + modulation[:own_samples, None, :width])
     grad_scale = jnp.sum(grad_normed * whitened, axis=1)
     grad_shift = jnp.sum(grad_normed, axis=1)
     grad_tokens = (
         cotangent.astype(f32)
-        + inv_std[:own_samples]
+        + inv_std
         * (
             grad_whitened
             - jnp.mean(grad_whitened, axis=2, keepdims=True)
@@ -267,71 +454,44 @@
     grad_pair_part = jnp.einsum(
         "ijc,hji->ch", pair_feats, grad_bias_half, preferred_element_type=f32
     )
-    col_at = (zy * 2 + core) * col_count
-    col_chain = lax.dynamic_slice_in_dim(chains, col_at, col_count)
-    row_chain = lax.dynamic_slice_in_dim(chains, token * row_count, row_count)
-    differ = col_chain[:, None] != row_chain[None, :]
-    grad_cross_part = jnp.sum(
-        jnp.where(differ[None], grad_bias_half.astype(f32), 0.0), axis=(1, 2)
-    )
-
-    line = 2 * width
-    weight_part = dot(normed, grads, ((0,), (1,))).astype(bf16)
-    out_part = dot(gated, cots, ((1,), (0,))).astype(bf16)
-    at_own = (jnp.arange(zy_count) == zy).astype(f32)[:, None]
-    at_first = (jnp.arange(zy_count) == 0).astype(f32)[:, None]
-    table_rows = jnp.concatenate([grad_scale, grad_shift], axis=1)
-    level_row = jnp.pad(
-        levels.astype(f32) * (token == 0).astype(f32), (0, line - own_samples)
-    )
-    pair_rows = jnp.pad(
-        jnp.concatenate([grad_pair_part.reshape(-1), grad_cross_part]),
-        (0, 2 * line - grad_pair_part.size - heads),
-    ).reshape(2, line)
-    small = jnp.stack(
-        [
-            at_own * table_rows[0],
-            at_own * table_rows[1],
-            at_first * pair_rows[0],
-            at_first * pair_rows[1],
-            at_own * level_row,
-        ]
-        + [jnp.zeros((zy_count, line), f32)] * (blocks - 5),
-        axis=1,
-    ).reshape(chip_count, 1, line)
-    payload = jnp.concatenate(
-        [
-            weight_part.reshape(chip_count, -1, line),
-            out_part.reshape(chip_count, -1, line),
-            small.astype(bf16),
-        ],
-        axis=1,
-    )
+
     parts = exchange(payload, chip_axes)
     summed = jnp.sum(parts.astype(f32), axis=0).astype(bf16)
-    gathered = spread(summed, chip_axes, chip_count)
+    pair_size = pair_weight.shape[0] * heads
+    cross_part = jnp.sum(cross_sum[0])
+    cross_high = cross_part.astype(bf16).astype(f32)
+    last = jnp.concatenate(
+        [jnp.stack([cross_high, cross_part - cross_high]), levels.astype(f32)]
+    )
+    flat = jnp.concatenate([grad_scale, grad_shift], axis=1).reshape(-1)
+    flat = jnp.concatenate([flat, grad_pair_part.reshape(-1), last])
+    small_depth = 16
+    small = jnp.pad(flat, (0, small_depth * half - flat.size)).reshape(small_depth, half)
+    block = jnp.concatenate([summed, small.astype(bf16)], axis=0)
+    gathered = spread(block, chip_axes, chip_count)
     other = swap(gathered)
-    pair_of = jnp.where(core == 0, jnp.stack([gathered, other]), jnp.stack([other, gathered]))
-    depth = width // chip_count
-    input_weight_grad = (
-        pair_of[:, :, :depth]
-        .reshape(2, width, 4, half)
-        .transpose(1, 2, 0, 3)
-        .reshape(width, 4 * width)
-        .astype(f32)
-    )
-    output_weight_grad = pair_of[:, :, depth : depth + depth // 4].reshape(width, width).astype(f32)
-    small_all = pair_of[:, :, -1].reshape(2, zy_count, blocks, line).astype(f32)
-    table_all = small_all[:, :, :2].transpose(1, 0, 2, 3).reshape(-1, line)
-    level_all = small_all[:, :, 4, :own_samples].transpose(1, 0, 2).reshape(-1)
+    input_weight_grad, output_weight_grad = assemble(core_at, gathered, other)
+    output_weight_grad = output_weight_grad.reshape(width, width)
+    mine_small = gathered[:, -small_depth:].reshape(zy_count, blocks, small_depth * half)
+    other_small = other[:, -small_depth:].reshape(zy_count, blocks, small_depth * half)
+    small_all = jnp.where(
+        core == 0, jnp.stack([mine_small, other_small]), jnp.stack([other_small, mine_small])
+    ).astype(f32)
+    line = 2 * width
+    table_all = jnp.sum(small_all[..., : own_samples * line], axis=2)
+    table_all = table_all.reshape(2, zy_count, own_samples, line)
+    table_all = table_all.transpose(1, 0, 2, 3).reshape(-1, line)
+    at = own_samples * line
+    grad_pair_weight = jnp.sum(small_all[..., at : at + pair_size], axis=(0, 1, 2)).reshape(
+        pair_weight.shape
+    )
+    at = at + pair_size
+    grad_cross = jnp.sum(small_all[..., at : at + 2], axis=(1, 3)).reshape(-1)
+    level_all = small_all[:, :, 0, at + 2 : at + 2 + own_samples].transpose(1, 0, 2).reshape(-1)
     onehot_all = (
         level_all[None, :] == jnp.arange(level_count, dtype=f32)[:, None]
     ).astype(f32)
     grad_table = jnp.dot(onehot_all, table_all, precision=lax.Precision.HIGHEST)
-    pair_flat = jnp.sum(small_all[:, 0, 2:4], axis=0).reshape(-1)
-    pair_size = pair_weight.shape[0] * heads
-    grad_pair_weight = pair_flat[:pair_size].reshape(pair_weight.shape)
-    grad_cross = pair_flat[pair_size : pair_size + heads]
     return (
         updated,
         grad_tokens,

time: 408 us -> 337 us (0.83)
  local copies, waits for them, and re-layouts: 101 us -> 33.8 us
  Pallas kernels: 22.8 us -> 51 us
  other arithmetic: 45.4 us -> 19.8 us
  waiting for transfers between devices: 71.5 us -> 85.2 us
  matrix products: 15.9 us -> 6 us
  starting transfers between devices: 42.3 us -> 34 us
    convert_element_type x6 -> x1, local copies, waits for them, and re-layouts: 52.8 us -> 0.02 us  [shards(): block = jnp.concatenate([summed, small.astype(bf16)], axis=0)]
    pallas_call x0 -> x3, Pallas kernels: none -> 27.7 us  [the longest x1 14 us: assemble(): pl.pallas_call(assemble_kernel, grid_spec=pltpu.PrefetchScalarGridSpec(nu...]
    convert_element_type x9 -> x2, other arithmetic: 16.5 us -> 2.93 us  [the longest x1 1.74 us: shards(): small_all = jnp.where(core == 0, jnp.stack([mine_small, other_small]), jn...]
    all_to_all x6 -> x5, waiting for transfers between devices: 66.5 us -> 77.9 us  [exchange(): return lax.all_to_all(array, axes, 0, 0, tiled=True)]
    dot_general x6 -> x0, matrix products: 10.2 us -> none  [dot(): return lax.dot_general(a, b, (dims, ((), ())), preferred_element_type=f32)]
    all_to_all x6 -> x5, starting transfers between devices: 34.9 us -> 27.8 us  [exchange(): return lax.all_to_all(array, axes, 0, 0, tiled=True)]
    select_n x1 -> x0, other arithmetic: 5.45 us -> none  [shards(): jnp.where(core == 0, jnp.stack([gathered, other]), jnp.stack([other, gath...]
    unnamed x78 -> x53, local copies, waits for them, and re-layouts: 22.7 us -> 17.8 us
  transfers between devices with their start and end apart: 12 -> 11, of which waited for: 6 -> 6; matrix products, arithmetic and copies ran while one was open for 15% -> 8% of each run, Pallas kernels for 0% -> 4%
where the time goes in v2:
time: 337 us; the launch traced here: 335 us
  blocking collectives  103 us (31%)
  waiting for transfers between devices  85.2 us (25%)
  Pallas kernels  51 us (15%)
  starting transfers between devices  34 us (10%)
  local copies, waits for them, and re-layouts  33.8 us (10%)
  other arithmetic  19.8 us (6%)
  matrix products  6 us (2%)
    all_to_all x3, blocking collectives, exchange(): return lax.all_to_all(array, axes, 0, 0, tiled=True)  103 us
    all_to_all x5, waiting for transfers between devices, exchange(): return lax.all_to_all(array, axes, 0, 0, tiled=True)  77.9 us
    all_to_all x5, starting transfers between devices, exchange(): return lax.all_to_all(array, axes, 0, 0, tiled=True)  27.8 us
    pallas_call x1, Pallas kernels, attend(): pl.pallas_call(functools.partial(attend_kernel, factor), grid=(samples,),...  23.3 us
    unnamed x53, local copies, waits for them, and re-layouts  17.8 us
    pallas_call x1, Pallas kernels, assemble(): pl.pallas_call(assemble_kernel, grid_spec=pltpu.PrefetchScalarGridSpec(nu...  14 us
    pallas_call x1, Pallas kernels, after(): pl.pallas_call(after_kernel, grid_spec=pltpu.PrefetchScalarGridSpec(num_s...  8.27 us
    ppermute x6, waiting for transfers between devices, swap(): return lax.ppermute(array, 'core', [(0, 1), (1, 0)])  7.36 us
  transfers between devices with their start and end apart: 11, of which 6 were waited for; matrix products, arithmetic and copies ran while one was open for 8% of the time, Pallas kernels for 4%

profile of v2, /device:TPU:1, one launch (start us, length us, event | category | flops | bytes accessed | tf_op | source)
XLA Modules:
  0.0 334.8 jit_solution(12350917156346956706)
XLA Ops:
  2.2 1.9 fusion.6
  4.3 17.6 %all_to_all.40 = f16[16,64,128]{2,1,0:T(8,128)(2,1)S(1)} all-to-all(f16[16,64,128]{2,1,0:T(8,128)(2,1)S(1)} %copy.39), channel_id=1, replica_groups=mesh['z_lo'=2,'y'=4,'core'=2,'x'=4,'z_hi'=2] {'core','x','z_hi'}, dimensions={0} | all-to-all | bytes 524288 | tf_op jit(solution)/shard_map/all_to_all | solution.py:369
  21.9 1.9 broadcast_in_dim.10
  23.7 4.8 %all-to-all-start.2 = ((f16[8,16,64,128]{3,2,1,0:T(8,128)(2,1)}), f16[8,16,64,128]{3,2,1,0:T(8,128)(2,1)}, u32[]{:S(2)}, u32[]{:S(2)}) async-start(f16[8,16,64,128]{3,2,1,0:T(8,128)(2,1)} %broadcast_in_dim.10), calls=%async_computation.2 | async-start | bytes 4194304 | tf_op jit(solution)/shard_map/all_to_all | solution.py:369
  35.2 5.4 %shard_map.161 = (bf16[8,192,512]{2,1,0:T(8,128)(2,1)}, f32[384,512]{1,0:T(8,128)S(1)}, f32[384,512]{1,0:T(8,128)S(1)}, bf16[512,768]{1,0:T(8,128)(2,1)S(1)}) custom-call(s32[1]{0:T(128)} %bitcast.core_ref, bf16[512,768]{1,0:T(8,128)(2,1)S(1)} %bitcast.50, bf16[512,768]{1,0:T(8,128)(2,1)S(1)} %bitcast.48, f32[4,1536]{1,0:T(4,128)S(1)} %fusion.30.mod_ref, ...), custom_call_target="tpu_custom_call" | custom-call | flops 1509949440 | bytes 8388608 | tf_op jit(solution)/shard_map/pallas_call | solution.py:217
  43.3 12.4 %all-to-all-done.2 = f16[8,16,64,128]{3,2,1,0:T(8,128)(2,1)} async-done(((f16[8,16,64,128]{3,2,1,0:T(8,128)(2,1)}), f16[8,16,64,128]{3,2,1,0:T(8,128)(2,1)}, u32[]{:S(2)}, u32[]{:S(2)}) %all-to-all-start.2) | async-done | bytes 2097184 | tf_op jit(solution)/shard_map/all_to_all | solution.py:369
  55.7 4.3 %all-to-all-start = ((bf16[8,192,512]{2,1,0:T(8,128)(2,1)}), bf16[8,192,512]{2,1,0:T(8,128)(2,1)}, u32[]{:S(2)}, u32[]{:S(2)}) async-start(bf16[8,192,512]{2,1,0:T(8,128)(2,1)} %get-tuple-element.22), calls=%async_computation | async-start | bytes 3145728 | tf_op jit(solution)/shard_map/all_to_all | solution.py:369
  60.6 4.1 %convert.32.bias_ref = f32[8,2,8,64,128]{4,3,2,1,0:T(8,128)} convert(f16[8,2,8,64,128]{4,3,2,1,0:T(8,128)(2,1)} %bitcast.22) | non-fusion elementwise | flops 1048576 | bytes 6291456 | tf_op jit(solution)/shard_map/reshape | solution.py:404
  64.7 18.4 %all-to-all-done.rows_ref = bf16[8,192,512]{2,1,0:T(8,128)(2,1)} async-done(((bf16[8,192,512]{2,1,0:T(8,128)(2,1)}), bf16[8,192,512]{2,1,0:T(8,128)(2,1)}, u32[]{:S(2)}, u32[]{:S(2)}) %all-to-all-start) | async-done | bytes 1572896 | tf_op jit(solution)/shard_map/all_to_all | solution.py:369
  83.3 23.3 %shard_map.162 = (bf16[8,192,512]{2,1,0:T(8,128)(2,1)}, bf16[8,2,8,64,128]{4,3,2,1,0:T(8,128)(2,1)}, f32[8,1024]{1,0:T(8,128)S(1)}) custom-call(f32[1]{0:T(128)} %dynamic_slice.3.cross_ref, s32[1024,128]{1,0:T(8,128)S(1)} %broadcast_in_dim.8.chain_col_ref, s32[8,1024]{1,0:T(8,128)S(1)} %broadcast_in_dim.9.chain_row_ref, ...), custom_call_target="tpu_custom_call" | custom-call | flops 2415919104 | bytes 16777216 | tf_op jit(solution)/shard_map/pallas_call | solution.py:125
  106.7 30.0 %all_to_all.41 = bf16[8,2,8,64,128]{4,3,2,1,0:T(8,128)(2,1)} all-to-all(bf16[8,2,8,64,128]{4,3,2,1,0:T(8,128)(2,1)} %get-tuple-element.31), channel_id=1, replica_groups=mesh['z_lo'=2,'y'=4,'core'=2,'x'=4,'z_hi'=2] {'z_lo','y'}, dimensions={0} | all-to-all | bytes 4194304 | tf_op jit(solution)/shard_map/all_to_all | solution.py:369
  136.7 4.5 %all-to-all-start.3 = ((bf16[8,192,512]{2,1,0:T(8,128)(2,1)}), bf16[8,192,512]{2,1,0:T(8,128)(2,1)}, u32[]{:S(2)}, u32[]{:S(2)}) async-start(bf16[8,192,512]{2,1,0:T(8,128)(2,1)} %get-tuple-element.23), calls=%async_computation.3 | async-start | bytes 3145728 | tf_op jit(solution)/shard_map/all_to_all | solution.py:369
  141.2 2.7 reduce_sum.118
  143.9 18.6 %all-to-all-done.3.back_ref = bf16[8,192,512]{2,1,0:T(8,128)(2,1)} async-done(((bf16[8,192,512]{2,1,0:T(8,128)(2,1)}), bf16[8,192,512]{2,1,0:T(8,128)(2,1)}, u32[]{:S(2)}, u32[]{:S(2)}) %all-to-all-start.3) | async-done | bytes 1572896 | tf_op jit(solution)/shard_map/all_to_all | solution.py:369
  162.5 6.2 %all-to-all-start.5 = ((bf16[16,64,128]{2,1,0:T(8,128)(2,1)}), bf16[16,64,128]{2,1,0:T(8,128)(2,1)}, u32[]{:S(2)}, u32[]{:S(2)}) async-start(bf16[16,64,128]{2,1,0:T(8,128)(2,1)} %bitcast.10), calls=%async_computation.5 | async-start | bytes 524288 | tf_op jit(solution)/shard_map/all_to_all | solution.py:369
  172.1 8.3 %shard_map.163 = (f32[256,768]{1,0:T(8,128)S(1)}, bf16[256,768]{1,0:T(8,128)(2,1)S(1)}, f32[256,768]{1,0:T(8,128)S(1)}, bf16[256,768]{1,0:T(8,128)(2,1)S(1)}, bf16[64,64,384]{2,1,0:T(8,128)(2,1)}) custom-call(s32[1]{0:T(128)} %bitcast.core_ref, bf16[8,192,512]{2,1,0:T(8,128)(2,1)} %all-to-all-done.3.back_ref, f32[384,512]{1,0:T(8,128)S(1)} %copy-done.3, ...), custom_call_target="tpu_custom_call" | custom-call | flops 3019898880 | bytes 12582912 | tf_op jit(solution)/shard_map/pallas_call | solution.py:292
  182.9 8.1 %all-to-all-start.6 = ((bf16[64,64,384]{2,1,0:T(8,128)(2,1)}), bf16[64,64,384]{2,1,0:T(8,128)(2,1)}, u32[]{:S(2)}, u32[]{:S(2)}) async-start(bf16[64,64,384]{2,1,0:T(8,128)(2,1)} %get-tuple-element.32), calls=%async_computation.6 | async-start | bytes 6291456 | tf_op jit(solution)/shard_map/all_to_all | solution.py:369
  200.8 28.5 %all-to-all-done.6 = bf16[64,64,384]{2,1,0:T(8,128)(2,1)} async-done(((bf16[64,64,384]{2,1,0:T(8,128)(2,1)}), bf16[64,64,384]{2,1,0:T(8,128)(2,1)}, u32[]{:S(2)}, u32[]{:S(2)}) %all-to-all-start.6) | async-done | bytes 3145760 | tf_op jit(solution)/shard_map/all_to_all | solution.py:369
  229.2 2.3 reduce_sum.119
  231.9 55.1 %all_to_all.42.mine_ref = bf16[64,80,384]{2,1,0:T(8,128)(2,1)} all-to-all(bf16[64,80,384]{2,1,0:T(8,128)(2,1)S(1)} %broadcast_in_dim.11), channel_id=1, replica_groups=mesh['z_lo'=2,'y'=4,'core'=2,'x'=4,'z_hi'=2] {'z_lo','y','x','z_hi'}, dimensions={0} | all-to-all | bytes 7864320 | tf_op jit(solution)/shard_map/all_to_all | solution.py:369
  287.0 3.2 collective-permute-start.5
  290.5 6.5 %collective-permute-done.3 = bf16[256,768]{1,0:T(8,128)(2,1)S(1)} collective-permute-done((bf16[256,768]{1,0:T(8,128)(2,1)S(1)}, bf16[256,768]{1,0:T(8,128)(2,1)S(1)}, u32[]{:S(2)}, u32[]{:S(2)}) %collective-permute-start.3) | collective-permute-done | bytes 393248 | tf_op jit(solution)/shard_map/ppermute | solution.py:365
  298.3 1.7 convert_bitcast_fusion
  300.1 2.7 copy.50
  302.7 2.1 slice.33
  306.3 2.1 slice.34
  308.4 2.2 stack_reshape.9
  310.6 1.7 fusion.2
  313.1 2.2 copy.57
  315.2 2.3 copy.49
  319.2 1.7 fusion.26
  320.8 14.0 %shard_map.164 = (f32[768,3072]{1,0:T(8,128)}, f32[2,384,768]{2,1,0:T(8,128)}) custom-call(s32[1]{0:T(128)} %bitcast.core_ref, bf16[64,80,384]{2,1,0:T(8,128)(2,1)} %all_to_all.42.mine_ref, bf16[64,80,384]{2,1,0:T(8,128)(2,1)} %collective-permute-done.5.other_ref), custom_call_target="tpu_custom_call" | custom-call | bytes 20971520 | tf_op jit(solution)/shard_map/pallas_call | solution.py:342
  (104 shorter events, 31.7 us)
Async XLA Ops:
  0.6 1.6 copy-start
  23.7 4.8 %copy-start.18 = (bf16[2,128,768]{2,1,0:T(8,128)(2,1)S(1)}, bf16[2,128,768]{2,1,0:T(8,128)(2,1)}, u32[]{:S(2)}) copy-start(bf16[2,128,768]{2,1,0:T(8,128)(2,1)} %param.19) | copy-start | bytes 1179652
  23.7 6.3 %copy-start.24 = (s32[2]{0:T(128)S(1)}, s32[2]{0:T(128)}, u32[]{:S(2)}) copy-start(s32[2]{0:T(128)} %param.11) | copy-start | bytes 28
  23.7 6.4 %copy-start.15 = (bf16[2,128,768]{2,1,0:T(8,128)(2,1)S(1)}, bf16[2,128,768]{2,1,0:T(8,128)(2,1)}, u32[]{:S(2)}) copy-start(bf16[2,128,768]{2,1,0:T(8,128)(2,1)} %param.10) | copy-start | bytes 1179652
  23.7 7.7 %copy-start.20 = (bf16[200,1536]{1,0:T(8,128)(2,1)S(1)}, bf16[200,1536]{1,0:T(8,128)(2,1)}, u32[]{:S(2)}) copy-start(bf16[200,1536]{1,0:T(8,128)(2,1)} %param.12) | copy-start | bytes 1843204
  23.7 31.9 %all-to-all-start.2 = ((f16[8,16,64,128]{3,2,1,0:T(8,128)(2,1)}), f16[8,16,64,128]{3,2,1,0:T(8,128)(2,1)}, u32[]{:S(2)}, u32[]{:S(2)}) async-start(f16[8,16,64,128]{3,2,1,0:T(8,128)(2,1)} %broadcast_in_dim.10), calls=%async_computation.2 | async-start | bytes 4194304 | tf_op jit(solution)/shard_map/all_to_all | solution.py:369
  28.5 3.1 collective-permute-start.1
  30.0 1.3 collective-permute-start.2
  30.1 2.8 collective-permute-start
  33.9 1.3 copy-start.1
  40.6 0.9 copy-start.2
  42.4 0.9 copy-start.6
  43.3 16.7 %copy-start.23 = (f32[16]{0:T(128)S(1)}, f32[16]{0:T(128)}, u32[]{:S(2)}) copy-start(f32[16]{0:T(128)} %param.17) | copy-start | bytes 196
  55.7 27.5 %all-to-all-start = ((bf16[8,192,512]{2,1,0:T(8,128)(2,1)}), bf16[8,192,512]{2,1,0:T(8,128)(2,1)}, u32[]{:S(2)}, u32[]{:S(2)}) async-start(bf16[8,192,512]{2,1,0:T(8,128)(2,1)} %get-tuple-element.22), calls=%async_computation | async-start | bytes 3145728 | tf_op jit(solution)/shard_map/all_to_all | solution.py:369
  60.6 22.5 %copy-start.22 = (s32[1024]{0:T(1024)S(1)}, s32[1024]{0:T(1024)}, u32[]{:S(2)}) copy-start(s32[1024]{0:T(1024)} %param.18) | copy-start | bytes 12292
  136.7 25.8 %all-to-all-start.3 = ((bf16[8,192,512]{2,1,0:T(8,128)(2,1)}), bf16[8,192,512]{2,1,0:T(8,128)(2,1)}, u32[]{:S(2)}, u32[]{:S(2)}) async-start(bf16[8,192,512]{2,1,0:T(8,128)(2,1)} %get-tuple-element.23), calls=%async_computation.3 | async-start | bytes 3145728 | tf_op jit(solution)/shard_map/all_to_all | solution.py:369
  162.5 20.4 %all-to-all-start.5 = ((bf16[16,64,128]{2,1,0:T(8,128)(2,1)}), bf16[16,64,128]{2,1,0:T(8,128)(2,1)}, u32[]{:S(2)}, u32[]{:S(2)}) async-start(bf16[16,64,128]{2,1,0:T(8,128)(2,1)} %bitcast.10), calls=%async_computation.5 | async-start | bytes 524288 | tf_op jit(solution)/shard_map/all_to_all | solution.py:369
  168.7 1.1 copy-start.3
  169.8 1.1 copy-start.5
  171.0 1.1 copy-start.7
  182.9 13.1 %copy-start.9 = (f32[256,768]{1,0:T(8,128)S(1)}, f32[256,768]{1,0:T(8,128)}, u32[]{:S(2)}) copy-start(f32[256,768]{1,0:T(8,128)} %copy-done.8) | copy-start | bytes 2359300
  182.9 46.3 %all-to-all-start.6 = ((bf16[64,64,384]{2,1,0:T(8,128)(2,1)}), bf16[64,64,384]{2,1,0:T(8,128)(2,1)}, u32[]{:S(2)}, u32[]{:S(2)}) async-start(bf16[64,64,384]{2,1,0:T(8,128)(2,1)} %get-tuple-element.32), calls=%async_computation.6 | async-start | bytes 6291456 | tf_op jit(solution)/shard_map/all_to_all | solution.py:369
  193.3 2.7 collective-permute-start.4
  196.0 2.2 copy-start.16
  197.3 0.9 copy-start.13
  231.9 65.1 %copy-start.11 = (f32[256,768]{1,0:T(8,128)S(1)}, f32[256,768]{1,0:T(8,128)}, u32[]{:S(2)}) copy-start(f32[256,768]{1,0:T(8,128)} %copy-done.10) | copy-start | bytes 2359300
  287.0 19.3 %collective-permute-start.5 = (bf16[64,80,384]{2,1,0:T(8,128)(2,1)}, bf16[64,80,384]{2,1,0:T(8,128)(2,1)}, u32[]{:S(2)}, u32[]{:S(2)}) collective-permute-start(bf16[64,80,384]{2,1,0:T(8,128)(2,1)} %all_to_all.42.mine_ref), channel_id=1, source_target_pairs={{0,8},{8,0},{1,9},{9,1},{2,10},{10,2},{3,11},{11,3},{4,12},{12,4},... | collective-permute-start | bytes 11796488 | tf_op jit(solution)/shard_map/ppermute | solution.py:365
  290.2 6.9 %copy-start.14 = (f32[256,768]{1,0:T(8,128)S(1)}, f32[256,768]{1,0:T(8,128)}, u32[]{:S(2)}) copy-start(f32[256,768]{1,0:T(8,128)} %copy-done.13) | copy-start | bytes 2359300
  290.2 6.9 %copy-start.17 = (bf16[2,128,768]{2,1,0:T(8,128)(2,1)S(1)}, bf16[2,128,768]{2,1,0:T(8,128)(2,1)}, u32[]{:S(2)}) copy-start(bf16[2,128,768]{2,1,0:T(8,128)(2,1)} %param.10) | copy-start | bytes 1179652
  290.2 7.0 %copy-start.19 = (bf16[2,128,768]{2,1,0:T(8,128)(2,1)S(1)}, bf16[2,128,768]{2,1,0:T(8,128)(2,1)}, u32[]{:S(2)}) copy-start(bf16[2,128,768]{2,1,0:T(8,128)(2,1)} %param.19) | copy-start | bytes 1179652
  290.2 6.8 %collective-permute-start.3 = (bf16[256,768]{1,0:T(8,128)(2,1)S(1)}, bf16[256,768]{1,0:T(8,128)(2,1)S(1)}, u32[]{:S(2)}, u32[]{:S(2)}) collective-permute-start(bf16[256,768]{1,0:T(8,128)(2,1)S(1)} %get-tuple-element.28), channel_id=1, source_target_pairs={{0,8},{8,0},{1,9},{9,1},{2,10},{10,2},{3,11},{11,3},{4,12},{12,4},... | collective-permute-start | bytes 1179656 | tf_op jit(solution)/shard_map/ppermute | solution.py:365
  297.0 1.3 copy-start.21
  (4 other events, 3.4 us)

commit v3 on v2

--- a/solution.py
+++ b/solution.py
@@ -21,22 +21,16 @@
     return lax.dot_general(a, b, (dims, ((), ())), preferred_element_type=f32)
 
 
-def attend_kernel(
-    factor,
-    cross_ref,
-    chain_col_ref,
-    chain_row_ref,
-    rows_ref,
-    bias_ref,
-    out_ref,
-    grad_bias_ref,
-    cross_sum_ref,
-    bias_full,
-    logits,
-    exp_half,
-    grad_half,
-    grad_sum,
-):
+def bias_block(refs, place, part):
+    dz, dy = place // 4, place % 4
+    if dy == 2:
+        return refs[5 * dz + 3 + part], 0
+    return refs[5 * dz + (0, 1, None, 2)[dy]], part
+
+
+def attend_kernel(factor, base_ref, cross_ref, chain_col_ref, chain_row_ref, rows_ref, *refs):
+    bias_refs, out_ref, grad_bias_refs = refs[:10], refs[10], refs[11:19]
+    cross_sum_ref, bias_full, logits, exp_half, grad_half, grad_sum = refs[19:]
     blocks, width, lanes = rows_ref.shape
     size = width // 4
     count = blocks * lanes
@@ -46,14 +40,17 @@
     @pl.when(step == 0)
     def _():
         cross = cross_ref[0]
-        part = bias_ref.shape[3]
+        part = (bias_refs[0].shape[1] - 16) // blocks
         for p in range(count // part):
-            at = pl.ds(part * p, part)
-            block = jnp.concatenate(
-                [bias_ref[p // 2, p % 2, t] for t in range(blocks)], axis=1
+            at = pl.ds(pl.multiple_of(base_ref[p // 2] * (2 * part), 2 * part) + part * (p % 2), part)
+            ref, first = bias_block(bias_refs, p // 2, p % 2)
+            moved = jnp.concatenate(
+                [ref[first, part * t : part * (t + 1), :].astype(f32) for t in range(blocks)], axis=1
             )
+            shifts = ref[first, part * blocks :, :].astype(f32)
+            shift = jnp.concatenate([shifts[t : t + 1] for t in range(blocks)], axis=1)
             differ = chain_col_ref[at, 0:1] != chain_row_ref[0:1, :]
-            bias_full[at, :] = block + jnp.where(differ, cross, 0.0)
+            bias_full[at, :] = (moved + shift) + jnp.where(differ, cross, 0.0)
             grad_sum[at, :] = jnp.zeros((part, count), f32)
 
     def take(index):
@@ -101,20 +98,20 @@
 
     @pl.when(step == pl.num_programs(0) - 1)
     def _():
-        part = grad_bias_ref.shape[3]
+        part = grad_bias_refs[0].shape[2]
         cross_sum = jnp.zeros((1, count), f32)
         for p in range(count // part):
-            at = pl.ds(part * p, part)
+            at = pl.ds(pl.multiple_of(base_ref[p // 2] * (2 * part), 2 * part) + part * (p % 2), part)
             block = grad_sum[at, :]
             differ = chain_col_ref[at, 0:1] != chain_row_ref[0:1, :]
             cross_sum += jnp.sum(jnp.where(differ, block, 0.0), axis=0, keepdims=True)
             half = block.astype(bf16)
             for t in range(blocks):
-                grad_bias_ref[p // 2, p % 2, t] = half[:, t * lanes : (t + 1) * lanes]
+                grad_bias_refs[p // 2][p % 2, t] = half[:, t * lanes : (t + 1) * lanes]
         cross_sum_ref[...] = jnp.broadcast_to(cross_sum, cross_sum_ref.shape)
 
 
-def attend(rows, bias, cross, chains, factor):
+def attend(base, rows, biases, cross, chains, factor):
     blocks, width, total = rows.shape
     lanes = 128
     samples = total // lanes
@@ -122,26 +119,27 @@
     chain_col = jnp.broadcast_to(chains[:, None], (count, 128))
     chain_row = jnp.broadcast_to(chains[None, :], (8, count))
     whole = lambda shape: pl.BlockSpec(shape, lambda s: (0,) * len(shape))
+    block_shape = (2, blocks, (biases[0].shape[1] - 16) // blocks, lanes)
+    once = lambda shape: pl.BlockSpec(
+        shape, lambda s: (0,) * len(shape), pipeline_mode=pl.Buffered(1)
+    )
     return pl.pallas_call(
         functools.partial(attend_kernel, factor),
         grid=(samples,),
         in_specs=[
             pl.BlockSpec(memory_space=pltpu.SMEM),
+            pl.BlockSpec(memory_space=pltpu.SMEM),
             whole(chain_col.shape),
             whole(chain_row.shape),
             pl.BlockSpec((blocks, width, lanes), lambda s: (0, 0, s)),
-            whole(bias.shape),
-        ],
-        out_specs=[
-            pl.BlockSpec((blocks, width, lanes), lambda s: (0, 0, s)),
-            whole(bias.shape),
-            whole((8, count)),
-        ],
-        out_shape=[
-            jax.ShapeDtypeStruct(rows.shape, bf16),
-            jax.ShapeDtypeStruct(bias.shape, bf16),
-            jax.ShapeDtypeStruct((8, count), f32),
-        ],
+        ]
+        + [once(bias.shape) for bias in biases],
+        out_specs=[pl.BlockSpec((blocks, width, lanes), lambda s: (0, 0, s))]
+        + [whole(block_shape)] * 8
+        + [whole((8, count))],
+        out_shape=[jax.ShapeDtypeStruct(rows.shape, bf16)]
+        + [jax.ShapeDtypeStruct(block_shape, bf16)] * 8
+        + [jax.ShapeDtypeStruct((8, count), f32)],
         scratch_shapes=[
             pltpu.VMEM((count, count), f32),
             pltpu.VMEM((count, count), f32),
@@ -149,13 +147,13 @@
             pltpu.VMEM((count, count), bf16),
             pltpu.VMEM((count, count), f32),
         ],
-        compiler_params=pltpu.CompilerParams(vmem_limit_bytes=52 * 1024 * 1024),
+        compiler_params=pltpu.CompilerParams(vmem_limit_bytes=48 * 1024 * 1024),
         cost_estimate=pl.CostEstimate(
             flops=12 * samples * count * count * 48,
             bytes_accessed=16 * 1024 * 1024,
             transcendentals=samples * count * count,
         ),
-    )(cross, chain_col, chain_row, rows, bias)
+    )(base, cross, chain_col, chain_row, rows, *biases)
 
 
 def before_kernel(factor, core_ref, acts_ref, cots_ref, mod_ref, *refs):
@@ -307,58 +305,158 @@
     )(core, *operands, *([input_weight] * 4), output_matrix)
 
 
-def assemble_kernel(core_ref, mine_ref, other_ref, input_ref, output_ref):
-    step = pl.program_id(0)
-    half = mine_ref.shape[2]
-    depth = input_ref.shape[0]
-
-    def write(position, ref):
-        for b in range(4):
-            at = (2 * b + position) * half
-            input_ref[:, at : at + half] = ref[b, :depth, :].astype(f32)
-
-        @pl.when(step < 12)
-        def _():
-            for b in range(4):
-                output_ref[
-                    position, 16 * (b // 2) : 16 * (b // 2 + 1), half * (b % 2) : half * (b % 2 + 1)
-                ] = ref[b, depth : depth + 16, :].astype(f32)
-
-    @pl.when(core_ref[0] == 0)
-    def _():
-        write(0, mine_ref)
-        write(1, other_ref)
-
-    @pl.when(core_ref[0] == 1)
-    def _():
-        write(1, mine_ref)
-        write(0, other_ref)
-
-
-def assemble(core, mine, other):
-    chips, depth, half = mine.shape
+def assemble_kernel(place_ref, block_ref, *refs):
+    input_ref, output_ref, stage, stage_out, sems = refs[-5:]
+    half = block_ref.shape[2]
+    depth = 48
+    place = place_ref[0]
+    copies = []
+    for b in range(4):
+        for group in range(2):
+            for a in range(8 * group, 8 * group + 8):
+                stage[b, depth * a : depth * (a + 1), :] = block_ref[4 * a + b, :depth, :].astype(f32)
+            rows = slice(8 * depth * group, 8 * depth * (group + 1))
+            at = pl.multiple_of((2 * b + place) * half, 128)
+            copies.append(
+                pltpu.make_async_copy(
+                    stage.at[b, rows, :],
+                    input_ref.at[rows, pl.ds(at, half)],
+                    sems.at[len(copies)],
+                )
+            )
+            copies[-1].start()
+    for d in range(half // 8):
+        stage_out[16 * (d // 2) : 16 * (d // 2 + 1), half * (d % 2) : half * (d % 2 + 1)] = block_ref[
+            d, depth : depth + 16, :
+        ].astype(f32)
+    copies.append(pltpu.make_async_copy(stage_out, output_ref.at[place], sems.at[len(copies)]))
+    copies[-1].start()
+    for copy in copies:
+        copy.wait()
+
+
+def assemble(place, gathered, earlier):
+    chips, depth, half = gathered.shape
     width = 2 * half
-    block = pl.BlockSpec((4, depth, half), lambda a, c: (a, 0, 0))
+    anywhere = pl.BlockSpec(memory_space=pl.ANY)
     return pl.pallas_call(
         assemble_kernel,
-        grid_spec=pltpu.PrefetchScalarGridSpec(
-            num_scalar_prefetch=1,
-            grid=(16,),
-            in_specs=[block, block],
-            out_specs=[
-                pl.BlockSpec((width // 16, 4 * width), lambda a, c: (a, 0)),
-                pl.BlockSpec((2, 32, width), lambda a, c: (0, jnp.minimum(a, 11), 0)),
-            ],
-        ),
+        in_specs=[
+            pl.BlockSpec(memory_space=pltpu.SMEM),
+            pl.BlockSpec(memory_space=pltpu.VMEM),
+        ]
+        + [anywhere] * len(earlier),
+        out_specs=[anywhere, anywhere],
         out_shape=[
             jax.ShapeDtypeStruct((width, 4 * width), f32),
             jax.ShapeDtypeStruct((2, half, width), f32),
         ],
-        compiler_params=pltpu.CompilerParams(vmem_limit_bytes=32 * 1024 * 1024),
+        scratch_shapes=[
+            pltpu.VMEM((4, width, half), f32),
+            pltpu.VMEM((half, width), f32),
+            pltpu.SemaphoreType.DMA((9,)),
+        ],
+        input_output_aliases={2 + k: k for k in range(len(earlier))},
+        compiler_params=pltpu.CompilerParams(vmem_limit_bytes=24 * 1024 * 1024),
         cost_estimate=pl.CostEstimate(
-            flops=0, bytes_accessed=20 * 1024 * 1024, transcendentals=0
+            flops=0, bytes_accessed=10 * 1024 * 1024, transcendentals=0
         ),
-    )(core, mine, other)
+    )(place, gathered, *earlier)
+
+
+def gather_small_kernel(block_ref, out_ref):
+    zy, rows, half = out_ref.shape
+    blocks = block_ref.shape[0] // zy
+    for p in range(zy):
+        total = block_ref[blocks * p].astype(f32)
+        for t in range(1, blocks):
+            total = total + block_ref[blocks * p + t].astype(f32)
+        out_ref[p] = total
+
+
+def gather_small(gathered, zy, small_depth):
+    chips, depth, half = gathered.shape
+    return pl.pallas_call(
+        gather_small_kernel,
+        grid=(1,),
+        in_specs=[
+            pl.BlockSpec((chips, small_depth, half), lambda i: (0, depth // small_depth - 1, 0))
+        ],
+        out_specs=pl.BlockSpec((zy, small_depth, half), lambda i: (0, 0, 0)),
+        out_shape=jax.ShapeDtypeStruct((zy, small_depth, half), f32),
+        cost_estimate=pl.CostEstimate(flops=0, bytes_accessed=1 << 20, transcendentals=0),
+    )(gathered)
+
+
+def finish_small_kernel(tokens, mine_ref, other_ref, table_ref, sums_ref):
+    zy, rows, half = mine_ref.shape
+    levels = table_ref.shape[0]
+    for r in range(4):
+        total = jnp.zeros((levels, half), f32)
+        for ref in (mine_ref, other_ref):
+            row = lax.broadcasted_iota(jnp.int32, (rows, 1), 0)
+            hot = []
+            for p in range(zy):
+                first = ref[p, 13:14, 144:145] * (1.0 / tokens)
+                second = ref[p, 13:14, 145:146] * (1.0 / tokens)
+                level = jnp.where(row < 4, first, second)
+                kept = (row < 8) & (row % 4 == r)
+                at = lax.broadcasted_iota(jnp.int32, (rows, levels), 1).astype(f32)
+                hot.append(jnp.where((level == at) & kept, 1.0, 0.0))
+            total += lax.dot_general(
+                jnp.concatenate(hot, axis=0),
+                ref[...].reshape(zy * rows, half),
+                (((0,), (0,)), ((), ())),
+                precision=lax.Precision.HIGHEST,
+                preferred_element_type=f32,
+            )
+        table_ref[:, r * half : (r + 1) * half] = total
+    sums_ref[0] = jnp.sum(mine_ref[...], axis=0)
+    sums_ref[1] = jnp.sum(other_ref[...], axis=0)
+
+
+def finish_small(mine, other, levels, tokens):
+    zy, rows, half = mine.shape
+    return pl.pallas_call(
+        functools.partial(finish_small_kernel, tokens),
+        out_shape=[
+            jax.ShapeDtypeStruct((levels, 4 * half), f32),
+            jax.ShapeDtypeStruct((2, rows, half), f32),
+        ],
+        cost_estimate=pl.CostEstimate(flops=0, bytes_accessed=2 << 20, transcendentals=0),
+    )(mine, other)
+
+
+def ring(array, shift):
+    return lax.ppermute(array, "y", [(i, (i + shift) % 4) for i in range(4)])
+
+
+def other_z(array):
+    return lax.ppermute(array, "z_lo", [(0, 1), (1, 0)])
+
+
+def spread_bias(own, far):
+    result = []
+    for block in (own, far):
+        above = ring(block, 3)
+        below = ring(block, 1)
+        result += [block, above, below, ring(below[:1], 1), ring(above[1:], 3)]
+    return result
+
+
+def sum_bias(parts):
+    add = lambda *arrays: sum(a.astype(f32) for a in arrays)
+    ends = []
+    for dz in (1, 0):
+        near, above, far, below = parts[4 * dz : 4 * dz + 4]
+        from_below = ring(far[:1], 1)
+        from_above = ring(far[1:], 3)
+        above = jnp.concatenate([add(above[:1], from_below).astype(bf16), above[1:]], axis=0)
+        below = jnp.concatenate([below[:1], add(below[1:], from_above).astype(bf16)], axis=0)
+        total = add(near, ring(above, 1), ring(below, 3))
+        ends.append(total)
+    far, near = ends
+    return near + other_z(far.astype(bf16)).astype(f32)
 
 
 def swap(array):
@@ -399,9 +497,22 @@
     half = width // 2
 
     pair_part = jnp.einsum("ijc,ch->hji", pair_feats, pair_weight, preferred_element_type=f32)
-    bias_own = exchange(pair_part.astype(jnp.float16), head_axes)
-    bias = spread(bias_own, column_axes, zy_count).astype(f32)
-    bias = bias.reshape(zy_count, 2, blocks, col_count, row_count)
+    shift = jnp.max(pair_part, axis=1, keepdims=True).astype(bf16)
+    moved = (pair_part - shift.astype(f32)).astype(bf16)
+    bias_sent = jnp.concatenate(
+        [moved, jnp.broadcast_to(shift, (heads, 16, row_count))], axis=1
+    )
+    bias_got = exchange(bias_sent, head_axes)
+    bias_own = jnp.concatenate(
+        [
+            bias_got[:, :col_count].reshape(2, blocks * col_count, row_count),
+            bias_got[:, col_count].reshape(2, blocks, row_count),
+            bias_got[:, col_count].reshape(2, blocks, row_count),
+        ],
+        axis=1,
+    )
+    bias_own = lax.optimization_barrier(bias_own)
+    bias_far = other_z(bias_own)
 
     rows = own_samples * 2 * row_count
     core_at = jnp.reshape(core, (1,)).astype(jnp.int32)
@@ -416,9 +527,17 @@
     sent, gate_open, grad_gated, normed = before(
         core_at, acts, cots, modulation, input_weight, output_matrix, blocks, factor
     )
+    sent, bias_own, bias_far = lax.optimization_barrier((sent, bias_own, bias_far))
+    biases = spread_bias(bias_own, bias_far)
     head_rows = exchange(sent, token_axes)
+    z_at, y_at = lax.axis_index("z_lo"), lax.axis_index("y")
+    base = jnp.stack(
+        [((z_at + p // 4) % 2) * 4 + (y_at + p % 4) % 4 for p in range(8)]
+    ).astype(jnp.int32)
     own_cross = lax.dynamic_slice_in_dim(cross_bias, core * blocks + token, 1)
-    head_grads, grad_bias, cross_sum = attend(head_rows, bias, own_cross, chains, factor)
+    head_grads, *grad_biases, cross_sum = attend(
+        base, head_rows, biases, own_cross, chains, factor
+    )
 
     back = exchange(head_grads, token_axes)
     own_normed, other_normed, own_output, other_output, payload = after(
@@ -445,8 +564,7 @@
         )
     ).astype(bf16)
 
-    bias_parts = exchange(grad_bias, column_axes)
-    bias_sum = jnp.sum(bias_parts.astype(f32), axis=0).astype(bf16)
+    bias_sum = sum_bias(grad_biases).astype(bf16)
     grad_bias_half = exchange(bias_sum.reshape(heads, col_count, row_count), head_axes)
     grad_pair = jnp.einsum(
         "hji,ch->ijc", grad_bias_half, pair_weight, preferred_element_type=f32
@@ -460,8 +578,9 @@
     pair_size = pair_weight.shape[0] * heads
     cross_part = jnp.sum(cross_sum[0])
     cross_high = cross_part.astype(bf16).astype(f32)
+    at_token = (jnp.arange(blocks) == token).astype(f32)
     last = jnp.concatenate(
-        [jnp.stack([cross_high, cross_part - cross_high]), levels.astype(f32)]
+        [at_token * cross_high, at_token * (cross_part - cross_high), levels.astype(f32)]
     )
     flat = jnp.concatenate([grad_scale, grad_shift], axis=1).reshape(-1)
     flat = jnp.concatenate([flat, grad_pair_part.reshape(-1), last])
@@ -469,29 +588,22 @@
     small = jnp.pad(flat, (0, small_depth * half - flat.size)).reshape(small_depth, half)
     block = jnp.concatenate([summed, small.astype(bf16)], axis=0)
     gathered = spread(block, chip_axes, chip_count)
+    pair_shape = grad_pair.shape
+    gathered, updated, grad_tokens, grad_pair = lax.optimization_barrier(
+        (gathered, updated, grad_tokens, grad_pair.reshape(-1, pair_shape[2]))
+    )
+    grad_pair = grad_pair.reshape(pair_shape)
+    mine_small = gather_small(gathered, zy_count, small_depth)
     other = swap(gathered)
-    input_weight_grad, output_weight_grad = assemble(core_at, gathered, other)
+    other_small = swap(mine_small)
+    earlier = assemble(core_at, gathered, ())
+    input_weight_grad, output_weight_grad = assemble(1 - core_at, other, earlier)
     output_weight_grad = output_weight_grad.reshape(width, width)
-    mine_small = gathered[:, -small_depth:].reshape(zy_count, blocks, small_depth * half)
-    other_small = other[:, -small_depth:].reshape(zy_count, blocks, small_depth * half)
-    small_all = jnp.where(
-        core == 0, jnp.stack([mine_small, other_small]), jnp.stack([other_small, mine_small])
-    ).astype(f32)
-    line = 2 * width
-    table_all = jnp.sum(small_all[..., : own_samples * line], axis=2)
-    table_all = table_all.reshape(2, zy_count, own_samples, line)
-    table_all = table_all.transpose(1, 0, 2, 3).reshape(-1, line)
-    at = own_samples * line
-    grad_pair_weight = jnp.sum(small_all[..., at : at + pair_size], axis=(0, 1, 2)).reshape(
-        pair_weight.shape
-    )
-    at = at + pair_size
-    grad_cross = jnp.sum(small_all[..., at : at + 2], axis=(1, 3)).reshape(-1)
-    level_all = small_all[:, :, 0, at + 2 : at + 2 + own_samples].transpose(1, 0, 2).reshape(-1)
-    onehot_all = (
-        level_all[None, :] == jnp.arange(level_count, dtype=f32)[:, None]
-    ).astype(f32)
-    grad_table = jnp.dot(onehot_all, table_all, precision=lax.Precision.HIGHEST)
+    grad_table, sums = finish_small(mine_small, other_small, level_count, blocks)
+    pair_rows = (sums[0] + sums[1])[8:].reshape(-1)
+    grad_pair_weight = pair_rows[:pair_size].reshape(pair_weight.shape)
+    crosses = sums[:, 13, 128:144].reshape(2, 2, blocks).sum(axis=1)
+    grad_cross = jnp.where(core == 0, crosses, crosses[::-1]).reshape(-1)
     return (
         updated,
         grad_tokens,

time: 337 us -> 290 us (0.86)
  blocking collectives: 103 us -> 0 us
  starting transfers between devices: 34 us -> 81.1 us
  waiting for transfers between devices: 85.2 us -> 91.5 us
  other arithmetic: 19.8 us -> 15.4 us
    all_to_all x3 -> x0, blocking collectives: 103 us -> none  [exchange(): return lax.all_to_all(array, axes, 0, 0, tiled=True)]
    ppermute x0 -> x18, starting transfers between devices: none -> 24.1 us  [the longest x16 22.5 us: ring(): return lax.ppermute(array, 'y', [(i, (i + shift) % 4) for i in range(4)])]
    all_to_all x5 -> x6, starting transfers between devices: 27.8 us -> 51 us  [exchange(): return lax.all_to_all(array, axes, 0, 0, tiled=True)]
    ppermute x0 -> x18, waiting for transfers between devices: none -> 17.7 us  [the longest x16 14.4 us: ring(): return lax.ppermute(array, 'y', [(i, (i + shift) % 4) for i in range(4)])]
    ppermute x6 -> x7, waiting for transfers between devices: 7.36 us -> 0.34 us  [swap(): return lax.ppermute(array, 'core', [(0, 1), (1, 0)])]
    all_to_all x5 -> x6, waiting for transfers between devices: 77.9 us -> 73.5 us  [exchange(): return lax.all_to_all(array, axes, 0, 0, tiled=True)]
    reshape x1 -> x0, other arithmetic: 4.12 us -> none  [shards(): bias = bias.reshape(zy_count, 2, blocks, col_count, row_count)]
    another operation x2, local copies, waits for them, and re-layouts: 3.68 us -> 0.17 us  [the longest x1 0.08 us: shards(): crosses = sums[:, 13, 128:144].reshape(2, 2, blocks).sum(axis=1)]
  transfers between devices with their start and end apart: 11 -> 31, of which waited for: 6 -> 14; matrix products, arithmetic and copies ran while one was open for 8% -> 12% of each run, Pallas kernels for 4% -> 9%
where the time goes in v3:
time: 290 us; the launch traced here: 286 us
  waiting for transfers between devices  91.5 us (32%)
  starting transfers between devices  81.1 us (28%)
  Pallas kernels  51.9 us (18%)
  local copies, waits for them, and re-layouts  37 us (13%)
  other arithmetic  15.4 us (5%)
  matrix products  6.4 us (2%)
    all_to_all x6, waiting for transfers between devices, exchange(): return lax.all_to_all(array, axes, 0, 0, tiled=True)  73.5 us
    all_to_all x6, starting transfers between devices, exchange(): return lax.all_to_all(array, axes, 0, 0, tiled=True)  51 us
    ppermute x16, starting transfers between devices, ring(): return lax.ppermute(array, 'y', [(i, (i + shift) % 4) for i in range(4)])  22.5 us
    pallas_call x1, Pallas kernels, attend(): pl.pallas_call(functools.partial(attend_kernel, factor), grid=(samples,),...  21.8 us
    unnamed x82, local copies, waits for them, and re-layouts  20.8 us
    ppermute x16, waiting for transfers between devices, ring(): return lax.ppermute(array, 'y', [(i, (i + shift) % 4) for i in range(4)])  14.4 us
    pallas_call x2, Pallas kernels, assemble(): pl.pallas_call(assemble_kernel, in_specs=[pl.BlockSpec(memory_space=pltpu...  9.59 us
    pallas_call x1, Pallas kernels, after(): pl.pallas_call(after_kernel, grid_spec=pltpu.PrefetchScalarGridSpec(num_s...  8.26 us
  transfers between devices with their start and end apart: 31, of which 14 were waited for; matrix products, arithmetic and copies ran while one was open for 12% of the time, Pallas kernels for 9%

profile of v3, /device:TPU:1, one launch (start us, length us, event | category | flops | bytes accessed | tf_op | source)
XLA Modules:
  0.0 286.1 jit_solution(16582090806826083671)
XLA Ops:
  5.5 8.8 %all-to-all-start = ((bf16[16,80,128]{2,1,0:T(8,128)(2,1)}), bf16[16,80,128]{2,1,0:T(8,128)(2,1)S(1)}, u32[]{:S(2)}, u32[]{:S(2)}) async-start(bf16[16,80,128]{2,1,0:T(8,128)(2,1)} %copy.41), calls=%async_computation | async-start | bytes 655360 | tf_op jit(solution)/shard_map/all_to_all | solution.py:467
  15.7 7.9 %all-to-all-done = bf16[16,80,128]{2,1,0:T(8,128)(2,1)S(1)} async-done(((bf16[16,80,128]{2,1,0:T(8,128)(2,1)}), bf16[16,80,128]{2,1,0:T(8,128)(2,1)S(1)}, u32[]{:S(2)}, u32[]{:S(2)}) %all-to-all-start) | async-done | bytes 327712 | tf_op jit(solution)/shard_map/all_to_all | solution.py:467
  27.1 5.5 %shard_map.161 = (bf16[8,192,512]{2,1,0:T(8,128)(2,1)}, f32[384,512]{1,0:T(8,128)S(1)}, f32[384,512]{1,0:T(8,128)S(1)}, bf16[512,768]{1,0:T(8,128)(2,1)S(1)}) custom-call(s32[1]{0:T(128)} %bitcast.core_ref.place_ref, bf16[512,768]{1,0:T(8,128)(2,1)S(1)} %bitcast.56, bf16[512,768]{1,0:T(8,128)(2,1)S(1)} %bitcast.54, f32[4,1536]{1,0:T(4,128)S(1)} %fusion.24.mod_ref, ...), custom_call_target="tpu_custom_call" | custom-call | flops 1509949440 | bytes 8388608 | tf_op jit(solution)/shard_map/pallas_call | solution.py:215
  35.9 4.3 %all-to-all-start.1 = ((bf16[8,192,512]{2,1,0:T(8,128)(2,1)}), bf16[8,192,512]{2,1,0:T(8,128)(2,1)}, u32[]{:S(2)}, u32[]{:S(2)}) async-start(bf16[8,192,512]{2,1,0:T(8,128)(2,1)} %get-tuple-element.41), calls=%async_computation.1 | async-start | bytes 3145728 | tf_op jit(solution)/shard_map/all_to_all | solution.py:467
  43.1 2.7 collective-permute-start.8
  45.8 2.5 collective-permute-done.5.refs_2_
  49.8 2.7 collective-permute-start.7
  56.2 2.6 collective-permute-start.11
  68.7 21.8 %shard_map.162 = (bf16[8,192,512]{2,1,0:T(8,128)(2,1)}, bf16[2,8,64,128]{3,2,1,0:T(8,128)(2,1)S(1)}, bf16[2,8,64,128]{3,2,1,0:T(8,128)(2,1)S(1)}, bf16[2,8,64,12...) custom-call(s32[8]{0:T(128)S(1)} %stack.35.base_ref, ...), custom_call_target="tpu_custom_call" | custom-call | flops 2415919104 | bytes 16777216 | tf_op jit(solution)/shard_map/pallas_call | solution.py:126
  93.2 5.0 %all-to-all-start.2 = ((bf16[8,192,512]{2,1,0:T(8,128)(2,1)}), bf16[8,192,512]{2,1,0:T(8,128)(2,1)}, u32[]{:S(2)}, u32[]{:S(2)}) async-start(bf16[8,192,512]{2,1,0:T(8,128)(2,1)} %get-tuple-element.44), calls=%async_computation.2 | async-start | bytes 3145728 | tf_op jit(solution)/shard_map/all_to_all | solution.py:467
  99.3 3.2 %collective-permute-start.19 = (bf16[1,8,64,128]{3,2,1,0:T(8,128)(2,1)S(1)}, bf16[1,8,64,128]{3,2,1,0:T(8,128)(2,1)S(1)}, u32[]{:S(2)}, u32[]{:S(2)}) collective-permute-start(bf16[1,8,64,128]{3,2,1,0:T(8,128)(2,1)S(1)} %get-tuple-element.104), channel_id=1, source_target_pairs={{0,48},{16,0},{32,16},{48,32},{1,49},{17,1},{33,17},{49,33},{2,50}... | collective-permute-start | bytes 393224 | tf_op jit(solution)/shard_map/ppermute | solution.py:431
  103.6 2.7 collective-permute-start.15
  106.4 2.7 collective-permute-start.20
  109.1 2.6 collective-permute-done.17
  112.0 2.7 collective-permute-start.16
  114.9 5.2 %collective-permute-done.18 = bf16[2,8,64,128]{3,2,1,0:T(8,128)(2,1)S(1)} collective-permute-done((bf16[2,8,64,128]{3,2,1,0:T(8,128)(2,1)S(1)}, bf16[2,8,64,128]{3,2,1,0:T(8,128)(2,1)S(1)}, u32[]{:S(2)}, u32[]{:S(2)}) %collective-permute-start.18) | collective-permute-done | bytes 262176 | tf_op jit(solution)/shard_map/ppermute | solution.py:431
  122.5 3.3 %collective-permute-done.21 = bf16[2,8,64,128]{3,2,1,0:T(8,128)(2,1)S(1)} collective-permute-done((bf16[2,8,64,128]{3,2,1,0:T(8,128)(2,1)S(1)}, bf16[2,8,64,128]{3,2,1,0:T(8,128)(2,1)S(1)}, u32[]{:S(2)}, u32[]{:S(2)}) %collective-permute-start.21) | collective-permute-done | bytes 262176 | tf_op jit(solution)/shard_map/ppermute | solution.py:435
  126.7 15.8 %all-to-all-start.4 = ((bf16[16,64,128]{2,1,0:T(8,128)(2,1)}), bf16[16,64,128]{2,1,0:T(8,128)(2,1)}, u32[]{:S(2)}, u32[]{:S(2)}) async-start(bf16[16,64,128]{2,1,0:T(8,128)(2,1)} %bitcast.16), calls=%async_computation.4 | async-start | bytes 524288 | tf_op jit(solution)/shard_map/all_to_all | solution.py:467
  147.0 8.3 %shard_map.163 = (f32[256,768]{1,0:T(8,128)S(1)}, bf16[256,768]{1,0:T(8,128)(2,1)S(1)}, f32[256,768]{1,0:T(8,128)S(1)}, bf16[256,768]{1,0:T(8,128)(2,1)S(1)}, bf16[64,64,384]{2,1,0:T(8,128)(2,1)}) custom-call(s32[1]{0:T(128)} %bitcast.core_ref.place_ref, bf16[8,192,512]{2,1,0:T(8,128)(2,1)} %all-to-all-done.2.back_ref, f32[384,512]{1,0:T(8,128)S(1)} %copy-done.5, ...), custom_call_target="tpu_custom_call" | custom-call | flops 3019898880 | bytes 12582912 | tf_op jit(solution)/shard_map/pallas_call | solution.py:290
  156.9 7.9 %all-to-all-start.3 = ((bf16[64,64,384]{2,1,0:T(8,128)(2,1)}), bf16[64,64,384]{2,1,0:T(8,128)(2,1)}, u32[]{:S(2)}, u32[]{:S(2)}) async-start(bf16[64,64,384]{2,1,0:T(8,128)(2,1)} %get-tuple-element.48), calls=%async_computation.3 | async-start | bytes 6291456 | tf_op jit(solution)/shard_map/all_to_all | solution.py:467
  169.9 2.1 copy.43
  176.5 26.7 %all-to-all-done.3 = bf16[64,64,384]{2,1,0:T(8,128)(2,1)} async-done(((bf16[64,64,384]{2,1,0:T(8,128)(2,1)}), bf16[64,64,384]{2,1,0:T(8,128)(2,1)}, u32[]{:S(2)}, u32[]{:S(2)}) %all-to-all-start.3) | async-done | bytes 3145760 | tf_op jit(solution)/shard_map/all_to_all | solution.py:467
  203.1 2.3 reduce_sum.84
  205.5 2.3 broadcast_in_dim.11
  207.7 9.1 %all-to-all-start.5 = ((bf16[64,80,384]{2,1,0:T(8,128)(2,1)}), bf16[64,80,384]{2,1,0:T(8,128)(2,1)}, u32[]{:S(2)}, u32[]{:S(2)}) async-start(bf16[64,80,384]{2,1,0:T(8,128)(2,1)} %broadcast_in_dim.11), calls=%async_computation.5 | async-start | bytes 7864320 | tf_op jit(solution)/shard_map/all_to_all | solution.py:467
  218.6 2.7 copy.46
  223.9 2.2 fusion.17
  226.1 37.3 %all-to-all-done.5.block_ref = bf16[64,80,384]{2,1,0:T(8,128)(2,1)} async-done(((bf16[64,80,384]{2,1,0:T(8,128)(2,1)}), bf16[64,80,384]{2,1,0:T(8,128)(2,1)}, u32[]{:S(2)}, u32[]{:S(2)}) %all-to-all-start.5) | async-done | bytes 3932192 | tf_op jit(solution)/shard_map/all_to_all | solution.py:467
  263.3 2.2 collective-permute-start.23
  267.5 4.8 %shard_map.164 = (f32[768,3072]{1,0:T(8,128)}, f32[2,384,768]{2,1,0:T(8,128)}) custom-call(s32[1]{0:T(128)} %bitcast.core_ref.place_ref, bf16[64,80,384]{2,1,0:T(8,128)(2,1)} %all-to-all-done.5.block_ref), custom_call_target="tpu_custom_call" | custom-call | bytes 10485760 | tf_op jit(solution)/shard_map/pallas_call | solution.py:342
  273.1 4.9 %shard_map.167 = (f32[200,1536]{1,0:T(8,128)}, f32[2,16,384]{2,1,0:T(8,128)}) custom-call(f32[8,16,384]{2,1,0:T(8,128)} %shard_map.166.mine_ref, f32[8,16,384]{2,1,0:T(8,128)} %copy-done.35), custom_call_target="tpu_custom_call" | custom-call | bytes 2097152 | tf_op jit(solution)/shard_map/pallas_call | solution.py:420
  281.1 4.8 %shard_map.165 = (f32[768,3072]{1,0:T(8,128)}, f32[2,384,768]{2,1,0:T(8,128)}) custom-call(s32[1]{0:T(128)S(6)} %sub.41.place_ref, bf16[64,80,384]{2,1,0:T(8,128)(2,1)} %collective-permute-done.23.block_ref, f32[768,3072]{1,0:T(8,128)} %get-tuple-element.66.refs_0_, ...), custom_call_target="tpu_custom_call", output_to_operand_aliasing={{0}: (2, {}), {1}: (3, {})} | custom-call | bytes 10485760 | tf_op jit(solution)/shard_map/pallas_call | solution.py:342
  (195 shorter events, 63.8 us)
Async XLA Ops:
  0.7 13.7 %collective-permute-start.2 = (s32[2]{0:T(128)}, s32[2]{0:T(128)S(1)}, u32[]{:S(2)}, u32[]{:S(2)}) collective-permute-start(s32[2]{0:T(128)} %param.11), channel_id=1, source_target_pairs={{0,8},{8,0},{1,9},{9,1},{2,10},{10,2},{3,11},{11,3},{4,12},{12,4},... | collective-permute-start | bytes 32 | tf_op jit(solution)/shard_map/ppermute | solution.py:463
  2.2 22.4 %collective-permute-start.1 = (bf16[2,128,768]{2,1,0:T(8,128)(2,1)}, bf16[2,128,768]{2,1,0:T(8,128)(2,1)}, u32[]{:S(2)}, u32[]{:S(2)}) collective-permute-start(bf16[2,128,768]{2,1,0:T(8,128)(2,1)} %param.19), channel_id=1, source_target_pairs={{0,8},{8,0},{1,9},{9,1},{2,10},{10,2},{3,11},{11,3},{4,12},{12,4},... | collective-permute-start | bytes 1179656 | tf_op jit(solution)/shard_map/ppermute | solution.py:463
  2.3 23.5 %collective-permute-start = (bf16[2,128,768]{2,1,0:T(8,128)(2,1)}, bf16[2,128,768]{2,1,0:T(8,128)(2,1)}, u32[]{:S(2)}, u32[]{:S(2)}) collective-permute-start(bf16[2,128,768]{2,1,0:T(8,128)(2,1)} %param.10), channel_id=1, source_target_pairs={{0,8},{8,0},{1,9},{9,1},{2,10},{10,2},{3,11},{11,3},{4,12},{12,4},... | collective-permute-start | bytes 1179656 | tf_op jit(solution)/shard_map/ppermute | solution.py:463
  5.5 18.1 %all-to-all-start = ((bf16[16,80,128]{2,1,0:T(8,128)(2,1)}), bf16[16,80,128]{2,1,0:T(8,128)(2,1)S(1)}, u32[]{:S(2)}, u32[]{:S(2)}) async-start(bf16[16,80,128]{2,1,0:T(8,128)(2,1)} %copy.41), calls=%async_computation | async-start | bytes 655360 | tf_op jit(solution)/shard_map/all_to_all | solution.py:467
  23.7 11.5 %collective-permute-start.3 = (bf16[2,528,128]{2,1,0:T(8,128)(2,1)S(1)}, bf16[2,528,128]{2,1,0:T(8,128)(2,1)S(1)}, u32[]{:S(2)}, u32[]{:S(2)}) collective-permute-start(bf16[2,528,128]{2,1,0:T(8,128)(2,1)S(1)} %pad_maximum_fusion.3.refs_0_), channel_id=1, source_target_pairs={{0,64},{64,0},{1,65},{65,1},{2,66},{66,2},{3,67},{67,3},{4,68},{68... | collective-permute-start | bytes 811016 | tf_op jit(solution)/shard_map/ppermute | solution.py:435
  35.2 27.5 %copy-start.37 = (s32[1024]{0:T(1024)S(1)}, s32[1024]{0:T(1024)}, u32[]{:S(2)}) copy-start(s32[1024]{0:T(1024)} %param.18) | copy-start | bytes 12292
  35.9 26.8 %all-to-all-start.1 = ((bf16[8,192,512]{2,1,0:T(8,128)(2,1)}), bf16[8,192,512]{2,1,0:T(8,128)(2,1)}, u32[]{:S(2)}, u32[]{:S(2)}) async-start(bf16[8,192,512]{2,1,0:T(8,128)(2,1)} %get-tuple-element.41), calls=%async_computation.1 | async-start | bytes 3145728 | tf_op jit(solution)/shard_map/all_to_all | solution.py:467
  40.2 8.1 %collective-permute-start.5 = (bf16[2,528,128]{2,1,0:T(8,128)(2,1)S(1)}, bf16[2,528,128]{2,1,0:T(8,128)(2,1)S(1)}, u32[]{:S(2)}, u32[]{:S(2)}) collective-permute-start(bf16[2,528,128]{2,1,0:T(8,128)(2,1)S(1)} %pad_maximum_fusion.3.refs_0_), channel_id=1, source_target_pairs={{0,16},{16,32},{32,48},{48,0},{1,17},{17,33},{33,49},{49,1},{2,18}... | collective-permute-start | bytes 811016 | tf_op jit(solution)/shard_map/ppermute | solution.py:431
  41.6 7.4 %collective-permute-start.4 = (bf16[2,528,128]{2,1,0:T(8,128)(2,1)S(1)}, bf16[2,528,128]{2,1,0:T(8,128)(2,1)S(1)}, u32[]{:S(2)}, u32[]{:S(2)}) collective-permute-start(bf16[2,528,128]{2,1,0:T(8,128)(2,1)S(1)} %pad_maximum_fusion.3.refs_0_), channel_id=1, source_target_pairs={{0,48},{16,0},{32,16},{48,32},{1,49},{17,1},{33,17},{49,33},{2,50}... | collective-permute-start | bytes 811016 | tf_op jit(solution)/shard_map/ppermute | solution.py:431
  43.1 10.9 %collective-permute-start.9 = (bf16[2,528,128]{2,1,0:T(8,128)(2,1)}, bf16[2,528,128]{2,1,0:T(8,128)(2,1)S(1)}, u32[]{:S(2)}, u32[]{:S(2)}) collective-permute-start(bf16[2,528,128]{2,1,0:T(8,128)(2,1)} %copy-done.27), channel_id=1, source_target_pairs={{0,16},{16,32},{32,48},{48,0},{1,17},{17,33},{33,49},{49,1},{2,18}... | collective-permute-start | bytes 811016 | tf_op jit(solution)/shard_map/ppermute | solution.py:431
  43.1 11.7 %collective-permute-start.8 = (bf16[2,528,128]{2,1,0:T(8,128)(2,1)}, bf16[2,528,128]{2,1,0:T(8,128)(2,1)S(1)}, u32[]{:S(2)}, u32[]{:S(2)}) collective-permute-start(bf16[2,528,128]{2,1,0:T(8,128)(2,1)} %copy-done.27), channel_id=1, source_target_pairs={{0,48},{16,0},{32,16},{48,32},{1,49},{17,1},{33,17},{49,33},{2,50}... | collective-permute-start | bytes 811016 | tf_op jit(solution)/shard_map/ppermute | solution.py:431
  49.1 10.5 %collective-permute-start.6 = (bf16[1,528,128]{2,1,0:T(8,128)(2,1)}, bf16[1,528,128]{2,1,0:T(8,128)(2,1)S(1)}, u32[]{:S(2)}, u32[]{:S(2)}) collective-permute-start(bf16[1,528,128]{2,1,0:T(8,128)(2,1)} %slice.108), channel_id=1, source_target_pairs={{0,16},{16,32},{32,48},{48,0},{1,17},{17,33},{33,49},{49,1},{2,18}... | collective-permute-start | bytes 405512 | tf_op jit(solution)/shard_map/ppermute | solution.py:431
  49.8 10.4 %collective-permute-start.7 = (bf16[1,528,128]{2,1,0:T(8,128)(2,1)}, bf16[1,528,128]{2,1,0:T(8,128)(2,1)}, u32[]{:S(2)}, u32[]{:S(2)}) collective-permute-start(bf16[1,528,128]{2,1,0:T(8,128)(2,1)} %slice.109), channel_id=1, source_target_pairs={{0,48},{16,0},{32,16},{48,32},{1,49},{17,1},{33,17},{49,33},{2,50}... | collective-permute-start | bytes 405512 | tf_op jit(solution)/shard_map/ppermute | solution.py:431
  54.7 5.9 %collective-permute-start.10 = (bf16[1,528,128]{2,1,0:T(8,128)(2,1)}, bf16[1,528,128]{2,1,0:T(8,128)(2,1)}, u32[]{:S(2)}, u32[]{:S(2)}) collective-permute-start(bf16[1,528,128]{2,1,0:T(8,128)(2,1)} %slice.110), channel_id=1, source_target_pairs={{0,16},{16,32},{32,48},{48,0},{1,17},{17,33},{33,49},{49,1},{2,18}... | collective-permute-start | bytes 405512 | tf_op jit(solution)/shard_map/ppermute | solution.py:431
  56.2 4.9 %collective-permute-start.11 = (bf16[1,528,128]{2,1,0:T(8,128)(2,1)}, bf16[1,528,128]{2,1,0:T(8,128)(2,1)}, u32[]{:S(2)}, u32[]{:S(2)}) collective-permute-start(bf16[1,528,128]{2,1,0:T(8,128)(2,1)} %slice.111), channel_id=1, source_target_pairs={{0,48},{16,0},{32,16},{48,32},{1,49},{17,1},{33,17},{49,33},{2,50}... | collective-permute-start | bytes 405512 | tf_op jit(solution)/shard_map/ppermute | solution.py:431
  93.2 33.5 %all-to-all-start.2 = ((bf16[8,192,512]{2,1,0:T(8,128)(2,1)}), bf16[8,192,512]{2,1,0:T(8,128)(2,1)}, u32[]{:S(2)}, u32[]{:S(2)}) async-start(bf16[8,192,512]{2,1,0:T(8,128)(2,1)} %get-tuple-element.44), calls=%async_computation.2 | async-start | bytes 3145728 | tf_op jit(solution)/shard_map/all_to_all | solution.py:467
  99.3 7.0 %collective-permute-start.19 = (bf16[1,8,64,128]{3,2,1,0:T(8,128)(2,1)S(1)}, bf16[1,8,64,128]{3,2,1,0:T(8,128)(2,1)S(1)}, u32[]{:S(2)}, u32[]{:S(2)}) collective-permute-start(bf16[1,8,64,128]{3,2,1,0:T(8,128)(2,1)S(1)} %get-tuple-element.104), channel_id=1, source_target_pairs={{0,48},{16,0},{32,16},{48,32},{1,49},{17,1},{33,17},{49,33},{2,50}... | collective-permute-start | bytes 393224 | tf_op jit(solution)/shard_map/ppermute | solution.py:431
  103.5 11.2 %collective-permute-start.13 = (bf16[1,8,64,128]{3,2,1,0:T(8,128)(2,1)S(1)}, bf16[1,8,64,128]{3,2,1,0:T(8,128)(2,1)S(1)}, u32[]{:S(2)}, u32[]{:S(2)}) collective-permute-start(bf16[1,8,64,128]{3,2,1,0:T(8,128)(2,1)S(1)} %get-tuple-element.101), channel_id=1, source_target_pairs={{0,16},{16,32},{32,48},{48,0},{1,17},{17,33},{33,49},{49,1},{2,18}... | collective-permute-start | bytes 393224 | tf_op jit(solution)/shard_map/ppermute | solution.py:431
  103.6 8.3 %collective-permute-start.15 = (bf16[1,8,64,128]{3,2,1,0:T(8,128)(2,1)S(1)}, bf16[1,8,64,128]{3,2,1,0:T(8,128)(2,1)S(1)}, u32[]{:S(2)}, u32[]{:S(2)}) collective-permute-start(bf16[1,8,64,128]{3,2,1,0:T(8,128)(2,1)S(1)} %get-tuple-element.102), channel_id=1, source_target_pairs={{0,48},{16,0},{32,16},{48,32},{1,49},{17,1},{33,17},{49,33},{2,50}... | collective-permute-start | bytes 393224 | tf_op jit(solution)/shard_map/ppermute | solution.py:431
  106.3 5.4 %collective-permute-start.17 = (bf16[1,8,64,128]{3,2,1,0:T(8,128)(2,1)S(1)}, bf16[1,8,64,128]{3,2,1,0:T(8,128)(2,1)S(1)}, u32[]{:S(2)}, u32[]{:S(2)}) collective-permute-start(bf16[1,8,64,128]{3,2,1,0:T(8,128)(2,1)S(1)} %get-tuple-element.103), channel_id=1, source_target_pairs={{0,16},{16,32},{32,48},{48,0},{1,17},{17,33},{33,49},{49,1},{2,18}... | collective-permute-start | bytes 393224 | tf_op jit(solution)/shard_map/ppermute | solution.py:431
  106.4 8.5 %collective-permute-start.20 = (bf16[2,8,64,128]{3,2,1,0:T(8,128)(2,1)S(1)}, bf16[2,8,64,128]{3,2,1,0:T(8,128)(2,1)S(1)}, u32[]{:S(2)}, u32[]{:S(2)}) collective-permute-start(bf16[2,8,64,128]{3,2,1,0:T(8,128)(2,1)S(1)} %pad_maximum_fusion.7), channel_id=1, source_target_pairs={{0,48},{16,0},{32,16},{48,32},{1,49},{17,1},{33,17},{49,33},{2,50}... | collective-permute-start | bytes 786440 | tf_op jit(solution)/shard_map/ppermute | solution.py:431
  111.8 8.3 %collective-permute-start.18 = (bf16[2,8,64,128]{3,2,1,0:T(8,128)(2,1)S(1)}, bf16[2,8,64,128]{3,2,1,0:T(8,128)(2,1)S(1)}, u32[]{:S(2)}, u32[]{:S(2)}) collective-permute-start(bf16[2,8,64,128]{3,2,1,0:T(8,128)(2,1)S(1)} %pad_maximum_fusion.6), channel_id=1, source_target_pairs={{0,16},{16,32},{32,48},{48,0},{1,17},{17,33},{33,49},{49,1},{2,18}... | collective-permute-start | bytes 786440 | tf_op jit(solution)/shard_map/ppermute | solution.py:431
  112.0 9.1 %collective-permute-start.16 = (bf16[2,8,64,128]{3,2,1,0:T(8,128)(2,1)S(1)}, bf16[2,8,64,128]{3,2,1,0:T(8,128)(2,1)S(1)}, u32[]{:S(2)}, u32[]{:S(2)}) collective-permute-start(bf16[2,8,64,128]{3,2,1,0:T(8,128)(2,1)S(1)} %pad_maximum_fusion.5), channel_id=1, source_target_pairs={{0,48},{16,0},{32,16},{48,32},{1,49},{17,1},{33,17},{49,33},{2,50}... | collective-permute-start | bytes 786440 | tf_op jit(solution)/shard_map/ppermute | solution.py:431
  114.8 7.7 %collective-permute-start.14 = (bf16[2,8,64,128]{3,2,1,0:T(8,128)(2,1)S(1)}, bf16[2,8,64,128]{3,2,1,0:T(8,128)(2,1)S(1)}, u32[]{:S(2)}, u32[]{:S(2)}) collective-permute-start(bf16[2,8,64,128]{3,2,1,0:T(8,128)(2,1)S(1)} %pad_maximum_fusion.4), channel_id=1, source_target_pairs={{0,16},{16,32},{32,48},{48,0},{1,17},{17,33},{33,49},{49,1},{2,18}... | collective-permute-start | bytes 786440 | tf_op jit(solution)/shard_map/ppermute | solution.py:431
  120.2 5.6 %collective-permute-start.21 = (bf16[2,8,64,128]{3,2,1,0:T(8,128)(2,1)S(1)}, bf16[2,8,64,128]{3,2,1,0:T(8,128)(2,1)S(1)}, u32[]{:S(2)}, u32[]{:S(2)}) collective-permute-start(bf16[2,8,64,128]{3,2,1,0:T(8,128)(2,1)S(1)} %add_convert_fusion.1), channel_id=1, source_target_pairs={{0,64},{64,0},{1,65},{65,1},{2,66},{66,2},{3,67},{67,3},{4,68},{68... | collective-permute-start | bytes 786440 | tf_op jit(solution)/shard_map/ppermute | solution.py:435
  126.7 30.2 %all-to-all-start.4 = ((bf16[16,64,128]{2,1,0:T(8,128)(2,1)}), bf16[16,64,128]{2,1,0:T(8,128)(2,1)}, u32[]{:S(2)}, u32[]{:S(2)}) async-start(bf16[16,64,128]{2,1,0:T(8,128)(2,1)} %bitcast.16), calls=%async_computation.4 | async-start | bytes 524288 | tf_op jit(solution)/shard_map/all_to_all | solution.py:467
  156.9 46.2 %all-to-all-start.3 = ((bf16[64,64,384]{2,1,0:T(8,128)(2,1)}), bf16[64,64,384]{2,1,0:T(8,128)(2,1)}, u32[]{:S(2)}, u32[]{:S(2)}) async-start(bf16[64,64,384]{2,1,0:T(8,128)(2,1)} %get-tuple-element.48), calls=%async_computation.3 | async-start | bytes 6291456 | tf_op jit(solution)/shard_map/all_to_all | solution.py:467
  169.2 4.6 %collective-permute-start.12 = (bf16[256,768]{1,0:T(8,128)(2,1)}, bf16[256,768]{1,0:T(8,128)(2,1)}, u32[]{:S(2)}, u32[]{:S(2)}) collective-permute-start(bf16[256,768]{1,0:T(8,128)(2,1)} %copy-done.26), channel_id=1, source_target_pairs={{0,8},{8,0},{1,9},{9,1},{2,10},{10,2},{3,11},{11,3},{4,12},{12,4},... | collective-permute-start | bytes 1179656 | tf_op jit(solution)/shard_map/ppermute | solution.py:463
  207.7 55.6 %all-to-all-start.5 = ((bf16[64,80,384]{2,1,0:T(8,128)(2,1)}), bf16[64,80,384]{2,1,0:T(8,128)(2,1)}, u32[]{:S(2)}, u32[]{:S(2)}) async-start(bf16[64,80,384]{2,1,0:T(8,128)(2,1)} %broadcast_in_dim.11), calls=%async_computation.5 | async-start | bytes 7864320 | tf_op jit(solution)/shard_map/all_to_all | solution.py:467
  221.3 2.5 collective-permute-start.22
  263.3 17.7 %collective-permute-start.23 = (bf16[64,80,384]{2,1,0:T(8,128)(2,1)}, bf16[64,80,384]{2,1,0:T(8,128)(2,1)}, u32[]{:S(2)}, u32[]{:S(2)}) collective-permute-start(bf16[64,80,384]{2,1,0:T(8,128)(2,1)} %all-to-all-done.5.block_ref), channel_id=1, source_target_pairs={{0,8},{8,0},{1,9},{9,1},{2,10},{10,2},{3,11},{11,3},{4,12},{12,4},... | collective-permute-start | bytes 11796488 | tf_op jit(solution)/shard_map/ppermute | solution.py:463
  267.5 5.0 %collective-permute-start.24 = (f32[8,16,384]{2,1,0:T(8,128)}, f32[8,16,384]{2,1,0:T(8,128)S(1)}, u32[]{:S(2)}, u32[]{:S(2)}) collective-permute-start(f32[8,16,384]{2,1,0:T(8,128)} %shard_map.166.mine_ref), channel_id=1, source_target_pairs={{0,8},{8,0},{1,9},{9,1},{2,10},{10,2},{3,11},{11,3},{4,12},{12,4},... | collective-permute-start | bytes 589832 | tf_op jit(solution)/shard_map/ppermute | solution.py:463
  (39 other events, 170.1 us)

commit v4 on v3

v4 whole, which is shorter than its diff:
```python
import functools
import math

import jax
import jax.numpy as jnp
from jax import lax
from jax.experimental import pallas as pl
from jax.experimental.pallas import tpu as pltpu
from jax.sharding import Mesh, PartitionSpec as P

norm_epsilon = 1e-05
bf16 = jnp.bfloat16
f32 = jnp.float32
token_axes = ("x", "z_hi")
head_axes = ("z_lo", "x", "z_hi")
column_axes = ("z_lo", "y")
chip_axes = ("z_lo", "y", "x", "z_hi")
vmem_bytes = 60 * 1024 * 1024


def dot(a, b, dims):
    return lax.dot_general(a, b, (dims, ((), ())), preferred_element_type=f32)


def attend_places(refs):
    near, above, below, first, second = refs

    def find(place, part):
        dcore, dy = place // 4, place % 4
        if dy == 2:
            return (first, second)[part], (dcore, 0)
        return (near, above, None, below)[dy], (dcore, part)

    return find


def rows_of(base_ref, index, part):
    return pl.ds(pl.multiple_of(base_ref[index] * part, part), part)


def attend_kernel(factor, part, base_ref, cross_ref, chain_col_ref, chain_row_ref, rows_ref, *refs):
    bias_at, out_ref, grad_sum = attend_places(refs[:5]), refs[5], refs[6]
    bias_full, logits, exp_half, grad_half = refs[7:]
    blocks, width, lanes = rows_ref.shape
    size = width // 4
    count = blocks * lanes
    chunk = 128

    @pl.when(pl.program_id(0) == 0)
    def _():
        cross = cross_ref[0]
        for p in range(count // part):
            at = rows_of(base_ref, p, part)
            ref, lead = bias_at(p // 2, p % 2)
            moved = jnp.concatenate(
                [ref[(*lead, slice(part * t, part * (t + 1)))].astype(f32) for t in range(blocks)], axis=1
            )
            shifts = ref[(*lead, slice(part * blocks, part * blocks + 16))].astype(f32)
            shift = jnp.concatenate([shifts[t : t + 1] for t in range(blocks)], axis=1)
            differ = chain_col_ref[at, 0:1] != chain_row_ref[0:1, :]
            bias_full[at, :] = (moved + shift) + jnp.where(differ, cross, 0.0)
            grad_sum[at, :] = jnp.zeros((part, count), f32)

    def take(index):
        return jnp.concatenate(
            [rows_ref[t, index * size : (index + 1) * size, :] for t in range(blocks)], axis=1
        )

    query_t, key_t, value_t, grad_t = take(0), take(1), take(2), take(3)
    key = key_t.T
    value = value_t.T
    peak = jnp.full((1, count), -jnp.inf, f32)
    for p in range(count // chunk):
        at = pl.ds(chunk * p, chunk)
        scores = dot(key[chunk * p : chunk * (p + 1)], query_t, ((1,), (0,))) + bias_full[at, :]
        logits[at, :] = scores
        peak = jnp.maximum(peak, jnp.max(scores, axis=0, keepdims=True))
    for p in range(count // chunk):
        at = pl.ds(chunk * p, chunk)
        exp_half[at, :] = jnp.exp(logits[at, :] - peak).astype(bf16)
    value_ones = jnp.concatenate([value_t, jnp.ones((16, count), bf16)], axis=0)
    summed = dot(value_ones, exp_half[...], ((1,), (0,)))
    inverse = 1.0 / summed[size : size + 1]
    attended_t = summed[:size] * inverse
    scaled_t = (grad_t.astype(f32) * inverse).astype(bf16)
    delta = jnp.sum(scaled_t.astype(f32) * attended_t, axis=0, keepdims=True)
    key_grad = []
    value_grad = []
    for p in range(count // chunk):
        at = pl.ds(chunk * p, chunk)
        weights = dot(value[chunk * p : chunk * (p + 1)], scaled_t, ((1,), (0,)))
        terms = exp_half[at, :]
        grad = terms.astype(f32) * (weights - delta)
        half = grad.astype(bf16)
        grad_half[at, :] = half
        grad_sum[at, :] += grad
        key_grad.append(dot(half, query_t, ((1,), (1,))))
        value_grad.append(dot(terms, scaled_t, ((1,), (1,))))
    query_grad_t = dot(key_t, grad_half[...], ((1,), (0,))) * factor
    key_grad_t = jnp.concatenate(key_grad, axis=0).T
    value_grad_t = jnp.concatenate(value_grad, axis=0).T
    for index, array in enumerate((attended_t, query_grad_t, key_grad_t, value_grad_t)):
        array = array.astype(bf16)
        for t in range(blocks):
            out_ref[t, index * size : (index + 1) * size, :] = array[:, t * lanes : (t + 1) * lanes]


def pack_kernel(part, base_ref, chain_col_ref, chain_row_ref, sum_ref, *refs):
    grad_at, cross_ref = attend_places(refs[:5]), refs[5]
    count = sum_ref.shape[0]
    lanes = refs[0].shape[4]
    cross = jnp.zeros((1, count), f32)
    for p in range(count // part):
        at = rows_of(base_ref, p, part)
        block = sum_ref[at, :]
        differ = chain_col_ref[at, 0:1] != chain_row_ref[0:1, :]
        cross += jnp.sum(jnp.where(differ, block, 0.0), axis=0, keepdims=True)
        half = block.astype(bf16)
        ref, lead = grad_at(p // 2, p % 2)
        for t in range(count // lanes):
            ref[(*lead, t)] = half[:, t * lanes : (t + 1) * lanes]
    cross_ref[...] = jnp.broadcast_to(cross, cross_ref.shape)


def attend(base, rows, biases, cross, chains, factor):
    sources, width, total = rows.shape
    lanes = 128
    blocks = sources // 2
    own = total // lanes
    samples = 2 * own
    count = blocks * lanes
    chain_col = jnp.broadcast_to(chains[:, None], (count, 128))
    chain_row = jnp.broadcast_to(chains[None, :], (8, count))
    part = (biases[0].shape[2] - 16) // blocks
    once = lambda shape: pl.BlockSpec(
        shape, lambda s: (0,) * len(shape), pipeline_mode=pl.Buffered(1)
    )
    smem = pl.BlockSpec(memory_space=pltpu.SMEM)
    by_sample = pl.BlockSpec((blocks, width, lanes), lambda s: (s // own, 0, s % own))
    head_grads, grad_sum = pl.pallas_call(
        functools.partial(attend_kernel, factor, part),
        grid=(samples,),
        in_specs=[smem, smem, once(chain_col.shape), once(chain_row.shape), by_sample]
        + [once(bias.shape) for bias in biases],
        out_specs=[by_sample, once((count, count))],
        out_shape=[
            jax.ShapeDtypeStruct(rows.shape, bf16),
            jax.ShapeDtypeStruct((count, count), f32),
        ],
        scratch_shapes=[
            pltpu.VMEM((count, count), f32),
            pltpu.VMEM((count, count), f32),
            pltpu.VMEM((count, count), bf16),
            pltpu.VMEM((count, count), bf16),
        ],
        compiler_params=pltpu.CompilerParams(vmem_limit_bytes=vmem_bytes),
        cost_estimate=pl.CostEstimate(
            flops=12 * samples * count * count * 48,
            bytes_accessed=16 * 1024 * 1024,
            transcendentals=samples * count * count,
        ),
    )(base, cross, chain_col, chain_row, rows, *biases)
    whole_block = (2, 2, blocks, part, lanes)
    half_block = (2, 1, blocks, part, lanes)
    block_shapes = [whole_block] * 3 + [half_block] * 2
    vmem = pl.BlockSpec(memory_space=pltpu.VMEM)
    packed = pl.pallas_call(
        functools.partial(pack_kernel, part),
        in_specs=[smem, vmem, vmem, vmem],
        out_specs=[vmem] * 6,
        out_shape=[jax.ShapeDtypeStruct(shape, bf16) for shape in block_shapes]
        + [jax.ShapeDtypeStruct((8, count), f32)],
        compiler_params=pltpu.CompilerParams(vmem_limit_bytes=vmem_bytes),
        cost_estimate=pl.CostEstimate(
            flops=2 * count * count, bytes_accessed=8 * 1024 * 1024, transcendentals=0
        ),
    )(base, chain_col, chain_row, grad_sum)
    return head_grads, packed[:5], packed[5]


def norm_parts(wide):
    centred = wide - jnp.mean(wide, axis=1, keepdims=True)
    inv_std = lax.rsqrt(jnp.mean(centred * centred, axis=1, keepdims=True) + norm_epsilon)
    return centred * inv_std, inv_std


def before_kernel(
    factor,
    acts_ref,
    cots_ref,
    mod_ref,
    weight_ref,
    out_weight_ref,
    sent_ref,
    gate_ref,
    grad_gated_ref,
    normed_ref,
):
    rows, width = acts_ref.shape
    heads = sent_ref.shape[0]
    size = sent_ref.shape[1] // 4
    samples = mod_ref.shape[0]
    part = rows // samples
    for s in range(samples):
        at = slice(s * part, (s + 1) * part)
        whitened, _ = norm_parts(acts_ref[at, :].astype(f32))
        scale = 1.0 + mod_ref[s : s + 1, :width]
        shift = mod_ref[s : s + 1, width:]
        normed_ref[at, :] = (whitened * scale + shift).astype(bf16)
    normed = normed_ref[...]

    def project(index):
        return dot(normed, weight_ref[:, index * width : (index + 1) * width], ((1,), (0,)))

    def put(index, array):
        for h in range(heads):
            sent_ref[h, index * size : (index + 1) * size, :] = array[h * size : (h + 1) * size]

    put(0, (project(0) * factor).T.astype(bf16))
    put(1, project(1).T.astype(bf16))
    put(2, project(2).T.astype(bf16))
    gate = jax.nn.sigmoid(project(3)).T
    gate_ref[...] = gate
    grad_gated = dot(cots_ref[...], out_weight_ref[...], ((1,), (1,))).T
    grad_gated_ref[...] = grad_gated
    put(3, (grad_gated * gate).astype(bf16))


def in_vmem(kernel, shapes, operands, flops, smem=0):
    vmem = pl.BlockSpec(memory_space=pltpu.VMEM)
    scalars = [pl.BlockSpec(memory_space=pltpu.SMEM)] * smem
    size = sum(a.size * a.dtype.itemsize for a in operands)
    return pl.pallas_call(
        kernel,
        in_specs=scalars + [vmem] * (len(operands) - smem),
        out_specs=[vmem] * len(shapes),
        out_shape=[jax.ShapeDtypeStruct(shape, kind) for shape, kind in shapes],
        compiler_params=pltpu.CompilerParams(vmem_limit_bytes=vmem_bytes),
        cost_estimate=pl.CostEstimate(flops=flops, bytes_accessed=size, transcendentals=0),
    )(*operands)


def before(acts, cots, modulation, input_weight, output_matrix, heads, factor):
    rows, width = acts.shape
    shapes = [
        ((heads, 4 * width // heads, rows), bf16),
        ((width, rows), f32),
        ((width, rows), f32),
        ((rows, width), bf16),
    ]
    return in_vmem(
        functools.partial(before_kernel, factor),
        shapes,
        (acts, cots, modulation, input_weight, output_matrix),
        10 * rows * width * width,
    )


def gate_kernel(core_ref, back_ref, gate_ref, grad_gated_ref, keep_ref, send_ref):
    heads = back_ref.shape[0]
    size = back_ref.shape[1] // 4
    half = heads * size // 2

    def take(index, side):
        return jnp.concatenate(
            [
                back_ref[h, index * size : (index + 1) * size, :]
                for h in range(side * heads // 2, (side + 1) * heads // 2)
            ],
            axis=0,
        )

    def write(side, ref):
        at = slice(side * half, (side + 1) * half)
        gate = gate_ref[at, :]
        gated = gate * take(0, side).astype(f32)
        ref[0] = gated.astype(bf16)
        for index in (1, 2, 3):
            ref[index] = take(index, side)
        ref[4] = (grad_gated_ref[at, :] * gated * (1.0 - gate)).astype(bf16)

    @pl.when(core_ref[0] == 0)
    def _():
        write(0, keep_ref)
        write(1, send_ref)

    @pl.when(core_ref[0] == 1)
    def _():
        write(1, keep_ref)
        write(0, send_ref)


def rows_kernel(
    core_ref,
    keep_ref,
    send_ref,
    acts_ref,
    cots_ref,
    mod_ref,
    weight_ref,
    out_weight_ref,
    updated_ref,
    grad_ref,
    table_ref,
):
    rows, width = acts_ref.shape
    half = width // 2
    samples = mod_ref.shape[0]
    part = rows // samples
    grad_normed = None
    output = None
    for side, ref in ((core_ref[0], keep_ref), (1 - core_ref[0], send_ref)):
        for index in range(4):
            at = pl.multiple_of((2 * index + side) * half, 128)
            term = dot(ref[index + 1].T, weight_ref[:, pl.ds(at, half)], ((1,), (1,)))
            grad_normed = term if grad_normed is None else grad_normed + term
        at = pl.multiple_of(side * half, 128)
        term = dot(ref[0].T, out_weight_ref[pl.ds(at, half), :], ((1,), (0,)))
        output = term if output is None else output + term
    for s in range(samples):
        at = slice(s * part, (s + 1) * part)
        wide = acts_ref[at, :].astype(f32)
        updated_ref[at, :] = (wide + output[at]).astype(bf16)
        whitened, inv_std = norm_parts(wide)
        grad = grad_normed[at]
        products = grad * whitened
        scaled = grad * (1.0 + mod_ref[s : s + 1, :width])
        moved = scaled - jnp.mean(scaled, axis=1, keepdims=True)
        moved = moved - whitened * jnp.mean(scaled * whitened, axis=1, keepdims=True)
        grad_ref[at, :] = (cots_ref[at, :].astype(f32) + inv_std * moved).astype(bf16)
        for index, array in enumerate((products, grad)):
            total = jnp.sum(array, axis=0, keepdims=True)
            for k in range(2):
                row = 4 * s + 2 * index + k
                table_ref[row : row + 1, :] = total[:, k * half : (k + 1) * half]


def weights_kernel(keep_ref, got_ref, own_normed_ref, other_normed_ref, own_cots_ref, other_cots_ref, payload_ref):
    width = own_normed_ref.shape[1]
    half = width // 2
    depth = 48
    normed_t = jnp.concatenate([own_normed_ref[...], other_normed_ref[...]], axis=0).T
    for index in range(4):
        grad = jnp.concatenate([keep_ref[index + 1], got_ref[index + 1]], axis=1).T
        weight_grad = dot(normed_t, grad, ((1,), (0,))).astype(bf16)
        for a in range(width // depth):
            payload_ref[4 * a + index, :depth, :] = weight_grad[depth * a : depth * (a + 1)]
    gated = jnp.concatenate([keep_ref[0], got_ref[0]], axis=1)
    cots = jnp.concatenate([own_cots_ref[...], other_cots_ref[...]], axis=0)
    out_grad = dot(gated, cots, ((1,), (0,))).astype(bf16)
    for d in range(payload_ref.shape[0]):
        if d < half // 8:
            block = out_grad[16 * (d // 2) : 16 * (d // 2 + 1), half * (d % 2) : half * (d % 2 + 1)]
        else:
            block = jnp.zeros((16, half), bf16)
        payload_ref[d, depth:, :] = block


def assemble_kernel(place_ref, block_ref, *refs):
    input_ref, output_ref, stage, stage_out, sems = refs[-5:]
    half = block_ref.shape[2]
    depth = 48
    place = place_ref[0]
    copies = []
    for b in range(4):
        for group in range(2):
            for a in range(8 * group, 8 * group + 8):
                stage[b, depth * a : depth * (a + 1), :] = block_ref[4 * a + b, :depth, :].astype(f32)
            rows = slice(8 * depth * group, 8 * depth * (group + 1))
            at = pl.multiple_of((2 * b + place) * half, 128)
            copies.append(
                pltpu.make_async_copy(
                    stage.at[b, rows, :],
                    input_ref.at[rows, pl.ds(at, half)],
                    sems.at[len(copies)],
                )
            )
            copies[-1].start()
    for d in range(half // 8):
        stage_out[16 * (d // 2) : 16 * (d // 2 + 1), half * (d % 2) : half * (d % 2 + 1)] = block_ref[
            d, depth : depth + 16, :
        ].astype(f32)
    copies.append(pltpu.make_async_copy(stage_out, output_ref.at[place], sems.at[len(copies)]))
    copies[-1].start()
    for copy in copies:
        copy.wait()


def assemble(place, gathered, earlier):
    chips, depth, half = gathered.shape
    width = 2 * half
    anywhere = pl.BlockSpec(memory_space=pl.ANY)
    return pl.pallas_call(
        assemble_kernel,
        in_specs=[
            pl.BlockSpec(memory_space=pltpu.SMEM),
            pl.BlockSpec(memory_space=pltpu.VMEM),
        ]
        + [anywhere] * len(earlier),
        out_specs=[anywhere, anywhere],
        out_shape=[
            jax.ShapeDtypeStruct((width, 4 * width), f32),
            jax.ShapeDtypeStruct((2, half, width), f32),
        ],
        scratch_shapes=[
            pltpu.VMEM((4, width, half), f32),
            pltpu.VMEM((half, width), f32),
            pltpu.SemaphoreType.DMA((9,)),
        ],
        input_output_aliases={2 + k: k for k in range(len(earlier))},
        compiler_params=pltpu.CompilerParams(vmem_limit_bytes=vmem_bytes),
        cost_estimate=pl.CostEstimate(
            flops=0, bytes_accessed=10 * 1024 * 1024, transcendentals=0
        ),
    )(place, gathered, *earlier)


def gather_small_kernel(block_ref, out_ref):
    zy, rows, half = out_ref.shape
    blocks = block_ref.shape[0] // zy
    for p in range(zy):
        total = block_ref[blocks * p].astype(f32)
        for t in range(1, blocks):
            total = total + block_ref[blocks * p + t].astype(f32)
        out_ref[p] = total


def gather_small(gathered, zy, small_depth):
    chips, depth, half = gathered.shape
    return pl.pallas_call(
        gather_small_kernel,
        grid=(1,),
        in_specs=[
            pl.BlockSpec((chips, small_depth, half), lambda i: (0, depth // small_depth - 1, 0))
        ],
        out_specs=pl.BlockSpec((zy, small_depth, half), lambda i: (0, 0, 0)),
        out_shape=jax.ShapeDtypeStruct((zy, small_depth, half), f32),
        cost_estimate=pl.CostEstimate(flops=0, bytes_accessed=1 << 20, transcendentals=0),
    )(gathered)


def finish_small_kernel(tokens, mine_ref, other_ref, table_ref, sums_ref):
    zy, rows, half = mine_ref.shape
    levels = table_ref.shape[0]
    refs = (mine_ref, other_ref)
    values = jnp.concatenate([ref[...].reshape(zy * rows, half) for ref in refs], axis=0)
    high = values.astype(bf16)
    low = (values - high.astype(f32)).astype(bf16)
    row = lax.broadcasted_iota(jnp.int32, (rows, 1), 0)
    at = lax.broadcasted_iota(jnp.int32, (rows, levels), 1).astype(f32)
    same = []
    for ref in refs:
        for p in range(zy):
            first = ref[p, 13:14, 160:161] * (1.0 / tokens)
            second = ref[p, 13:14, 161:162] * (1.0 / tokens)
            same.append(jnp.where(row < 4, first, second) == at)
    for r in range(4):
        kept = (row < 8) & (row % 4 == r)
        hot = jnp.concatenate([jnp.where(s & kept, 1.0, 0.0) for s in same], axis=0).astype(bf16)
        table_ref[:, r * half : (r + 1) * half] = dot(hot, high, ((0,), (0,))) + dot(
            hot, low, ((0,), (0,))
        )
    sums_ref[0] = jnp.sum(mine_ref[...], axis=0)
    sums_ref[1] = jnp.sum(other_ref[...], axis=0)


def finish_small(mine, other, levels, tokens):
    zy, rows, half = mine.shape
    return pl.pallas_call(
        functools.partial(finish_small_kernel, tokens),
        out_shape=[
            jax.ShapeDtypeStruct((levels, 4 * half), f32),
            jax.ShapeDtypeStruct((2, rows, half), f32),
        ],
        cost_estimate=pl.CostEstimate(flops=0, bytes_accessed=2 << 20, transcendentals=0),
    )(mine, other)


def ring(array, shift):
    return lax.ppermute(array, "y", [(i, (i + shift) % 4) for i in range(4)])


def spread_bias(near):
    above = ring(near, 3)
    below = ring(near, 1)
    return [near, above, below, ring(below[:, :1], 1), ring(above[:, 1:], 3)]


def sum_bias(near, above, below, first, second):
    add = lambda *arrays: sum(a.astype(f32) for a in arrays)
    from_below = ring(first, 1)
    from_above = ring(second, 3)
    above = jnp.concatenate([add(above[:, :1], from_below).astype(bf16), above[:, 1:]], axis=1)
    below = jnp.concatenate([below[:, :1], add(below[:, 1:], from_above).astype(bf16)], axis=1)
    total = add(near, ring(above, 1), ring(below, 3))
    return total[0] + swap(total[1].astype(bf16)).astype(f32)


def swap(array):
    return lax.ppermute(array, "core", [(0, 1), (1, 0)])


def exchange(array, axes):
    return lax.all_to_all(array, axes, 0, 0, tiled=True)


def spread(array, axes, count):
    return exchange(jnp.broadcast_to(array[None], (count,) + array.shape), axes)


def shards(
    activations,
    levels,
    ada_table,
    input_weight,
    output_matrix,
    pair_feats,
    pair_weight,
    cross_bias,
    chains,
    cotangent,
):
    own_samples, row_count, width = activations.shape
    heads = pair_weight.shape[1]
    size = width // heads
    col_count = pair_feats.shape[1]
    level_count = ada_table.shape[0]
    factor = 1.0 / math.sqrt(size)
    core = lax.axis_index("core")
    blocks = lax.axis_size("x") * lax.axis_size("z_hi")
    zy_count = lax.axis_size("z_lo") * lax.axis_size("y")
    chip_count = blocks * zy_count
    half = width // 2

    pair_part = jnp.einsum("ijc,ch->hji", pair_feats, pair_weight, preferred_element_type=f32)
    shift = jnp.max(pair_part, axis=1, keepdims=True).astype(bf16)
    moved = (pair_part - shift.astype(f32)).astype(bf16)
    bias_sent = jnp.concatenate(
        [moved, jnp.broadcast_to(shift, (heads, 16, row_count))], axis=1
    )
    bias_got = exchange(bias_sent, head_axes)

    core_at = jnp.reshape(core, (1,)).astype(jnp.int32)
    acts = activations.reshape(-1, width)
    cots = cotangent.reshape(-1, width)
    onehot = (
        levels[:, None] == lax.broadcasted_iota(jnp.int32, (own_samples, level_count), 1)
    ).astype(bf16)
    modulation = jnp.dot(onehot, ada_table, preferred_element_type=f32)
    sent, gate_open, grad_gated, normed = before(
        acts, cots, modulation, input_weight, output_matrix, heads, factor
    )
    sent, bias_got = lax.optimization_barrier((sent, bias_got))
    bias_own = jnp.concatenate(
        [
            bias_got[:, :col_count].reshape(2, blocks * col_count, row_count),
            bias_got[:, col_count].reshape(2, blocks, row_count),
            bias_got[:, col_count].reshape(2, blocks, row_count),
        ],
        axis=1,
    )
    near = jnp.stack([bias_own, swap(bias_own)])
    sent, near = lax.optimization_barrier((sent, near))
    biases = spread_bias(near)
    head_rows = exchange(sent, head_axes)
    y_at = lax.axis_index("y")
    base = jnp.stack(
        [
            ((p % 2) * 4 + (y_at + p // 2) % 4) * 2 + (core + p // 8) % 2
            for p in range(16)
        ]
    ).astype(jnp.int32)
    head = lax.axis_index(head_axes)
    own_cross = lax.dynamic_slice_in_dim(cross_bias, head, 1)
    other_normed = swap(normed)
    other_cots = swap(cots)
    head_grads, grad_biases, cross_sum = attend(
        base, head_rows, biases, own_cross, chains, factor
    )

    back = exchange(head_grads, head_axes)
    half_shape = ((5, half, acts.shape[0]), bf16)
    keep, send = in_vmem(
        gate_kernel, [half_shape] * 2, (core_at, back, gate_open, grad_gated), 0, 1
    )
    got = swap(send)
    updated, grad_tokens, table_rows = in_vmem(
        rows_kernel,
        [(acts.shape, bf16), (acts.shape, bf16), ((8, half), f32)],
        (core_at, keep, send, acts, cots, modulation, input_weight, output_matrix),
        10 * acts.size * width,
        1,
    )
    updated = updated.reshape(activations.shape)
    grad_tokens = grad_tokens.reshape(activations.shape)
    (payload,) = in_vmem(
        weights_kernel,
        [((chip_count, 64, half), bf16)],
        (keep, got, normed, other_normed, cots, other_cots),
        10 * acts.size * width,
    )

    bias_sum = sum_bias(*grad_biases).astype(bf16)
    grad_bias_half = exchange(bias_sum.reshape(heads, col_count, row_count), head_axes)
    grad_pair = jnp.einsum(
        "hji,ch->ijc", grad_bias_half, pair_weight, preferred_element_type=f32
    ).astype(bf16)
    grad_pair_part = jnp.einsum(
        "ijc,hji->ch", pair_feats, grad_bias_half, preferred_element_type=f32
    )

    parts = exchange(payload, chip_axes)
    summed = jnp.sum(parts.astype(f32), axis=0).astype(bf16)
    pair_size = pair_weight.shape[0] * heads
    cross_part = jnp.sum(cross_sum[0])
    cross_high = cross_part.astype(bf16).astype(f32)
    at_head = (jnp.arange(heads) == head).astype(f32)
    last = jnp.concatenate(
        [at_head * cross_high, at_head * (cross_part - cross_high), levels.astype(f32)]
    )
    flat = jnp.concatenate([table_rows.reshape(-1), grad_pair_part.reshape(-1), last])
    small_depth = 16
    small = jnp.pad(flat, (0, small_depth * half - flat.size)).reshape(small_depth, half)
    block = jnp.concatenate([summed, small.astype(bf16)], axis=0)
    gathered = spread(block, chip_axes, chip_count)
    pair_shape = grad_pair.shape
    gathered, updated, grad_tokens, grad_pair = lax.optimization_barrier(
        (gathered, updated, grad_tokens, grad_pair.reshape(-1, pair_shape[2]))
    )
    grad_pair = grad_pair.reshape(pair_shape)
    mine_small = gather_small(gathered, zy_count, small_depth)
    other = swap(gathered)
    other_small = swap(mine_small)
    earlier = assemble(core_at, gathered, ())
    input_weight_grad, output_weight_grad = assemble(1 - core_at, other, earlier)
    output_weight_grad = output_weight_grad.reshape(width, width)
    grad_table, sums = finish_small(mine_small, other_small, level_count, blocks)
    pair_rows = (sums[0] + sums[1])[8:].reshape(-1)
    grad_pair_weight = pair_rows[:pair_size].reshape(pair_weight.shape)
    crosses = sums[0, 13] + sums[1, 13]
    grad_cross = crosses[128:144] + crosses[144:160]
    return (
        updated,
        grad_tokens,
        grad_pair,
        input_weight_grad,
        output_weight_grad,
        grad_pair_weight,
        grad_cross,
        grad_table,
    )


def solution(mesh):
    fine = Mesh(mesh.devices.reshape(2, 4, 2, 4, 2), ("z_lo", "y", "core", "x", "z_hi"))
    sample = ("z_lo", "y", "core")
    token = ("x", "z_hi")
    placed = (
        P(sample, token, None),
        P(sample),
        P(),
        P(),
        P(),
        P(token, sample, None),
        P(),
        P(),
        P(),
        P(sample, token, None),
    )
    return jax.shard_map(
        shards,
        mesh=fine,
        in_specs=placed,
        out_specs=(
            P(sample, token, None),
            P(sample, token, None),
            P(token, sample, None),
            P(),
            P(),
            P(),
            P(),
            P(),
        ),
        check_vma=False,
    )
```

time: 290 us -> 264 us (0.910)
  local copies, waits for them, and re-layouts: 37 us -> 14.3 us
  starting transfers between devices: 81.1 us -> 60.1 us
  waiting for transfers between devices: 91.5 us -> 107 us
  Pallas kernels: 51.9 us -> 64 us
  other arithmetic: 15.4 us -> 10.1 us
    unnamed x82 -> x37, local copies, waits for them, and re-layouts: 20.8 us -> 3.83 us
    pallas_call x3 -> x6, Pallas kernels: 35.5 us -> 49.5 us  [the longest x1 22.8 us: attend(): pl.pallas_call(functools.partial(attend_kernel, factor, part), grid=(samp...]
    all_to_all x6, starting transfers between devices: 51 us -> 37.6 us  [exchange(): return lax.all_to_all(array, axes, 0, 0, tiled=True)]
    all_to_all x6, waiting for transfers between devices: 73.5 us -> 86 us  [exchange(): return lax.all_to_all(array, axes, 0, 0, tiled=True)]
    ppermute x16 -> x8, starting transfers between devices: 22.5 us -> 11.4 us  [ring(): return lax.ppermute(array, 'y', [(i, (i + shift) % 4) for i in range(4)])]
    slice x12 -> x4, local copies, waits for them, and re-layouts: 5.56 us -> 0.08 us  [the longest x2 0.04 us: spread_bias(): return [near, above, below, ring(below[:, :1], 1), ring(above[:, 1:], 3)]]
    ppermute x7, starting transfers between devices: 6.07 us -> 11 us  [swap(): return lax.ppermute(array, 'core', [(0, 1), (1, 0)])]
    reduce_sum x5 -> x0, other arithmetic: 4.95 us -> none  [the longest x1 1.38 us: shards(): grad_scale = jnp.sum(grad_normed * whitened, axis=1)]
  transfers between devices with their start and end apart: 31 -> 21, of which waited for: 14 -> 12; matrix products, arithmetic and copies ran while one was open for 12% -> 6% of each run, Pallas kernels for 9% -> 12%
where the time goes in v4:
time: 264 us; the launch traced here: 262 us
  waiting for transfers between devices  107 us (41%)
  Pallas kernels  64 us (24%)
  starting transfers between devices  60.1 us (23%)
  local copies, waits for them, and re-layouts  14.3 us (5%)
  other arithmetic  10.1 us (4%)
  matrix products  3.94 us (1%)
    all_to_all x6, waiting for transfers between devices, exchange(): return lax.all_to_all(array, axes, 0, 0, tiled=True)  86 us
    all_to_all x6, starting transfers between devices, exchange(): return lax.all_to_all(array, axes, 0, 0, tiled=True)  37.6 us
    pallas_call x1, Pallas kernels, attend(): pl.pallas_call(functools.partial(attend_kernel, factor, part), grid=(samp...  22.8 us
    pallas_call x4, Pallas kernels, in_vmem(): pl.pallas_call(kernel, in_specs=scalars + [vmem] * (len(operands) - smem)...  22.5 us
    ppermute x8, waiting for transfers between devices, ring(): return lax.ppermute(array, 'y', [(i, (i + shift) % 4) for i in range(4)])  19.1 us
    ppermute x8, starting transfers between devices, ring(): return lax.ppermute(array, 'y', [(i, (i + shift) % 4) for i in range(4)])  11.4 us
    ppermute x7, starting transfers between devices, swap(): return lax.ppermute(array, 'core', [(0, 1), (1, 0)])  11 us
    pallas_call x2, Pallas kernels, assemble(): pl.pallas_call(assemble_kernel, in_specs=[pl.BlockSpec(memory_space=pltpu...  9.74 us
  transfers between devices with their start and end apart: 21, of which 12 were waited for; matrix products, arithmetic and copies ran while one was open for 6% of the time, Pallas kernels for 12%

profile of v4, /device:TPU:1, one launch (start us, length us, event | category | flops | bytes accessed | tf_op | source)
XLA Modules:
  0.0 262.4 jit_solution(8234021782972225862)
XLA Ops:
  2.2 1.9 fusion.22
  5.1 8.4 %all-to-all-start = ((bf16[16,80,128]{2,1,0:T(8,128)(2,1)}), bf16[16,80,128]{2,1,0:T(8,128)(2,1)S(1)}, u32[]{:S(2)}, u32[]{:S(2)}) async-start(bf16[16,80,128]{2,1,0:T(8,128)(2,1)} %copy.41), calls=%async_computation | async-start | bytes 655360 | tf_op jit(solution)/shard_map/all_to_all | solution.py:504
  14.4 6.6 %shard_map.161 = (bf16[16,192,256]{2,1,0:T(8,128)(2,1)}, f32[768,256]{1,0:T(8,128)}, f32[768,256]{1,0:T(8,128)}, bf16[256,768]{1,0:T(8,128)(2,1)}) custom-call(bf16[256,768]{1,0:T(8,128)(2,1)} %bitcast.68, bf16[256,768]{1,0:T(8,128)(2,1)} %bitcast.63, f32[2,1536]{1,0:T(2,128)} %fusion.13.mod_ref, bf16[768,3072]{1,0:T(8,128)(2,1)} %weight_ref.3, ...), custom_call_target="tpu_custom_call" | custom-call | flops 1509949440 | bytes 6696960 | tf_op jit(solution)/shard_map/pallas_call | solution.py:233
  21.8 2.4 collective-permute-start
  25.5 5.2 %all-to-all-start.1 = ((bf16[16,192,256]{2,1,0:T(8,128)(2,1)}), bf16[16,192,256]{2,1,0:T(8,128)(2,1)}, u32[]{:S(2)}, u32[]{:S(2)}) async-start(bf16[16,192,256]{2,1,0:T(8,128)(2,1)} %get-tuple-element.42), calls=%async_computation.1 | async-start | bytes 3145728 | tf_op jit(solution)/shard_map/all_to_all | solution.py:504
  33.5 11.8 %collective-permute-done.2.refs_2_ = bf16[2,2,528,128]{3,2,1,0:T(8,128)(2,1)S(1)} collective-permute-done((bf16[2,2,528,128]{3,2,1,0:T(8,128)(2,1)S(1)}, bf16[2,2,528,128]{3,2,1,0:T(8,128)(2,1)S(1)}, u32[]{:S(2)}, u32[]{:S(2)}) %collective-permute-start.2) | collective-permute-done | bytes 540704 | tf_op jit(solution)/shard_map/ppermute | solution.py:480
  45.5 2.9 %collective-permute-start.4 = (bf16[2,1,528,128]{3,2,1,0:T(8,128)(2,1)S(1)}, bf16[2,1,528,128]{3,2,1,0:T(8,128)(2,1)}, u32[]{:S(2)}, u32[]{:S(2)}) collective-permute-start(bf16[2,1,528,128]{3,2,1,0:T(8,128)(2,1)S(1)} %slice.87), channel_id=1, source_target_pairs={{0,48},{16,0},{32,16},{48,32},{1,49},{17,1},{33,17},{49,33},{2,50}... | collective-permute-start | bytes 811016 | tf_op jit(solution)/shard_map/ppermute | solution.py:480
  49.7 3.7 %collective-permute-done.3.refs_3_ = bf16[2,1,528,128]{3,2,1,0:T(8,128)(2,1)S(1)} collective-permute-done((bf16[2,1,528,128]{3,2,1,0:T(8,128)(2,1)S(1)}, bf16[2,1,528,128]{3,2,1,0:T(8,128)(2,1)S(1)}, u32[]{:S(2)}, u32[]{:S(2)}) %collective-permute-start.3) | collective-permute-done | bytes 270368 | tf_op jit(solution)/shard_map/ppermute | solution.py:480
  56.8 22.8 %shard_map.162 = (bf16[16,192,256]{2,1,0:T(8,128)(2,1)}, f32[1024,1024]{1,0:T(8,128)}) custom-call(s32[16]{0:T(128)} %stack.76.base_ref, f32[1]{0:T(128)} %dynamic_slice.3.cross_ref, s32[1024,128]{1,0:T(8,128)} %broadcast_in_dim.8.chain_col_ref, s32[8,1024]{1,0:T(8,128)} %broadcast_in_dim.9.chain_row_ref, bf16[16,192,256]{2,1,0:T(8,128)(2,1)} %all-to-all-done.1.rows_ref, ...), custom_call_target="tpu_custom_call" | custom-call | flops 2415919104 | bytes 16777216 | tf_op jit(solution)/shard_map/pallas_call | solution.py:140
  79.6 4.1 %shard_map.166 = (bf16[2,2,8,64,128]{4,3,2,1,0:T(8,128)(2,1)}, bf16[2,2,8,64,128]{4,3,2,1,0:T(8,128)(2,1)}, bf16[2,2,8,64,128]{4,3,2,1,0:T(8,128)(2,1)}, bf16[2,...) custom-call(s32[16]{0:T(128)} %stack.76.base_ref, ...), custom_call_target="tpu_custom_call" | custom-call | flops 2097152 | bytes 8388608 | tf_op jit(solution)/shard_map/pallas_call | solution.py:167
  83.7 2.8 %collective-permute-start.10 = (bf16[2,1,8,64,128]{4,3,2,1,0:T(8,128)(2,1)}, bf16[2,1,8,64,128]{4,3,2,1,0:T(8,128)(2,1)S(1)}, u32[]{:S(2)}, u32[]{:S(2)}) collective-permute-start(bf16[2,1,8,64,128]{4,3,2,1,0:T(8,128)(2,1)} %get-tuple-element.56), channel_id=1, source_target_pairs={{0,48},{16,0},{32,16},{48,32},{1,49},{17,1},{33,17},{49,33},{2,50}... | collective-permute-start | bytes 786440 | tf_op jit(solution)/shard_map/ppermute | solution.py:480
  86.5 5.4 %all-to-all-start.2 = ((bf16[16,192,256]{2,1,0:T(8,128)(2,1)}), bf16[16,192,256]{2,1,0:T(8,128)(2,1)}, u32[]{:S(2)}, u32[]{:S(2)}) async-start(bf16[16,192,256]{2,1,0:T(8,128)(2,1)} %get-tuple-element.44), calls=%async_computation.2 | async-start | bytes 3145728 | tf_op jit(solution)/shard_map/all_to_all | solution.py:504
  93.0 2.7 %collective-permute-start.11 = (bf16[2,2,8,64,128]{4,3,2,1,0:T(8,128)(2,1)}, bf16[2,2,8,64,128]{4,3,2,1,0:T(8,128)(2,1)}, u32[]{:S(2)}, u32[]{:S(2)}) collective-permute-start(bf16[2,2,8,64,128]{4,3,2,1,0:T(8,128)(2,1)} %pad_maximum_fusion.2), channel_id=1, source_target_pairs={{0,48},{16,0},{32,16},{48,32},{1,49},{17,1},{33,17},{49,33},{2,50}... | collective-permute-start | bytes 1572872 | tf_op jit(solution)/shard_map/ppermute | solution.py:480
  95.7 3.6 %collective-permute-done.8 = bf16[2,1,8,64,128]{4,3,2,1,0:T(8,128)(2,1)S(1)} collective-permute-done((bf16[2,1,8,64,128]{4,3,2,1,0:T(8,128)(2,1)}, bf16[2,1,8,64,128]{4,3,2,1,0:T(8,128)(2,1)S(1)}, u32[]{:S(2)}, u32[]{:S(2)}) %collective-permute-start.8) | collective-permute-done | bytes 262176 | tf_op jit(solution)/shard_map/ppermute | solution.py:480
  100.3 13.1 %all-to-all-done.2.back_ref = bf16[16,192,256]{2,1,0:T(8,128)(2,1)} async-done(((bf16[16,192,256]{2,1,0:T(8,128)(2,1)}), bf16[16,192,256]{2,1,0:T(8,128)(2,1)}, u32[]{:S(2)}, u32[]{:S(2)}) %all-to-all-start.2) | async-done | bytes 1572896 | tf_op jit(solution)/shard_map/all_to_all | solution.py:504
  113.4 3.4 %shard_map.163 = (bf16[5,384,256]{2,1,0:T(8,128)(2,1)}, bf16[5,384,256]{2,1,0:T(8,128)(2,1)}) custom-call(s32[1]{0:T(128)} %bitcast.core_ref.place_ref, bf16[16,192,256]{2,1,0:T(8,128)(2,1)} %all-to-all-done.2.back_ref, f32[768,256]{1,0:T(8,128)} %get-tuple-element.45.gate_ref, f32[768,256]{1,0:T(8,128)} %get-tuple-element.46.grad_gated_ref), custom_call_target="tpu_custom_call" | custom-call | bytes 3145732 | tf_op jit(solution)/shard_map/pallas_call | solution.py:233
  116.8 4.4 %collective-permute-start.5 = (bf16[5,384,256]{2,1,0:T(8,128)(2,1)}, bf16[5,384,256]{2,1,0:T(8,128)(2,1)}, u32[]{:S(2)}, u32[]{:S(2)}) collective-permute-start(bf16[5,384,256]{2,1,0:T(8,128)(2,1)} %get-tuple-element.48.send_ref), channel_id=1, source_target_pairs={{0,8},{8,0},{1,9},{9,1},{2,10},{10,2},{3,11},{11,3},{4,12},{12,4},... | collective-permute-start | bytes 2949128 | tf_op jit(solution)/shard_map/ppermute | solution.py:500
  125.1 3.9 %all-to-all-start.4 = ((bf16[16,64,128]{2,1,0:T(8,128)(2,1)}), bf16[16,64,128]{2,1,0:T(8,128)(2,1)S(1)}, u32[]{:S(2)}, u32[]{:S(2)}) async-start(bf16[16,64,128]{2,1,0:T(8,128)(2,1)} %bitcast.27), calls=%async_computation.4 | async-start | bytes 524288 | tf_op jit(solution)/shard_map/all_to_all | solution.py:504
  130.0 5.8 %shard_map.164 = bf16[64,64,384]{2,1,0:T(8,128)(2,1)} custom-call(bf16[5,384,256]{2,1,0:T(8,128)(2,1)} %get-tuple-element.47.keep_ref, bf16[5,384,256]{2,1,0:T(8,128)(2,1)} %collective-permute-done.5.got_ref, bf16[256,768]{1,0:T(8,128)(2,1)} %get-tuple-element.49.own_normed_ref, bf16[256,768]{1,0:T(8,128)(2,1)} %copy-done.9, bf16[256,768]{1,0:T(8,128)(2,1)} %bitcast.64, ...), custom_call_target="tpu_custom_call" | custom-call | flops 1509949440 | bytes 3538944 | tf_op jit(solution)/shard_map/pallas_call | solution.py:233
  137.1 6.6 %all-to-all-start.3 = ((bf16[64,64,384]{2,1,0:T(8,128)(2,1)}), bf16[64,64,384]{2,1,0:T(8,128)(2,1)}, u32[]{:S(2)}, u32[]{:S(2)}) async-start(bf16[64,64,384]{2,1,0:T(8,128)(2,1)} %shard_map.164), calls=%async_computation.3 | async-start | bytes 6291456 | tf_op jit(solution)/shard_map/all_to_all | solution.py:504
  147.5 6.8 %shard_map.165 = (bf16[256,768]{1,0:T(8,128)(2,1)}, bf16[256,768]{1,0:T(8,128)(2,1)}, f32[8,384]{1,0:T(8,128)}) custom-call(s32[1]{0:T(128)} %bitcast.core_ref.place_ref, bf16[5,384,256]{2,1,0:T(8,128)(2,1)} %get-tuple-element.47.keep_ref, bf16[5,384,256]{2,1,0:T(8,128)(2,1)} %get-tuple-element.48.send_ref, bf16[256,768]{1,0:T(8,128)(2,1)} %bitcast.69, ...), custom_call_target="tpu_custom_call" | custom-call | flops 1509949440 | bytes 8663044 | tf_op jit(solution)/shard_map/pallas_call | solution.py:233
  155.2 26.5 %all-to-all-done.3 = bf16[64,64,384]{2,1,0:T(8,128)(2,1)} async-done(((bf16[64,64,384]{2,1,0:T(8,128)(2,1)}), bf16[64,64,384]{2,1,0:T(8,128)(2,1)}, u32[]{:S(2)}, u32[]{:S(2)}) %all-to-all-start.3) | async-done | bytes 3145760 | tf_op jit(solution)/shard_map/all_to_all | solution.py:504
  181.7 2.3 reduce_sum.21
  184.0 2.3 broadcast_in_dim.11
  186.3 8.1 %all-to-all-start.5 = ((bf16[64,80,384]{2,1,0:T(8,128)(2,1)}), bf16[64,80,384]{2,1,0:T(8,128)(2,1)}, u32[]{:S(2)}, u32[]{:S(2)}) async-start(bf16[64,80,384]{2,1,0:T(8,128)(2,1)} %broadcast_in_dim.11), calls=%async_computation.5 | async-start | bytes 7864320 | tf_op jit(solution)/shard_map/all_to_all | solution.py:504
  195.2 2.7 %copy.46 = bf16[128,64,128]{2,1,0:T(8,128)(2,1)} copy(bf16[128,64,128]{2,0,1:T(8,128)(2,1)S(1)} %convert_bitcast_fusion) | data formatting | bytes 4194304 | tf_op jit(solution)/shard_map/convert_element_type | solution.py:607
  197.8 42.7 %all-to-all-done.5.block_ref = bf16[64,80,384]{2,1,0:T(8,128)(2,1)} async-done(((bf16[64,80,384]{2,1,0:T(8,128)(2,1)}), bf16[64,80,384]{2,1,0:T(8,128)(2,1)}, u32[]{:S(2)}, u32[]{:S(2)}) %all-to-all-start.5) | async-done | bytes 3932192 | tf_op jit(solution)/shard_map/all_to_all | solution.py:504
  240.5 3.5 %collective-permute-start.13 = (bf16[64,80,384]{2,1,0:T(8,128)(2,1)}, bf16[64,80,384]{2,1,0:T(8,128)(2,1)}, u32[]{:S(2)}, u32[]{:S(2)}) collective-permute-start(bf16[64,80,384]{2,1,0:T(8,128)(2,1)} %all-to-all-done.5.block_ref), channel_id=1, source_target_pairs={{0,8},{8,0},{1,9},{9,1},{2,10},{10,2},{3,11},{11,3},{4,12},{12,4},... | collective-permute-start | bytes 11796488 | tf_op jit(solution)/shard_map/ppermute | solution.py:500
  244.0 1.9 shard_map.169.mine_ref
  245.9 4.8 %shard_map.167 = (f32[768,3072]{1,0:T(8,128)}, f32[2,384,768]{2,1,0:T(8,128)}) custom-call(s32[1]{0:T(128)} %bitcast.core_ref.place_ref, bf16[64,80,384]{2,1,0:T(8,128)(2,1)} %all-to-all-done.5.block_ref), custom_call_target="tpu_custom_call" | custom-call | bytes 10485760 | tf_op jit(solution)/shard_map/pallas_call | solution.py:393
  251.6 2.9 %shard_map.170 = (f32[200,1536]{1,0:T(8,128)}, f32[2,16,384]{2,1,0:T(8,128)}) custom-call(f32[8,16,384]{2,1,0:T(8,128)} %shard_map.169.mine_ref, f32[8,16,384]{2,1,0:T(8,128)} %copy-done.10), custom_call_target="tpu_custom_call" | custom-call | bytes 2097152 | tf_op jit(solution)/shard_map/pallas_call | solution.py:469
  257.3 4.9 %shard_map.168 = (f32[768,3072]{1,0:T(8,128)}, f32[2,384,768]{2,1,0:T(8,128)}) custom-call(s32[1]{0:T(128)S(6)} %sub.17.place_ref, bf16[64,80,384]{2,1,0:T(8,128)(2,1)} %collective-permute-done.13.block_ref, f32[768,3072]{1,0:T(8,128)} %get-tuple-element.64.refs_0_, ...), custom_call_target="tpu_custom_call", output_to_operand_aliasing={{0}: (2, {}), {1}: (3, {})} | custom-call | bytes 10485760 | tf_op jit(solution)/shard_map/pallas_call | solution.py:393
  (107 shorter events, 28.9 us)
Async XLA Ops:
  0.7 12.9 %copy-start.15 = (s32[2]{0:T(128)S(1)}, s32[2]{0:T(128)}, u32[]{:S(2)}) copy-start(s32[2]{0:T(128)} %param.11) | copy-start | bytes 28
  0.7 12.9 %copy-start.3 = (bf16[200,1536]{1,0:T(8,128)(2,1)S(1)}, bf16[200,1536]{1,0:T(8,128)(2,1)}, u32[]{:S(2)}) copy-start(bf16[200,1536]{1,0:T(8,128)(2,1)} %param.12) | copy-start | bytes 1843204
  5.1 16.5 %all-to-all-start = ((bf16[16,80,128]{2,1,0:T(8,128)(2,1)}), bf16[16,80,128]{2,1,0:T(8,128)(2,1)S(1)}, u32[]{:S(2)}, u32[]{:S(2)}) async-start(bf16[16,80,128]{2,1,0:T(8,128)(2,1)} %copy.41), calls=%async_computation | async-start | bytes 655360 | tf_op jit(solution)/shard_map/all_to_all | solution.py:504
  21.8 3.6 %collective-permute-start = (bf16[2,528,128]{2,1,0:T(8,128)(2,1)S(1)}, bf16[2,528,128]{2,1,0:T(8,128)(2,1)S(1)}, u32[]{:S(2)}, u32[]{:S(2)}) collective-permute-start(bf16[2,528,128]{2,1,0:T(8,128)(2,1)S(1)} %get-tuple-element.95), channel_id=1, source_target_pairs={{0,8},{8,0},{1,9},{9,1},{2,10},{10,2},{3,11},{11,3},{4,12},{12,4},... | collective-permute-start | bytes 811016 | tf_op jit(solution)/shard_map/ppermute | solution.py:500
  25.4 20.0 %copy-start.4 = (bf16[2,2,528,128]{3,2,1,0:T(8,128)(2,1)}, bf16[2,2,528,128]{3,2,1,0:T(8,128)(2,1)S(1)}, u32[]{:S(2)}) copy-start(bf16[2,2,528,128]{3,2,1,0:T(8,128)(2,1)S(1)} %pad_maximum_fusion.refs_0_) | copy-start | bytes 1622020
  25.4 22.9 %copy-start.17 = (f32[16]{0:T(128)S(1)}, f32[16]{0:T(128)}, u32[]{:S(2)}) copy-start(f32[16]{0:T(128)} %param.17) | copy-start | bytes 196
  25.5 29.7 %copy-start.14 = (s32[1024]{0:T(1024)S(1)}, s32[1024]{0:T(1024)}, u32[]{:S(2)}) copy-start(s32[1024]{0:T(1024)} %param.18) | copy-start | bytes 12292
  25.5 29.7 %all-to-all-start.1 = ((bf16[16,192,256]{2,1,0:T(8,128)(2,1)}), bf16[16,192,256]{2,1,0:T(8,128)(2,1)}, u32[]{:S(2)}, u32[]{:S(2)}) async-start(bf16[16,192,256]{2,1,0:T(8,128)(2,1)} %get-tuple-element.42), calls=%async_computation.1 | async-start | bytes 3145728 | tf_op jit(solution)/shard_map/all_to_all | solution.py:504
  30.6 14.7 %collective-permute-start.2 = (bf16[2,2,528,128]{3,2,1,0:T(8,128)(2,1)S(1)}, bf16[2,2,528,128]{3,2,1,0:T(8,128)(2,1)S(1)}, u32[]{:S(2)}, u32[]{:S(2)}) collective-permute-start(bf16[2,2,528,128]{3,2,1,0:T(8,128)(2,1)S(1)} %pad_maximum_fusion.refs_0_), channel_id=1, source_target_pairs={{0,16},{16,32},{32,48},{48,0},{1,17},{17,33},{33,49},{49,1},{2,18}... | collective-permute-start | bytes 1622024 | tf_op jit(solution)/shard_map/ppermute | solution.py:480
  32.0 13.4 %collective-permute-start.1 = (bf16[2,2,528,128]{3,2,1,0:T(8,128)(2,1)S(1)}, bf16[2,2,528,128]{3,2,1,0:T(8,128)(2,1)S(1)}, u32[]{:S(2)}, u32[]{:S(2)}) collective-permute-start(bf16[2,2,528,128]{3,2,1,0:T(8,128)(2,1)S(1)} %pad_maximum_fusion.refs_0_), channel_id=1, source_target_pairs={{0,48},{16,0},{32,16},{48,32},{1,49},{17,1},{33,17},{49,33},{2,50}... | collective-permute-start | bytes 1622024 | tf_op jit(solution)/shard_map/ppermute | solution.py:480
  45.4 8.0 %collective-permute-start.3 = (bf16[2,1,528,128]{3,2,1,0:T(8,128)(2,1)S(1)}, bf16[2,1,528,128]{3,2,1,0:T(8,128)(2,1)S(1)}, u32[]{:S(2)}, u32[]{:S(2)}) collective-permute-start(bf16[2,1,528,128]{3,2,1,0:T(8,128)(2,1)S(1)} %slice.86), channel_id=1, source_target_pairs={{0,16},{16,32},{32,48},{48,0},{1,17},{17,33},{33,49},{49,1},{2,18}... | collective-permute-start | bytes 811016 | tf_op jit(solution)/shard_map/ppermute | solution.py:480
  45.5 7.9 %collective-permute-start.4 = (bf16[2,1,528,128]{3,2,1,0:T(8,128)(2,1)S(1)}, bf16[2,1,528,128]{3,2,1,0:T(8,128)(2,1)}, u32[]{:S(2)}, u32[]{:S(2)}) collective-permute-start(bf16[2,1,528,128]{3,2,1,0:T(8,128)(2,1)S(1)} %slice.87), channel_id=1, source_target_pairs={{0,48},{16,0},{32,16},{48,32},{1,49},{17,1},{33,17},{49,33},{2,50}... | collective-permute-start | bytes 811016 | tf_op jit(solution)/shard_map/ppermute | solution.py:480
  83.7 8.2 %copy-start.6 = (bf16[2,2,8,64,128]{4,3,2,1,0:T(8,128)(2,1)S(1)}, bf16[2,2,8,64,128]{4,3,2,1,0:T(8,128)(2,1)}, u32[]{:S(2)}) copy-start(bf16[2,2,8,64,128]{4,3,2,1,0:T(8,128)(2,1)} %get-tuple-element.53) | copy-start | bytes 1572868
  83.7 8.3 %copy-start.7 = (bf16[2,2,8,64,128]{4,3,2,1,0:T(8,128)(2,1)S(1)}, bf16[2,2,8,64,128]{4,3,2,1,0:T(8,128)(2,1)}, u32[]{:S(2)}) copy-start(bf16[2,2,8,64,128]{4,3,2,1,0:T(8,128)(2,1)} %get-tuple-element.55) | copy-start | bytes 1572868
  83.7 8.4 %collective-permute-start.10 = (bf16[2,1,8,64,128]{4,3,2,1,0:T(8,128)(2,1)}, bf16[2,1,8,64,128]{4,3,2,1,0:T(8,128)(2,1)S(1)}, u32[]{:S(2)}, u32[]{:S(2)}) collective-permute-start(bf16[2,1,8,64,128]{4,3,2,1,0:T(8,128)(2,1)} %get-tuple-element.56), channel_id=1, source_target_pairs={{0,48},{16,0},{32,16},{48,32},{1,49},{17,1},{33,17},{49,33},{2,50}... | collective-permute-start | bytes 786440 | tf_op jit(solution)/shard_map/ppermute | solution.py:480
  86.5 26.9 %all-to-all-start.2 = ((bf16[16,192,256]{2,1,0:T(8,128)(2,1)}), bf16[16,192,256]{2,1,0:T(8,128)(2,1)}, u32[]{:S(2)}, u32[]{:S(2)}) async-start(bf16[16,192,256]{2,1,0:T(8,128)(2,1)} %get-tuple-element.44), calls=%async_computation.2 | async-start | bytes 3145728 | tf_op jit(solution)/shard_map/all_to_all | solution.py:504
  92.0 7.3 %collective-permute-start.8 = (bf16[2,1,8,64,128]{4,3,2,1,0:T(8,128)(2,1)}, bf16[2,1,8,64,128]{4,3,2,1,0:T(8,128)(2,1)S(1)}, u32[]{:S(2)}, u32[]{:S(2)}) collective-permute-start(bf16[2,1,8,64,128]{4,3,2,1,0:T(8,128)(2,1)} %get-tuple-element.54), channel_id=1, source_target_pairs={{0,16},{16,32},{32,48},{48,0},{1,17},{17,33},{33,49},{49,1},{2,18}... | collective-permute-start | bytes 786440 | tf_op jit(solution)/shard_map/ppermute | solution.py:480
  93.0 28.2 %collective-permute-start.11 = (bf16[2,2,8,64,128]{4,3,2,1,0:T(8,128)(2,1)}, bf16[2,2,8,64,128]{4,3,2,1,0:T(8,128)(2,1)}, u32[]{:S(2)}, u32[]{:S(2)}) collective-permute-start(bf16[2,2,8,64,128]{4,3,2,1,0:T(8,128)(2,1)} %pad_maximum_fusion.2), channel_id=1, source_target_pairs={{0,48},{16,0},{32,16},{48,32},{1,49},{17,1},{33,17},{49,33},{2,50}... | collective-permute-start | bytes 1572872 | tf_op jit(solution)/shard_map/ppermute | solution.py:480
  99.4 21.8 %copy-start.5 = (bf16[2,2,8,64,128]{4,3,2,1,0:T(8,128)(2,1)S(1)}, bf16[2,2,8,64,128]{4,3,2,1,0:T(8,128)(2,1)}, u32[]{:S(2)}) copy-start(bf16[2,2,8,64,128]{4,3,2,1,0:T(8,128)(2,1)} %get-tuple-element.52) | copy-start | bytes 1572868
  100.3 21.0 %collective-permute-start.9 = (bf16[2,2,8,64,128]{4,3,2,1,0:T(8,128)(2,1)}, bf16[2,2,8,64,128]{4,3,2,1,0:T(8,128)(2,1)}, u32[]{:S(2)}, u32[]{:S(2)}) collective-permute-start(bf16[2,2,8,64,128]{4,3,2,1,0:T(8,128)(2,1)} %pad_maximum_fusion.1), channel_id=1, source_target_pairs={{0,16},{16,32},{32,48},{48,0},{1,17},{17,33},{33,49},{49,1},{2,18}... | collective-permute-start | bytes 1572872 | tf_op jit(solution)/shard_map/ppermute | solution.py:480
  116.8 6.1 %copy-start.2 = (bf16[2,128,768]{2,1,0:T(8,128)(2,1)S(1)}, bf16[2,128,768]{2,1,0:T(8,128)(2,1)}, u32[]{:S(2)}) copy-start(bf16[2,128,768]{2,1,0:T(8,128)(2,1)} %param.19) | copy-start | bytes 1179652
  116.8 12.3 %collective-permute-start.5 = (bf16[5,384,256]{2,1,0:T(8,128)(2,1)}, bf16[5,384,256]{2,1,0:T(8,128)(2,1)}, u32[]{:S(2)}, u32[]{:S(2)}) collective-permute-start(bf16[5,384,256]{2,1,0:T(8,128)(2,1)} %get-tuple-element.48.send_ref), channel_id=1, source_target_pairs={{0,8},{8,0},{1,9},{9,1},{2,10},{10,2},{3,11},{11,3},{4,12},{12,4},... | collective-permute-start | bytes 2949128 | tf_op jit(solution)/shard_map/ppermute | solution.py:500
  122.7 1.6 collective-permute-start.12
  122.9 6.2 %collective-permute-start.7 = (bf16[256,768]{1,0:T(8,128)(2,1)S(1)}, bf16[256,768]{1,0:T(8,128)(2,1)S(1)}, u32[]{:S(2)}, u32[]{:S(2)}) collective-permute-start(bf16[256,768]{1,0:T(8,128)(2,1)S(1)} %bitcast.66), channel_id=1, source_target_pairs={{0,8},{8,0},{1,9},{9,1},{2,10},{10,2},{3,11},{11,3},{4,12},{12,4},... | collective-permute-start | bytes 1179656 | tf_op jit(solution)/shard_map/ppermute | solution.py:500
  123.3 5.8 %collective-permute-start.6 = (bf16[256,768]{1,0:T(8,128)(2,1)}, bf16[256,768]{1,0:T(8,128)(2,1)S(1)}, u32[]{:S(2)}, u32[]{:S(2)}) collective-permute-start(bf16[256,768]{1,0:T(8,128)(2,1)} %get-tuple-element.49.own_normed_ref), channel_id=1, source_target_pairs={{0,8},{8,0},{1,9},{9,1},{2,10},{10,2},{3,11},{11,3},{4,12},{12,4},... | collective-permute-start | bytes 1179656 | tf_op jit(solution)/shard_map/ppermute | solution.py:500
  125.1 12.0 %all-to-all-start.4 = ((bf16[16,64,128]{2,1,0:T(8,128)(2,1)}), bf16[16,64,128]{2,1,0:T(8,128)(2,1)S(1)}, u32[]{:S(2)}, u32[]{:S(2)}) async-start(bf16[16,64,128]{2,1,0:T(8,128)(2,1)} %bitcast.27), calls=%async_computation.4 | async-start | bytes 524288 | tf_op jit(solution)/shard_map/all_to_all | solution.py:504
  137.1 44.5 %all-to-all-start.3 = ((bf16[64,64,384]{2,1,0:T(8,128)(2,1)}), bf16[64,64,384]{2,1,0:T(8,128)(2,1)}, u32[]{:S(2)}, u32[]{:S(2)}) async-start(bf16[64,64,384]{2,1,0:T(8,128)(2,1)} %shard_map.164), calls=%async_computation.3 | async-start | bytes 6291456 | tf_op jit(solution)/shard_map/all_to_all | solution.py:504
  186.3 8.1 %copy-start.13 = (bf16[128,16]{0,1:T(8,128)(2,1)S(1)}, bf16[128,16]{0,1:T(8,128)(2,1)}, u32[]{:S(2)}) copy-start(bf16[128,16]{0,1:T(8,128)(2,1)} %param.16) | copy-start | bytes 12292
  186.3 54.2 %all-to-all-start.5 = ((bf16[64,80,384]{2,1,0:T(8,128)(2,1)}), bf16[64,80,384]{2,1,0:T(8,128)(2,1)}, u32[]{:S(2)}, u32[]{:S(2)}) async-start(bf16[64,80,384]{2,1,0:T(8,128)(2,1)} %broadcast_in_dim.11), calls=%async_computation.5 | async-start | bytes 7864320 | tf_op jit(solution)/shard_map/all_to_all | solution.py:504
  240.5 16.8 %collective-permute-start.13 = (bf16[64,80,384]{2,1,0:T(8,128)(2,1)}, bf16[64,80,384]{2,1,0:T(8,128)(2,1)}, u32[]{:S(2)}, u32[]{:S(2)}) collective-permute-start(bf16[64,80,384]{2,1,0:T(8,128)(2,1)} %all-to-all-done.5.block_ref), channel_id=1, source_target_pairs={{0,8},{8,0},{1,9},{9,1},{2,10},{10,2},{3,11},{11,3},{4,12},{12,4},... | collective-permute-start | bytes 11796488 | tf_op jit(solution)/shard_map/ppermute | solution.py:500
  245.9 5.0 %collective-permute-start.14 = (f32[8,16,384]{2,1,0:T(8,128)}, f32[8,16,384]{2,1,0:T(8,128)S(1)}, u32[]{:S(2)}, u32[]{:S(2)}) collective-permute-start(f32[8,16,384]{2,1,0:T(8,128)} %shard_map.169.mine_ref), channel_id=1, source_target_pairs={{0,8},{8,0},{1,9},{9,1},{2,10},{10,2},{3,11},{11,3},{4,12},{12,4},... | collective-permute-start | bytes 589832 | tf_op jit(solution)/shard_map/ppermute | solution.py:500
  257.3 5.0 %copy-start.1 = (bf16[128,64,128]{2,1,0:T(8,128)(2,1)S(1)}, bf16[128,64,128]{2,1,0:T(8,128)(2,1)}, u32[]{:S(2)}) copy-start(bf16[128,64,128]{2,1,0:T(8,128)(2,1)} %param.15) | copy-start | bytes 6291460
  (7 other events, 13.3 us)

commit v5 on v4

--- a/solution.py
+++ b/solution.py
@@ -39,12 +39,12 @@
 
 
 def attend_kernel(factor, part, base_ref, cross_ref, chain_col_ref, chain_row_ref, rows_ref, *refs):
-    bias_at, out_ref, grad_sum = attend_places(refs[:5]), refs[5], refs[6]
-    bias_full, logits, exp_half, grad_half = refs[7:]
+    bias_at, out_ref, grad_refs, cross_sum_ref = attend_places(refs[:5]), refs[5], refs[6:10], refs[10]
+    bias_full, logits, exp_half, grad_half, grad_sum = refs[11:]
     blocks, width, lanes = rows_ref.shape
     size = width // 4
     count = blocks * lanes
-    chunk = 128
+    chunk = 256
 
     @pl.when(pl.program_id(0) == 0)
     def _():
@@ -69,6 +69,7 @@
     query_t, key_t, value_t, grad_t = take(0), take(1), take(2), take(3)
     key = key_t.T
     value = value_t.T
+    query = query_t.T
     peak = jnp.full((1, count), -jnp.inf, f32)
     for p in range(count // chunk):
         at = pl.ds(chunk * p, chunk)
@@ -83,6 +84,7 @@
     inverse = 1.0 / summed[size : size + 1]
     attended_t = summed[:size] * inverse
     scaled_t = (grad_t.astype(f32) * inverse).astype(bf16)
+    scaled = scaled_t.T
     delta = jnp.sum(scaled_t.astype(f32) * attended_t, axis=0, keepdims=True)
     key_grad = []
     value_grad = []
@@ -94,8 +96,8 @@
         half = grad.astype(bf16)
         grad_half[at, :] = half
         grad_sum[at, :] += grad
-        key_grad.append(dot(half, query_t, ((1,), (1,))))
-        value_grad.append(dot(terms, scaled_t, ((1,), (1,))))
+        key_grad.append(dot(half, query, ((1,), (0,))))
+        value_grad.append(dot(terms, scaled, ((1,), (0,))))
     query_grad_t = dot(key_t, grad_half[...], ((1,), (0,))) * factor
     key_grad_t = jnp.concatenate(key_grad, axis=0).T
     value_grad_t = jnp.concatenate(value_grad, axis=0).T
@@ -104,22 +106,18 @@
         for t in range(blocks):
             out_ref[t, index * size : (index + 1) * size, :] = array[:, t * lanes : (t + 1) * lanes]
 
-
-def pack_kernel(part, base_ref, chain_col_ref, chain_row_ref, sum_ref, *refs):
-    grad_at, cross_ref = attend_places(refs[:5]), refs[5]
-    count = sum_ref.shape[0]
-    lanes = refs[0].shape[4]
-    cross = jnp.zeros((1, count), f32)
-    for p in range(count // part):
-        at = rows_of(base_ref, p, part)
-        block = sum_ref[at, :]
-        differ = chain_col_ref[at, 0:1] != chain_row_ref[0:1, :]
-        cross += jnp.sum(jnp.where(differ, block, 0.0), axis=0, keepdims=True)
-        half = block.astype(bf16)
-        ref, lead = grad_at(p // 2, p % 2)
-        for t in range(count // lanes):
-            ref[(*lead, t)] = half[:, t * lanes : (t + 1) * lanes]
-    cross_ref[...] = jnp.broadcast_to(cross, cross_ref.shape)
+    @pl.when(pl.program_id(0) == pl.num_programs(0) - 1)
+    def _():
+        cross_sum = jnp.zeros((1, count), f32)
+        for p in range(count // part):
+            at = rows_of(base_ref, p, part)
+            block = grad_sum[at, :]
+            differ = chain_col_ref[at, 0:1] != chain_row_ref[0:1, :]
+            cross_sum += jnp.sum(jnp.where(differ, block, 0.0), axis=0, keepdims=True)
+            half = block.astype(bf16)
+            for t in range(blocks):
+                grad_refs[p // 2 % 4][p // 8, p % 2, t] = half[:, t * lanes : (t + 1) * lanes]
+        cross_sum_ref[...] = jnp.broadcast_to(cross_sum, cross_sum_ref.shape)
 
 
 def attend(base, rows, biases, cross, chains, factor):
@@ -137,21 +135,22 @@
     )
     smem = pl.BlockSpec(memory_space=pltpu.SMEM)
     by_sample = pl.BlockSpec((blocks, width, lanes), lambda s: (s // own, 0, s % own))
-    head_grads, grad_sum = pl.pallas_call(
+    block_shape = (2, 2, blocks, part, lanes)
+    head_grads, *grad_biases, cross_sum = pl.pallas_call(
         functools.partial(attend_kernel, factor, part),
         grid=(samples,),
         in_specs=[smem, smem, once(chain_col.shape), once(chain_row.shape), by_sample]
         + [once(bias.shape) for bias in biases],
-        out_specs=[by_sample, once((count, count))],
-        out_shape=[
-            jax.ShapeDtypeStruct(rows.shape, bf16),
-            jax.ShapeDtypeStruct((count, count), f32),
-        ],
+        out_specs=[by_sample] + [once(block_shape)] * 4 + [once((8, count))],
+        out_shape=[jax.ShapeDtypeStruct(rows.shape, bf16)]
+        + [jax.ShapeDtypeStruct(block_shape, bf16)] * 4
+        + [jax.ShapeDtypeStruct((8, count), f32)],
         scratch_shapes=[
             pltpu.VMEM((count, count), f32),
             pltpu.VMEM((count, count), f32),
             pltpu.VMEM((count, count), bf16),
             pltpu.VMEM((count, count), bf16),
+            pltpu.VMEM((count, count), f32),
         ],
         compiler_params=pltpu.CompilerParams(vmem_limit_bytes=vmem_bytes),
         cost_estimate=pl.CostEstimate(
@@ -160,22 +159,7 @@
             transcendentals=samples * count * count,
         ),
     )(base, cross, chain_col, chain_row, rows, *biases)
-    whole_block = (2, 2, blocks, part, lanes)
-    half_block = (2, 1, blocks, part, lanes)
-    block_shapes = [whole_block] * 3 + [half_block] * 2
-    vmem = pl.BlockSpec(memory_space=pltpu.VMEM)
-    packed = pl.pallas_call(
-        functools.partial(pack_kernel, part),
-        in_specs=[smem, vmem, vmem, vmem],
-        out_specs=[vmem] * 6,
-        out_shape=[jax.ShapeDtypeStruct(shape, bf16) for shape in block_shapes]
-        + [jax.ShapeDtypeStruct((8, count), f32)],
-        compiler_params=pltpu.CompilerParams(vmem_limit_bytes=vmem_bytes),
-        cost_estimate=pl.CostEstimate(
-            flops=2 * count * count, bytes_accessed=8 * 1024 * 1024, transcendentals=0
-        ),
-    )(base, chain_col, chain_row, grad_sum)
-    return head_grads, packed[:5], packed[5]
+    return head_grads, grad_biases, cross_sum
 
 
 def norm_parts(wide):
@@ -357,16 +341,25 @@
 
 
 def assemble_kernel(place_ref, block_ref, *refs):
-    input_ref, output_ref, stage, stage_out, sems = refs[-5:]
-    half = block_ref.shape[2]
+    input_ref, output_ref, blocks, stage, stage_out, in_sems, sems = refs[-7:]
+    half = blocks.shape[2]
     depth = 48
+    groups = in_sems.shape[0]
+    chips = blocks.shape[0]
+    size = chips // groups
     place = place_ref[0]
+    arrivals = []
+    for g in range(groups):
+        at = slice(size * g, size * (g + 1))
+        arrivals.append(pltpu.make_async_copy(block_ref.at[at], blocks.at[at], in_sems.at[g]))
+        arrivals[-1].start()
     copies = []
-    for b in range(4):
-        for group in range(2):
-            for a in range(8 * group, 8 * group + 8):
-                stage[b, depth * a : depth * (a + 1), :] = block_ref[4 * a + b, :depth, :].astype(f32)
-            rows = slice(8 * depth * group, 8 * depth * (group + 1))
+    for g in range(groups):
+        arrivals[g].wait()
+        for b in range(4):
+            for a in range(size // 4 * g, size // 4 * (g + 1)):
+                stage[b, depth * a : depth * (a + 1), :] = blocks[4 * a + b, :depth, :].astype(f32)
+            rows = slice(size // 4 * depth * g, size // 4 * depth * (g + 1))
             at = pl.multiple_of((2 * b + place) * half, 128)
             copies.append(
                 pltpu.make_async_copy(
@@ -377,7 +370,7 @@
             )
             copies[-1].start()
     for d in range(half // 8):
-        stage_out[16 * (d // 2) : 16 * (d // 2 + 1), half * (d % 2) : half * (d % 2 + 1)] = block_ref[
+        stage_out[16 * (d // 2) : 16 * (d // 2 + 1), half * (d % 2) : half * (d % 2 + 1)] = blocks[
             d, depth : depth + 16, :
         ].astype(f32)
     copies.append(pltpu.make_async_copy(stage_out, output_ref.at[place], sems.at[len(copies)]))
@@ -389,23 +382,22 @@
 def assemble(place, gathered, earlier):
     chips, depth, half = gathered.shape
     width = 2 * half
+    groups = 4
     anywhere = pl.BlockSpec(memory_space=pl.ANY)
     return pl.pallas_call(
         assemble_kernel,
-        in_specs=[
-            pl.BlockSpec(memory_space=pltpu.SMEM),
-            pl.BlockSpec(memory_space=pltpu.VMEM),
-        ]
-        + [anywhere] * len(earlier),
+        in_specs=[pl.BlockSpec(memory_space=pltpu.SMEM), anywhere] + [anywhere] * len(earlier),
         out_specs=[anywhere, anywhere],
         out_shape=[
             jax.ShapeDtypeStruct((width, 4 * width), f32),
             jax.ShapeDtypeStruct((2, half, width), f32),
         ],
         scratch_shapes=[
+            pltpu.VMEM((chips, depth, half), bf16),
             pltpu.VMEM((4, width, half), f32),
             pltpu.VMEM((half, width), f32),
-            pltpu.SemaphoreType.DMA((9,)),
+            pltpu.SemaphoreType.DMA((groups,)),
+            pltpu.SemaphoreType.DMA((4 * groups + 1,)),
         ],
         input_output_aliases={2 + k: k for k in range(len(earlier))},
         compiler_params=pltpu.CompilerParams(vmem_limit_bytes=vmem_bytes),
@@ -413,6 +405,18 @@
             flops=0, bytes_accessed=10 * 1024 * 1024, transcendentals=0
         ),
     )(place, gathered, *earlier)
+
+
+def total_kernel(parts_ref, small_ref, out_ref):
+    chips, depth, _ = parts_ref.shape
+    total = parts_ref[0].astype(f32)
+    for p in range(1, chips):
+        total = total + parts_ref[p].astype(f32)
+    total = total.astype(bf16)
+    small = small_ref[...].astype(bf16)
+    for p in range(out_ref.shape[0]):
+        out_ref[p, :depth, :] = total
+        out_ref[p, depth:, :] = small
 
 
 def gather_small_kernel(block_ref, out_ref):
@@ -439,7 +443,7 @@
     )(gathered)
 
 
-def finish_small_kernel(tokens, mine_ref, other_ref, table_ref, sums_ref):
+def finish_small_kernel(tokens, mine_ref, other_ref, table_ref, pair_ref, cross_ref):
     zy, rows, half = mine_ref.shape
     levels = table_ref.shape[0]
     refs = (mine_ref, other_ref)
@@ -460,20 +464,16 @@
         table_ref[:, r * half : (r + 1) * half] = dot(hot, high, ((0,), (0,))) + dot(
             hot, low, ((0,), (0,))
         )
-    sums_ref[0] = jnp.sum(mine_ref[...], axis=0)
-    sums_ref[1] = jnp.sum(other_ref[...], axis=0)
-
-
-def finish_small(mine, other, levels, tokens):
-    zy, rows, half = mine.shape
-    return pl.pallas_call(
-        functools.partial(finish_small_kernel, tokens),
-        out_shape=[
-            jax.ShapeDtypeStruct((levels, 4 * half), f32),
-            jax.ShapeDtypeStruct((2, rows, half), f32),
-        ],
-        cost_estimate=pl.CostEstimate(flops=0, bytes_accessed=2 << 20, transcendentals=0),
-    )(mine, other)
+    sums = jnp.sum(mine_ref[...], axis=0) + jnp.sum(other_ref[...], axis=0)
+    heads, lanes = pair_ref.shape
+    per_row = half // lanes
+    pair = [
+        sums[8 + h // per_row : 9 + h // per_row, h % per_row * lanes : (h % per_row + 1) * lanes]
+        for h in range(heads)
+    ]
+    pair_ref[...] = jnp.concatenate(pair, axis=0)
+    last = sums[13:14, lanes : 2 * lanes]
+    cross_ref[...] = last[:, :heads] + last[:, heads : 2 * heads]
 
 
 def ring(array, shift):
@@ -486,13 +486,9 @@
     return [near, above, below, ring(below[:, :1], 1), ring(above[:, 1:], 3)]
 
 
-def sum_bias(near, above, below, first, second):
-    add = lambda *arrays: sum(a.astype(f32) for a in arrays)
-    from_below = ring(first, 1)
-    from_above = ring(second, 3)
-    above = jnp.concatenate([add(above[:, :1], from_below).astype(bf16), above[:, 1:]], axis=1)
-    below = jnp.concatenate([below[:, :1], add(below[:, 1:], from_above).astype(bf16)], axis=1)
-    total = add(near, ring(above, 1), ring(below, 3))
+def sum_bias(near, above, far, below):
+    arrived = [near, ring(above, 1), ring(far, 2), ring(below, 3)]
+    total = sum(a.astype(f32) for a in arrived)
     return total[0] + swap(total[1].astype(bf16)).astype(f32)
 
 
@@ -502,10 +498,6 @@
 
 def exchange(array, axes):
     return lax.all_to_all(array, axes, 0, 0, tiled=True)
-
-
-def spread(array, axes, count):
-    return exchange(jnp.broadcast_to(array[None], (count,) + array.shape), axes)
 
 
 def shards(
@@ -606,12 +598,10 @@
         "hji,ch->ijc", grad_bias_half, pair_weight, preferred_element_type=f32
     ).astype(bf16)
     grad_pair_part = jnp.einsum(
-        "ijc,hji->ch", pair_feats, grad_bias_half, preferred_element_type=f32
+        "ijc,hji->hc", pair_feats, grad_bias_half, preferred_element_type=f32
     )
 
     parts = exchange(payload, chip_axes)
-    summed = jnp.sum(parts.astype(f32), axis=0).astype(bf16)
-    pair_size = pair_weight.shape[0] * heads
     cross_part = jnp.sum(cross_sum[0])
     cross_high = cross_part.astype(bf16).astype(f32)
     at_head = (jnp.arange(heads) == head).astype(f32)
@@ -621,8 +611,13 @@
     flat = jnp.concatenate([table_rows.reshape(-1), grad_pair_part.reshape(-1), last])
     small_depth = 16
     small = jnp.pad(flat, (0, small_depth * half - flat.size)).reshape(small_depth, half)
-    block = jnp.concatenate([summed, small.astype(bf16)], axis=0)
-    gathered = spread(block, chip_axes, chip_count)
+    (block,) = in_vmem(
+        total_kernel,
+        [((chip_count, parts.shape[1] + small_depth, half), bf16)],
+        (parts, small),
+        parts.size,
+    )
+    gathered = exchange(block, chip_axes)
     pair_shape = grad_pair.shape
     gathered, updated, grad_tokens, grad_pair = lax.optimization_barrier(
         (gathered, updated, grad_tokens, grad_pair.reshape(-1, pair_shape[2]))
@@ -634,11 +629,14 @@
     earlier = assemble(core_at, gathered, ())
     input_weight_grad, output_weight_grad = assemble(1 - core_at, other, earlier)
     output_weight_grad = output_weight_grad.reshape(width, width)
-    grad_table, sums = finish_small(mine_small, other_small, level_count, blocks)
-    pair_rows = (sums[0] + sums[1])[8:].reshape(-1)
-    grad_pair_weight = pair_rows[:pair_size].reshape(pair_weight.shape)
-    crosses = sums[0, 13] + sums[1, 13]
-    grad_cross = crosses[128:144] + crosses[144:160]
+    grad_table, grad_pair_weight, grad_cross = in_vmem(
+        functools.partial(finish_small_kernel, blocks),
+        [((level_count, 4 * half), f32), (pair_weight.shape[::-1], f32), ((1, heads), f32)],
+        (mine_small, other_small),
+        0,
+    )
+    grad_pair_weight = grad_pair_weight.T
+    grad_cross = grad_cross.reshape(heads)
     return (
         updated,
         grad_tokens,

time: 264 us -> 256 us (0.970)
  other arithmetic: 10.1 us -> 4.07 us
  local copies, waits for them, and re-layouts: 14.3 us -> 11.5 us
    pallas_call x4 -> x6, Pallas kernels: 22.5 us -> 29.9 us  [in_vmem(): pl.pallas_call(kernel, in_specs=scalars + [vmem] * (len(operands) - smem)...]
    pallas_call x2 -> x0, Pallas kernels: 6.99 us -> none  [the longest x1 4.14 us: attend(): pl.pallas_call(functools.partial(pack_kernel, part), in_specs=[smem, vmem...]
    all_to_all x6, starting transfers between devices: 37.6 us -> 41.2 us  [exchange(): return lax.all_to_all(array, axes, 0, 0, tiled=True)]
    ppermute x8 -> x7, waiting for transfers between devices: 19.1 us -> 15.8 us  [ring(): return lax.ppermute(array, 'y', [(i, (i + shift) % 4) for i in range(4)])]
    all_to_all x6, waiting for transfers between devices: 86 us -> 89.3 us  [exchange(): return lax.all_to_all(array, axes, 0, 0, tiled=True)]
    ppermute x8 -> x7, starting transfers between devices: 11.4 us -> 10.7 us  [ring(): return lax.ppermute(array, 'y', [(i, (i + shift) % 4) for i in range(4)])]
  transfers between devices with their start and end apart: 21 -> 20, of which waited for: 12 -> 11; matrix products, arithmetic and copies ran while one was open for 6% -> 5% of each run, Pallas kernels for 12% -> 12%
where the time goes in v5:
time: 256 us; the launch traced here: 255 us
  waiting for transfers between devices  108 us (42%)
  starting transfers between devices  62.5 us (24%)
  Pallas kernels  62 us (24%)
  local copies, waits for them, and re-layouts  11.5 us (4%)
  other arithmetic  4.07 us (2%)
  matrix products  3.96 us (2%)
    all_to_all x6, waiting for transfers between devices, exchange(): return lax.all_to_all(array, axes, 0, 0, tiled=True)  89.3 us
    all_to_all x6, starting transfers between devices, exchange(): return lax.all_to_all(array, axes, 0, 0, tiled=True)  41.2 us
    pallas_call x6, Pallas kernels, in_vmem(): pl.pallas_call(kernel, in_specs=scalars + [vmem] * (len(operands) - smem)...  29.9 us
    pallas_call x1, Pallas kernels, attend(): pl.pallas_call(functools.partial(attend_kernel, factor, part), grid=(samp...  22.1 us
    ppermute x7, waiting for transfers between devices, ring(): return lax.ppermute(array, 'y', [(i, (i + shift) % 4) for i in range(4)])  15.8 us
    ppermute x7, starting transfers between devices, ring(): return lax.ppermute(array, 'y', [(i, (i + shift) % 4) for i in range(4)])  10.7 us
    ppermute x7, starting transfers between devices, swap(): return lax.ppermute(array, 'core', [(0, 1), (1, 0)])  10.6 us
    pallas_call x2, Pallas kernels, assemble(): pl.pallas_call(assemble_kernel, in_specs=[pl.BlockSpec(memory_space=pltpu...  8.07 us
  transfers between devices with their start and end apart: 20, of which 11 were waited for; matrix products, arithmetic and copies ran while one was open for 5% of the time, Pallas kernels for 12%

profile of v5, /device:TPU:1, one launch (start us, length us, event | category | flops | bytes accessed | tf_op | source)
XLA Modules:
  0.0 254.7 jit_solution(18396923214304087288)
XLA Ops:
  0.7 1.6 copy-done
  2.2 1.9 fusion.16
  5.1 8.4 %all-to-all-start = ((bf16[16,80,128]{2,1,0:T(8,128)(2,1)}), bf16[16,80,128]{2,1,0:T(8,128)(2,1)S(1)}, u32[]{:S(2)}, u32[]{:S(2)}) async-start(bf16[16,80,128]{2,1,0:T(8,128)(2,1)} %copy.36), calls=%async_computation | async-start | bytes 655360 | tf_op jit(solution)/shard_map/all_to_all | solution.py:500
  14.4 6.6 %shard_map.161 = (bf16[16,192,256]{2,1,0:T(8,128)(2,1)}, f32[768,256]{1,0:T(8,128)}, f32[768,256]{1,0:T(8,128)}, bf16[256,768]{1,0:T(8,128)(2,1)}) custom-call(bf16[256,768]{1,0:T(8,128)(2,1)} %bitcast.64, bf16[256,768]{1,0:T(8,128)(2,1)} %bitcast.59, f32[2,1536]{1,0:T(2,128)} %fusion.11.mod_ref, bf16[768,3072]{1,0:T(8,128)(2,1)} %weight_ref.3, ...), custom_call_target="tpu_custom_call" | custom-call | flops 1509949440 | bytes 6696960 | tf_op jit(solution)/shard_map/pallas_call | solution.py:217
  21.8 2.4 collective-permute-start
  25.5 5.2 %all-to-all-start.1 = ((bf16[16,192,256]{2,1,0:T(8,128)(2,1)}), bf16[16,192,256]{2,1,0:T(8,128)(2,1)}, u32[]{:S(2)}, u32[]{:S(2)}) async-start(bf16[16,192,256]{2,1,0:T(8,128)(2,1)} %get-tuple-element.41), calls=%async_computation.1 | async-start | bytes 3145728 | tf_op jit(solution)/shard_map/all_to_all | solution.py:500
  32.0 1.5 collective-permute-start.1
  33.5 11.8 %collective-permute-done.2.refs_2_ = bf16[2,2,528,128]{3,2,1,0:T(8,128)(2,1)S(1)} collective-permute-done((bf16[2,2,528,128]{3,2,1,0:T(8,128)(2,1)S(1)}, bf16[2,2,528,128]{3,2,1,0:T(8,128)(2,1)S(1)}, u32[]{:S(2)}, u32[]{:S(2)}) %collective-permute-start.2) | collective-permute-done | bytes 540704 | tf_op jit(solution)/shard_map/ppermute | solution.py:480
  45.5 2.7 %collective-permute-start.4 = (bf16[2,1,528,128]{3,2,1,0:T(8,128)(2,1)S(1)}, bf16[2,1,528,128]{3,2,1,0:T(8,128)(2,1)}, u32[]{:S(2)}, u32[]{:S(2)}) collective-permute-start(bf16[2,1,528,128]{3,2,1,0:T(8,128)(2,1)S(1)} %slice.32), channel_id=1, source_target_pairs={{0,48},{16,0},{32,16},{48,32},{1,49},{17,1},{33,17},{49,33},{2,50}... | collective-permute-start | bytes 811016 | tf_op jit(solution)/shard_map/ppermute | solution.py:480
  49.4 4.0 %collective-permute-done.3.refs_3_ = bf16[2,1,528,128]{3,2,1,0:T(8,128)(2,1)S(1)} collective-permute-done((bf16[2,1,528,128]{3,2,1,0:T(8,128)(2,1)S(1)}, bf16[2,1,528,128]{3,2,1,0:T(8,128)(2,1)S(1)}, u32[]{:S(2)}, u32[]{:S(2)}) %collective-permute-start.3) | collective-permute-done | bytes 270368 | tf_op jit(solution)/shard_map/ppermute | solution.py:480
  53.4 1.8 all-to-all-done.1.rows_ref
  56.8 22.1 %shard_map.162 = (bf16[16,192,256]{2,1,0:T(8,128)(2,1)}, bf16[2,2,8,64,128]{4,3,2,1,0:T(8,128)(2,1)}, bf16[2,2,8,64,128]{4,3,2,1,0:T(8,128)(2,1)}, bf16[2,2,8,64...) custom-call(s32[16]{0:T(128)} %stack.76.base_ref, f32[1]{0:T(128)} %dynamic_slice.3.cross_ref, ...), custom_call_target="tpu_custom_call" | custom-call | flops 2415919104 | bytes 16777216 | tf_op jit(solution)/shard_map/pallas_call | solution.py:139
  78.9 5.5 %all-to-all-start.2 = ((bf16[16,192,256]{2,1,0:T(8,128)(2,1)}), bf16[16,192,256]{2,1,0:T(8,128)(2,1)}, u32[]{:S(2)}, u32[]{:S(2)}) async-start(bf16[16,192,256]{2,1,0:T(8,128)(2,1)} %get-tuple-element.43), calls=%async_computation.2 | async-start | bytes 3145728 | tf_op jit(solution)/shard_map/all_to_all | solution.py:500
  85.7 2.6 %collective-permute-start.9 = (bf16[2,2,8,64,128]{4,3,2,1,0:T(8,128)(2,1)}, bf16[2,2,8,64,128]{4,3,2,1,0:T(8,128)(2,1)}, u32[]{:S(2)}, u32[]{:S(2)}) collective-permute-start(bf16[2,2,8,64,128]{4,3,2,1,0:T(8,128)(2,1)} %get-tuple-element.52), channel_id=1, source_target_pairs={{0,32},{16,48},{32,0},{48,16},{1,33},{17,49},{33,1},{49,17},{2,34}... | collective-permute-start | bytes 1572872 | tf_op jit(solution)/shard_map/ppermute | solution.py:480
  89.4 16.7 %all-to-all-done.2.back_ref = bf16[16,192,256]{2,1,0:T(8,128)(2,1)} async-done(((bf16[16,192,256]{2,1,0:T(8,128)(2,1)}), bf16[16,192,256]{2,1,0:T(8,128)(2,1)}, u32[]{:S(2)}, u32[]{:S(2)}) %all-to-all-start.2) | async-done | bytes 1572896 | tf_op jit(solution)/shard_map/all_to_all | solution.py:500
  106.1 3.4 %shard_map.163 = (bf16[5,384,256]{2,1,0:T(8,128)(2,1)}, bf16[5,384,256]{2,1,0:T(8,128)(2,1)}) custom-call(s32[1]{0:T(128)} %bitcast.core_ref.place_ref, bf16[16,192,256]{2,1,0:T(8,128)(2,1)} %all-to-all-done.2.back_ref, f32[768,256]{1,0:T(8,128)} %get-tuple-element.44.gate_ref, f32[768,256]{1,0:T(8,128)} %get-tuple-element.45.grad_gated_ref), custom_call_target="tpu_custom_call" | custom-call | bytes 3145732 | tf_op jit(solution)/shard_map/pallas_call | solution.py:217
  109.5 4.2 %collective-permute-start.5 = (bf16[5,384,256]{2,1,0:T(8,128)(2,1)}, bf16[5,384,256]{2,1,0:T(8,128)(2,1)}, u32[]{:S(2)}, u32[]{:S(2)}) collective-permute-start(bf16[5,384,256]{2,1,0:T(8,128)(2,1)} %get-tuple-element.47.send_ref), channel_id=1, source_target_pairs={{0,8},{8,0},{1,9},{9,1},{2,10},{10,2},{3,11},{11,3},{4,12},{12,4},... | collective-permute-start | bytes 2949128 | tf_op jit(solution)/shard_map/ppermute | solution.py:496
  113.7 1.7 convert_add_fusion
  117.9 5.3 %all-to-all-start.4 = ((bf16[16,64,128]{2,1,0:T(8,128)(2,1)}), bf16[16,64,128]{2,1,0:T(8,128)(2,1)S(1)}, u32[]{:S(2)}, u32[]{:S(2)}) async-start(bf16[16,64,128]{2,1,0:T(8,128)(2,1)} %bitcast.27), calls=%async_computation.4 | async-start | bytes 524288 | tf_op jit(solution)/shard_map/all_to_all | solution.py:500
  124.0 5.8 %shard_map.164 = bf16[64,64,384]{2,1,0:T(8,128)(2,1)} custom-call(bf16[5,384,256]{2,1,0:T(8,128)(2,1)} %get-tuple-element.46.keep_ref, bf16[5,384,256]{2,1,0:T(8,128)(2,1)} %collective-permute-done.5.got_ref, bf16[256,768]{1,0:T(8,128)(2,1)} %get-tuple-element.48.own_normed_ref, bf16[256,768]{1,0:T(8,128)(2,1)} %copy-done.7, bf16[256,768]{1,0:T(8,128)(2,1)} %bitcast.60, ...), custom_call_target="tpu_custom_call" | custom-call | flops 1509949440 | bytes 3538944 | tf_op jit(solution)/shard_map/pallas_call | solution.py:217
  131.2 8.4 %all-to-all-start.3 = ((bf16[64,64,384]{2,1,0:T(8,128)(2,1)}), bf16[64,64,384]{2,1,0:T(8,128)(2,1)}, u32[]{:S(2)}, u32[]{:S(2)}) async-start(bf16[64,64,384]{2,1,0:T(8,128)(2,1)} %shard_map.164), calls=%async_computation.3 | async-start | bytes 6291456 | tf_op jit(solution)/shard_map/all_to_all | solution.py:500
  143.2 6.8 %shard_map.165 = (bf16[256,768]{1,0:T(8,128)(2,1)}, bf16[256,768]{1,0:T(8,128)(2,1)}, f32[8,384]{1,0:T(8,128)}) custom-call(s32[1]{0:T(128)} %bitcast.core_ref.place_ref, bf16[5,384,256]{2,1,0:T(8,128)(2,1)} %get-tuple-element.46.keep_ref, bf16[5,384,256]{2,1,0:T(8,128)(2,1)} %get-tuple-element.47.send_ref, bf16[256,768]{1,0:T(8,128)(2,1)} %bitcast.65, ...), custom_call_target="tpu_custom_call" | custom-call | flops 1509949440 | bytes 8663044 | tf_op jit(solution)/shard_map/pallas_call | solution.py:217
  151.4 26.0 %all-to-all-done.3.parts_ref = bf16[64,64,384]{2,1,0:T(8,128)(2,1)} async-done(((bf16[64,64,384]{2,1,0:T(8,128)(2,1)}), bf16[64,64,384]{2,1,0:T(8,128)(2,1)}, u32[]{:S(2)}, u32[]{:S(2)}) %all-to-all-start.3) | async-done | bytes 3145760 | tf_op jit(solution)/shard_map/all_to_all | solution.py:500
  177.3 4.5 %shard_map.166 = bf16[64,80,384]{2,1,0:T(8,128)(2,1)} custom-call(bf16[64,64,384]{2,1,0:T(8,128)(2,1)} %all-to-all-done.3.parts_ref, f32[16,384]{1,0:T(8,128)} %reshape.77.small_ref), custom_call_target="tpu_custom_call" | custom-call | flops 1572864 | bytes 3170304 | tf_op jit(solution)/shard_map/pallas_call | solution.py:217
  181.8 8.5 %all-to-all-start.5 = ((bf16[64,80,384]{2,1,0:T(8,128)(2,1)}), bf16[64,80,384]{2,1,0:T(8,128)(2,1)}, u32[]{:S(2)}, u32[]{:S(2)}) async-start(bf16[64,80,384]{2,1,0:T(8,128)(2,1)} %shard_map.166), calls=%async_computation.5 | async-start | bytes 7864320 | tf_op jit(solution)/shard_map/all_to_all | solution.py:500
  191.1 2.7 %copy.40 = bf16[128,64,128]{2,1,0:T(8,128)(2,1)} copy(bf16[128,64,128]{2,0,1:T(8,128)(2,1)S(1)} %convert_bitcast_fusion) | data formatting | bytes 4194304 | tf_op jit(solution)/shard_map/convert_element_type | solution.py:599
  193.7 42.9 %all-to-all-done.5.block_ref = bf16[64,80,384]{2,1,0:T(8,128)(2,1)} async-done(((bf16[64,80,384]{2,1,0:T(8,128)(2,1)}), bf16[64,80,384]{2,1,0:T(8,128)(2,1)}, u32[]{:S(2)}, u32[]{:S(2)}) %all-to-all-start.5) | async-done | bytes 3932192 | tf_op jit(solution)/shard_map/all_to_all | solution.py:500
  236.7 3.2 %collective-permute-start.12 = (bf16[64,80,384]{2,1,0:T(8,128)(2,1)}, bf16[64,80,384]{2,1,0:T(8,128)(2,1)}, u32[]{:S(2)}, u32[]{:S(2)}) collective-permute-start(bf16[64,80,384]{2,1,0:T(8,128)(2,1)} %all-to-all-done.5.block_ref), channel_id=1, source_target_pairs={{0,8},{8,0},{1,9},{9,1},{2,10},{10,2},{3,11},{11,3},{4,12},{12,4},... | collective-permute-start | bytes 11796488 | tf_op jit(solution)/shard_map/ppermute | solution.py:496
  239.9 1.9 shard_map.169.mine_ref
  241.9 4.0 %shard_map.167 = (f32[768,3072]{1,0:T(8,128)}, f32[2,384,768]{2,1,0:T(8,128)}) custom-call(s32[1]{0:T(128)} %bitcast.core_ref.place_ref, bf16[64,80,384]{2,1,0:T(8,128)(2,1)} %all-to-all-done.5.block_ref), custom_call_target="tpu_custom_call" | custom-call | bytes 10485760 | tf_op jit(solution)/shard_map/pallas_call | solution.py:387
  247.5 2.9 %shard_map.170 = (f32[200,1536]{1,0:T(8,128)}, f32[16,128]{1,0:T(8,128)}, f32[1,16]{1,0:T(1,128)}) custom-call(f32[8,16,384]{2,1,0:T(8,128)} %shard_map.169.mine_ref, f32[8,16,384]{2,1,0:T(8,128)} %copy-done.8), custom_call_target="tpu_custom_call" | custom-call | bytes 393216 | tf_op jit(solution)/shard_map/pallas_call | solution.py:217
  250.4 4.1 %shard_map.168 = (f32[768,3072]{1,0:T(8,128)}, f32[2,384,768]{2,1,0:T(8,128)}) custom-call(s32[1]{0:T(128)S(6)} %sub.17.place_ref, bf16[64,80,384]{2,1,0:T(8,128)(2,1)} %collective-permute-done.12.block_ref, f32[768,3072]{1,0:T(8,128)} %get-tuple-element.61.refs_0_, ...), custom_call_target="tpu_custom_call", output_to_operand_aliasing={{0}: (2, {}), {1}: (3, {})} | custom-call | bytes 10485760 | tf_op jit(solution)/shard_map/pallas_call | solution.py:387
  (82 shorter events, 21.3 us)
Async XLA Ops:
  0.7 12.9 %copy-start.13 = (s32[2]{0:T(128)S(1)}, s32[2]{0:T(128)}, u32[]{:S(2)}) copy-start(s32[2]{0:T(128)} %param.11) | copy-start | bytes 28
  0.7 12.9 %copy-start.3 = (bf16[200,1536]{1,0:T(8,128)(2,1)S(1)}, bf16[200,1536]{1,0:T(8,128)(2,1)}, u32[]{:S(2)}) copy-start(bf16[200,1536]{1,0:T(8,128)(2,1)} %param.12) | copy-start | bytes 1843204
  5.1 16.5 %all-to-all-start = ((bf16[16,80,128]{2,1,0:T(8,128)(2,1)}), bf16[16,80,128]{2,1,0:T(8,128)(2,1)S(1)}, u32[]{:S(2)}, u32[]{:S(2)}) async-start(bf16[16,80,128]{2,1,0:T(8,128)(2,1)} %copy.36), calls=%async_computation | async-start | bytes 655360 | tf_op jit(solution)/shard_map/all_to_all | solution.py:500
  21.8 3.6 %collective-permute-start = (bf16[2,528,128]{2,1,0:T(8,128)(2,1)S(1)}, bf16[2,528,128]{2,1,0:T(8,128)(2,1)S(1)}, u32[]{:S(2)}, u32[]{:S(2)}) collective-permute-start(bf16[2,528,128]{2,1,0:T(8,128)(2,1)S(1)} %get-tuple-element.69), channel_id=1, source_target_pairs={{0,8},{8,0},{1,9},{9,1},{2,10},{10,2},{3,11},{11,3},{4,12},{12,4},... | collective-permute-start | bytes 811016 | tf_op jit(solution)/shard_map/ppermute | solution.py:496
  25.4 20.1 %copy-start.4 = (bf16[2,2,528,128]{3,2,1,0:T(8,128)(2,1)}, bf16[2,2,528,128]{3,2,1,0:T(8,128)(2,1)S(1)}, u32[]{:S(2)}) copy-start(bf16[2,2,528,128]{3,2,1,0:T(8,128)(2,1)S(1)} %pad_maximum_fusion.refs_0_) | copy-start | bytes 1622020
  25.4 22.8 %copy-start.15 = (f32[16]{0:T(128)S(1)}, f32[16]{0:T(128)}, u32[]{:S(2)}) copy-start(f32[16]{0:T(128)} %param.17) | copy-start | bytes 196
  25.5 29.7 %copy-start.12 = (s32[1024]{0:T(1024)S(1)}, s32[1024]{0:T(1024)}, u32[]{:S(2)}) copy-start(s32[1024]{0:T(1024)} %param.18) | copy-start | bytes 12292
  25.5 29.7 %all-to-all-start.1 = ((bf16[16,192,256]{2,1,0:T(8,128)(2,1)}), bf16[16,192,256]{2,1,0:T(8,128)(2,1)}, u32[]{:S(2)}, u32[]{:S(2)}) async-start(bf16[16,192,256]{2,1,0:T(8,128)(2,1)} %get-tuple-element.41), calls=%async_computation.1 | async-start | bytes 3145728 | tf_op jit(solution)/shard_map/all_to_all | solution.py:500
  30.6 14.7 %collective-permute-start.2 = (bf16[2,2,528,128]{3,2,1,0:T(8,128)(2,1)S(1)}, bf16[2,2,528,128]{3,2,1,0:T(8,128)(2,1)S(1)}, u32[]{:S(2)}, u32[]{:S(2)}) collective-permute-start(bf16[2,2,528,128]{3,2,1,0:T(8,128)(2,1)S(1)} %pad_maximum_fusion.refs_0_), channel_id=1, source_target_pairs={{0,16},{16,32},{32,48},{48,0},{1,17},{17,33},{33,49},{49,1},{2,18}... | collective-permute-start | bytes 1622024 | tf_op jit(solution)/shard_map/ppermute | solution.py:480
  32.0 13.4 %collective-permute-start.1 = (bf16[2,2,528,128]{3,2,1,0:T(8,128)(2,1)S(1)}, bf16[2,2,528,128]{3,2,1,0:T(8,128)(2,1)S(1)}, u32[]{:S(2)}, u32[]{:S(2)}) collective-permute-start(bf16[2,2,528,128]{3,2,1,0:T(8,128)(2,1)S(1)} %pad_maximum_fusion.refs_0_), channel_id=1, source_target_pairs={{0,48},{16,0},{32,16},{48,32},{1,49},{17,1},{33,17},{49,33},{2,50}... | collective-permute-start | bytes 1622024 | tf_op jit(solution)/shard_map/ppermute | solution.py:480
  45.3 2.9 %copy-start.9 = (bf16[2,2,528,128]{3,2,1,0:T(8,128)(2,1)}, bf16[2,2,528,128]{3,2,1,0:T(8,128)(2,1)S(1)}, u32[]{:S(2)}) copy-start(bf16[2,2,528,128]{3,2,1,0:T(8,128)(2,1)S(1)} %collective-permute-done.2.refs_2_) | copy-start | bytes 1622020
  45.4 8.0 %collective-permute-start.3 = (bf16[2,1,528,128]{3,2,1,0:T(8,128)(2,1)S(1)}, bf16[2,1,528,128]{3,2,1,0:T(8,128)(2,1)S(1)}, u32[]{:S(2)}, u32[]{:S(2)}) collective-permute-start(bf16[2,1,528,128]{3,2,1,0:T(8,128)(2,1)S(1)} %slice.31), channel_id=1, source_target_pairs={{0,16},{16,32},{32,48},{48,0},{1,17},{17,33},{33,49},{49,1},{2,18}... | collective-permute-start | bytes 811016 | tf_op jit(solution)/shard_map/ppermute | solution.py:480
  45.4 2.8 %copy-start.10 = (bf16[2,2,528,128]{3,2,1,0:T(8,128)(2,1)}, bf16[2,2,528,128]{3,2,1,0:T(8,128)(2,1)S(1)}, u32[]{:S(2)}) copy-start(bf16[2,2,528,128]{3,2,1,0:T(8,128)(2,1)S(1)} %collective-permute-done.1.refs_1_) | copy-start | bytes 1622020
  45.5 7.9 %collective-permute-start.4 = (bf16[2,1,528,128]{3,2,1,0:T(8,128)(2,1)S(1)}, bf16[2,1,528,128]{3,2,1,0:T(8,128)(2,1)}, u32[]{:S(2)}, u32[]{:S(2)}) collective-permute-start(bf16[2,1,528,128]{3,2,1,0:T(8,128)(2,1)S(1)} %slice.32), channel_id=1, source_target_pairs={{0,48},{16,0},{32,16},{48,32},{1,49},{17,1},{33,17},{49,33},{2,50}... | collective-permute-start | bytes 811016 | tf_op jit(solution)/shard_map/ppermute | solution.py:480
  53.4 3.4 %copy-start.14 = (bf16[2,1,528,128]{3,2,1,0:T(8,128)(2,1)}, bf16[2,1,528,128]{3,2,1,0:T(8,128)(2,1)S(1)}, u32[]{:S(2)}) copy-start(bf16[2,1,528,128]{3,2,1,0:T(8,128)(2,1)S(1)} %collective-permute-done.3.refs_3_) | copy-start | bytes 811012
  78.9 27.3 %all-to-all-start.2 = ((bf16[16,192,256]{2,1,0:T(8,128)(2,1)}), bf16[16,192,256]{2,1,0:T(8,128)(2,1)}, u32[]{:S(2)}, u32[]{:S(2)}) async-start(bf16[16,192,256]{2,1,0:T(8,128)(2,1)} %get-tuple-element.43), calls=%async_computation.2 | async-start | bytes 3145728 | tf_op jit(solution)/shard_map/all_to_all | solution.py:500
  84.3 29.4 %copy-start.5 = (bf16[2,2,8,64,128]{4,3,2,1,0:T(8,128)(2,1)S(1)}, bf16[2,2,8,64,128]{4,3,2,1,0:T(8,128)(2,1)}, u32[]{:S(2)}) copy-start(bf16[2,2,8,64,128]{4,3,2,1,0:T(8,128)(2,1)} %get-tuple-element.50) | copy-start | bytes 1572868
  84.3 29.4 %collective-permute-start.8 = (bf16[2,2,8,64,128]{4,3,2,1,0:T(8,128)(2,1)}, bf16[2,2,8,64,128]{4,3,2,1,0:T(8,128)(2,1)}, u32[]{:S(2)}, u32[]{:S(2)}) collective-permute-start(bf16[2,2,8,64,128]{4,3,2,1,0:T(8,128)(2,1)} %get-tuple-element.51), channel_id=1, source_target_pairs={{0,16},{16,32},{32,48},{48,0},{1,17},{17,33},{33,49},{49,1},{2,18}... | collective-permute-start | bytes 1572872 | tf_op jit(solution)/shard_map/ppermute | solution.py:480
  85.7 28.0 %collective-permute-start.9 = (bf16[2,2,8,64,128]{4,3,2,1,0:T(8,128)(2,1)}, bf16[2,2,8,64,128]{4,3,2,1,0:T(8,128)(2,1)}, u32[]{:S(2)}, u32[]{:S(2)}) collective-permute-start(bf16[2,2,8,64,128]{4,3,2,1,0:T(8,128)(2,1)} %get-tuple-element.52), channel_id=1, source_target_pairs={{0,32},{16,48},{32,0},{48,16},{1,33},{17,49},{33,1},{49,17},{2,34}... | collective-permute-start | bytes 1572872 | tf_op jit(solution)/shard_map/ppermute | solution.py:480
  88.3 25.4 %collective-permute-start.10 = (bf16[2,2,8,64,128]{4,3,2,1,0:T(8,128)(2,1)}, bf16[2,2,8,64,128]{4,3,2,1,0:T(8,128)(2,1)}, u32[]{:S(2)}, u32[]{:S(2)}) collective-permute-start(bf16[2,2,8,64,128]{4,3,2,1,0:T(8,128)(2,1)} %get-tuple-element.53), channel_id=1, source_target_pairs={{0,48},{16,0},{32,16},{48,32},{1,49},{17,1},{33,17},{49,33},{2,50}... | collective-permute-start | bytes 1572872 | tf_op jit(solution)/shard_map/ppermute | solution.py:480
  109.5 6.1 %copy-start.2 = (bf16[2,128,768]{2,1,0:T(8,128)(2,1)S(1)}, bf16[2,128,768]{2,1,0:T(8,128)(2,1)}, u32[]{:S(2)}) copy-start(bf16[2,128,768]{2,1,0:T(8,128)(2,1)} %param.19) | copy-start | bytes 1179652
  109.5 13.7 %collective-permute-start.5 = (bf16[5,384,256]{2,1,0:T(8,128)(2,1)}, bf16[5,384,256]{2,1,0:T(8,128)(2,1)}, u32[]{:S(2)}, u32[]{:S(2)}) collective-permute-start(bf16[5,384,256]{2,1,0:T(8,128)(2,1)} %get-tuple-element.47.send_ref), channel_id=1, source_target_pairs={{0,8},{8,0},{1,9},{9,1},{2,10},{10,2},{3,11},{11,3},{4,12},{12,4},... | collective-permute-start | bytes 2949128 | tf_op jit(solution)/shard_map/ppermute | solution.py:496
  115.5 1.6 collective-permute-start.11
  115.6 7.5 %collective-permute-start.7 = (bf16[256,768]{1,0:T(8,128)(2,1)S(1)}, bf16[256,768]{1,0:T(8,128)(2,1)S(1)}, u32[]{:S(2)}, u32[]{:S(2)}) collective-permute-start(bf16[256,768]{1,0:T(8,128)(2,1)S(1)} %bitcast.62), channel_id=1, source_target_pairs={{0,8},{8,0},{1,9},{9,1},{2,10},{10,2},{3,11},{11,3},{4,12},{12,4},... | collective-permute-start | bytes 1179656 | tf_op jit(solution)/shard_map/ppermute | solution.py:496
  116.1 7.1 %collective-permute-start.6 = (bf16[256,768]{1,0:T(8,128)(2,1)}, bf16[256,768]{1,0:T(8,128)(2,1)S(1)}, u32[]{:S(2)}, u32[]{:S(2)}) collective-permute-start(bf16[256,768]{1,0:T(8,128)(2,1)} %get-tuple-element.48.own_normed_ref), channel_id=1, source_target_pairs={{0,8},{8,0},{1,9},{9,1},{2,10},{10,2},{3,11},{11,3},{4,12},{12,4},... | collective-permute-start | bytes 1179656 | tf_op jit(solution)/shard_map/ppermute | solution.py:496
  117.9 13.3 %all-to-all-start.4 = ((bf16[16,64,128]{2,1,0:T(8,128)(2,1)}), bf16[16,64,128]{2,1,0:T(8,128)(2,1)S(1)}, u32[]{:S(2)}, u32[]{:S(2)}) async-start(bf16[16,64,128]{2,1,0:T(8,128)(2,1)} %bitcast.27), calls=%async_computation.4 | async-start | bytes 524288 | tf_op jit(solution)/shard_map/all_to_all | solution.py:500
  131.2 46.1 %all-to-all-start.3 = ((bf16[64,64,384]{2,1,0:T(8,128)(2,1)}), bf16[64,64,384]{2,1,0:T(8,128)(2,1)}, u32[]{:S(2)}, u32[]{:S(2)}) async-start(bf16[64,64,384]{2,1,0:T(8,128)(2,1)} %shard_map.164), calls=%async_computation.3 | async-start | bytes 6291456 | tf_op jit(solution)/shard_map/all_to_all | solution.py:500
  181.8 8.5 %copy-start.11 = (bf16[128,16]{0,1:T(8,128)(2,1)S(1)}, bf16[128,16]{0,1:T(8,128)(2,1)}, u32[]{:S(2)}) copy-start(bf16[128,16]{0,1:T(8,128)(2,1)} %param.16) | copy-start | bytes 12292
  181.8 54.9 %all-to-all-start.5 = ((bf16[64,80,384]{2,1,0:T(8,128)(2,1)}), bf16[64,80,384]{2,1,0:T(8,128)(2,1)}, u32[]{:S(2)}, u32[]{:S(2)}) async-start(bf16[64,80,384]{2,1,0:T(8,128)(2,1)} %shard_map.166), calls=%async_computation.5 | async-start | bytes 7864320 | tf_op jit(solution)/shard_map/all_to_all | solution.py:500
  236.7 13.7 %collective-permute-start.12 = (bf16[64,80,384]{2,1,0:T(8,128)(2,1)}, bf16[64,80,384]{2,1,0:T(8,128)(2,1)}, u32[]{:S(2)}, u32[]{:S(2)}) collective-permute-start(bf16[64,80,384]{2,1,0:T(8,128)(2,1)} %all-to-all-done.5.block_ref), channel_id=1, source_target_pairs={{0,8},{8,0},{1,9},{9,1},{2,10},{10,2},{3,11},{11,3},{4,12},{12,4},... | collective-permute-start | bytes 11796488 | tf_op jit(solution)/shard_map/ppermute | solution.py:496
  241.9 5.0 %collective-permute-start.13 = (f32[8,16,384]{2,1,0:T(8,128)}, f32[8,16,384]{2,1,0:T(8,128)S(1)}, u32[]{:S(2)}, u32[]{:S(2)}) collective-permute-start(f32[8,16,384]{2,1,0:T(8,128)} %shard_map.169.mine_ref), channel_id=1, source_target_pairs={{0,8},{8,0},{1,9},{9,1},{2,10},{10,2},{3,11},{11,3},{4,12},{12,4},... | collective-permute-start | bytes 589832 | tf_op jit(solution)/shard_map/ppermute | solution.py:496
  250.4 4.1 %copy-start.1 = (bf16[128,64,128]{2,1,0:T(8,128)(2,1)S(1)}, bf16[128,64,128]{2,1,0:T(8,128)(2,1)}, u32[]{:S(2)}) copy-start(bf16[128,64,128]{2,1,0:T(8,128)(2,1)} %param.15) | copy-start | bytes 6291460
  (4 other events, 3.9 us)

commit v6 on v5

--- a/solution.py
+++ b/solution.py
@@ -127,8 +127,7 @@
     own = total // lanes
     samples = 2 * own
     count = blocks * lanes
-    chain_col = jnp.broadcast_to(chains[:, None], (count, 128))
-    chain_row = jnp.broadcast_to(chains[None, :], (8, count))
+    chain_col, chain_row = chains
     part = (biases[0].shape[2] - 16) // blocks
     once = lambda shape: pl.BlockSpec(
         shape, lambda s: (0,) * len(shape), pipeline_mode=pl.Buffered(1)
@@ -420,34 +419,24 @@
 
 
 def gather_small_kernel(block_ref, out_ref):
-    zy, rows, half = out_ref.shape
+    zy = out_ref.shape[0]
     blocks = block_ref.shape[0] // zy
     for p in range(zy):
-        total = block_ref[blocks * p].astype(f32)
-        for t in range(1, blocks):
-            total = total + block_ref[blocks * p + t].astype(f32)
-        out_ref[p] = total
-
-
-def gather_small(gathered, zy, small_depth):
-    chips, depth, half = gathered.shape
-    return pl.pallas_call(
-        gather_small_kernel,
-        grid=(1,),
-        in_specs=[
-            pl.BlockSpec((chips, small_depth, half), lambda i: (0, depth // small_depth - 1, 0))
-        ],
-        out_specs=pl.BlockSpec((zy, small_depth, half), lambda i: (0, 0, 0)),
-        out_shape=jax.ShapeDtypeStruct((zy, small_depth, half), f32),
-        cost_estimate=pl.CostEstimate(flops=0, bytes_accessed=1 << 20, transcendentals=0),
-    )(gathered)
-
-
-def finish_small_kernel(tokens, mine_ref, other_ref, table_ref, pair_ref, cross_ref):
-    zy, rows, half = mine_ref.shape
+        for parity in range(2):
+            total = None
+            for t in range(blocks):
+                if t // 2 % 2 == parity:
+                    term = block_ref[blocks * p + t]
+                    total = term if total is None else total + term
+            out_ref[p, parity] = total
+
+
+def finish_small_kernel(sharers, mine_ref, other_ref, table_ref, pair_ref, cross_ref):
+    zy, _, rows, half = mine_ref.shape
     levels = table_ref.shape[0]
+    heads, lanes = pair_ref.shape
     refs = (mine_ref, other_ref)
-    values = jnp.concatenate([ref[...].reshape(zy * rows, half) for ref in refs], axis=0)
+    values = jnp.concatenate([ref[...].reshape(zy * 2 * rows, half) for ref in refs], axis=0)
     high = values.astype(bf16)
     low = (values - high.astype(f32)).astype(bf16)
     row = lax.broadcasted_iota(jnp.int32, (rows, 1), 0)
@@ -455,24 +444,25 @@
     same = []
     for ref in refs:
         for p in range(zy):
-            first = ref[p, 13:14, 160:161] * (1.0 / tokens)
-            second = ref[p, 13:14, 161:162] * (1.0 / tokens)
-            same.append(jnp.where(row < 4, first, second) == at)
+            for parity in range(2):
+                lane = 2 * lanes + 2 * heads + parity
+                level = ref[p, parity, 6:7, lane : lane + 1] * (1.0 / sharers)
+                same.append(level == at)
     for r in range(4):
-        kept = (row < 8) & (row % 4 == r)
-        hot = jnp.concatenate([jnp.where(s & kept, 1.0, 0.0) for s in same], axis=0).astype(bf16)
+        hot = jnp.concatenate([jnp.where(s & (row == r), 1.0, 0.0) for s in same], axis=0)
+        hot = hot.astype(bf16)
         table_ref[:, r * half : (r + 1) * half] = dot(hot, high, ((0,), (0,))) + dot(
             hot, low, ((0,), (0,))
         )
     sums = jnp.sum(mine_ref[...], axis=0) + jnp.sum(other_ref[...], axis=0)
-    heads, lanes = pair_ref.shape
     per_row = half // lanes
-    pair = [
-        sums[8 + h // per_row : 9 + h // per_row, h % per_row * lanes : (h % per_row + 1) * lanes]
-        for h in range(heads)
-    ]
+    pair = []
+    for h in range(heads):
+        parity, j = h // (heads // 2), h % (heads // 2)
+        at_row, at_lane = 4 + j // per_row, j % per_row * lanes
+        pair.append(sums[parity, at_row : at_row + 1, at_lane : at_lane + lanes])
     pair_ref[...] = jnp.concatenate(pair, axis=0)
-    last = sums[13:14, lanes : 2 * lanes]
+    last = sums[0, 6:7, 2 * lanes :] + sums[1, 6:7, 2 * lanes :]
     cross_ref[...] = last[:, :heads] + last[:, heads : 2 * heads]
 
 
@@ -542,7 +532,12 @@
     sent, gate_open, grad_gated, normed = before(
         acts, cots, modulation, input_weight, output_matrix, heads, factor
     )
-    sent, bias_got = lax.optimization_barrier((sent, bias_got))
+    count = chains.shape[0]
+    chain_col = jnp.broadcast_to(chains[:, None], (count, 128))
+    chain_row = jnp.broadcast_to(chains[None, :], (8, count))
+    sent, bias_got, chain_col, chain_row = lax.optimization_barrier(
+        (sent, bias_got, chain_col, chain_row)
+    )
     bias_own = jnp.concatenate(
         [
             bias_got[:, :col_count].reshape(2, blocks * col_count, row_count),
@@ -567,7 +562,7 @@
     other_normed = swap(normed)
     other_cots = swap(cots)
     head_grads, grad_biases, cross_sum = attend(
-        base, head_rows, biases, own_cross, chains, factor
+        base, head_rows, biases, own_cross, (chain_col, chain_row), factor
     )
 
     back = exchange(head_grads, head_axes)
@@ -608,8 +603,14 @@
     last = jnp.concatenate(
         [at_head * cross_high, at_head * (cross_part - cross_high), levels.astype(f32)]
     )
-    flat = jnp.concatenate([table_rows.reshape(-1), grad_pair_part.reshape(-1), last])
-    small_depth = 16
+    halves = jnp.concatenate(
+        [table_rows.reshape(2, -1), grad_pair_part.reshape(2, -1)], axis=1
+    )
+    odd = lax.axis_index("x") % 2
+    pick = lambda index: lax.dynamic_index_in_dim(halves, index, 0, keepdims=False)
+    shared = pick(odd) + lax.ppermute(pick(1 - odd), "x", [(i, i ^ 1) for i in range(4)])
+    flat = jnp.concatenate([shared, last])
+    small_depth = 8
     small = jnp.pad(flat, (0, small_depth * half - flat.size)).reshape(small_depth, half)
     (block,) = in_vmem(
         total_kernel,
@@ -623,14 +624,19 @@
         (gathered, updated, grad_tokens, grad_pair.reshape(-1, pair_shape[2]))
     )
     grad_pair = grad_pair.reshape(pair_shape)
-    mine_small = gather_small(gathered, zy_count, small_depth)
+    (mine_small,) = in_vmem(
+        gather_small_kernel,
+        [((zy_count, 2, small_depth, half), f32)],
+        (gathered[:, -small_depth:].astype(f32),),
+        0,
+    )
     other = swap(gathered)
     other_small = swap(mine_small)
     earlier = assemble(core_at, gathered, ())
     input_weight_grad, output_weight_grad = assemble(1 - core_at, other, earlier)
     output_weight_grad = output_weight_grad.reshape(width, width)
     grad_table, grad_pair_weight, grad_cross = in_vmem(
-        functools.partial(finish_small_kernel, blocks),
+        functools.partial(finish_small_kernel, blocks // 2),
         [((level_count, 4 * half), f32), (pair_weight.shape[::-1], f32), ((1, heads), f32)],
         (mine_small, other_small),
         0,

time: 256 us -> 251 us (0.980)
  waiting for transfers between devices: 108 us -> 99 us
  starting transfers between devices: 62.5 us -> 65.2 us
    all_to_all x6, waiting for transfers between devices: 89.3 us -> 58.9 us  [exchange(): return lax.all_to_all(array, axes, 0, 0, tiled=True)]
    ppermute x0 -> x1, waiting for transfers between devices: none -> 22.3 us  [shards(): lax.ppermute(pick(1 - odd), 'x', [(i, i ^ 1) for i in range(4)])]
    pallas_call x6 -> x7, Pallas kernels: 29.9 us -> 31.5 us  [in_vmem(): pl.pallas_call(kernel, in_specs=scalars + [vmem] * (len(operands) - smem)...]
  transfers between devices with their start and end apart: 20 -> 21, of which waited for: 11 -> 11; matrix products, arithmetic and copies ran while one was open for 5% -> 5% of each run, Pallas kernels for 12% -> 12%
where the time goes in v6:
time: 251 us; the launch traced here: 250 us
  waiting for transfers between devices  99 us (39%)
  starting transfers between devices  65.2 us (26%)
  Pallas kernels  61.6 us (25%)
  local copies, waits for them, and re-layouts  11.7 us (5%)
  matrix products  4.9 us (2%)
  other arithmetic  4.83 us (2%)
  between operations  2.54 us (1%)
    all_to_all x6, waiting for transfers between devices, exchange(): return lax.all_to_all(array, axes, 0, 0, tiled=True)  58.9 us
    all_to_all x6, starting transfers between devices, exchange(): return lax.all_to_all(array, axes, 0, 0, tiled=True)  41.2 us
    pallas_call x7, Pallas kernels, in_vmem(): pl.pallas_call(kernel, in_specs=scalars + [vmem] * (len(operands) - smem)...  31.5 us
    ppermute x1, waiting for transfers between devices, shards(): lax.ppermute(pick(1 - odd), 'x', [(i, i ^ 1) for i in range(4)])  22.3 us
    pallas_call x1, Pallas kernels, attend(): pl.pallas_call(functools.partial(attend_kernel, factor, part), grid=(samp...  22.1 us
    ppermute x7, waiting for transfers between devices, ring(): return lax.ppermute(array, 'y', [(i, (i + shift) % 4) for i in range(4)])  15.6 us
    ppermute x7, starting transfers between devices, swap(): return lax.ppermute(array, 'core', [(0, 1), (1, 0)])  12.2 us
    ppermute x7, starting transfers between devices, ring(): return lax.ppermute(array, 'y', [(i, (i + shift) % 4) for i in range(4)])  10.8 us
  transfers between devices with their start and end apart: 21, of which 11 were waited for; matrix products, arithmetic and copies ran while one was open for 5% of the time, Pallas kernels for 12%

profile of v6, /device:TPU:1, one launch (start us, length us, event | category | flops | bytes accessed | tf_op | source)
XLA Modules:
  0.0 249.8 jit_solution(9151733488069554332)
XLA Ops:
  0.7 1.6 copy-done
  2.2 1.9 fusion.16
  5.1 8.4 %all-to-all-start = ((bf16[16,80,128]{2,1,0:T(8,128)(2,1)}), bf16[16,80,128]{2,1,0:T(8,128)(2,1)S(1)}, u32[]{:S(2)}, u32[]{:S(2)}) async-start(bf16[16,80,128]{2,1,0:T(8,128)(2,1)} %copy.36), calls=%async_computation | async-start | bytes 655360 | tf_op jit(solution)/shard_map/all_to_all | solution.py:490
  14.4 6.6 %shard_map.161 = (bf16[16,192,256]{2,1,0:T(8,128)(2,1)}, f32[768,256]{1,0:T(8,128)}, f32[768,256]{1,0:T(8,128)}, bf16[256,768]{1,0:T(8,128)(2,1)}) custom-call(bf16[256,768]{1,0:T(8,128)(2,1)} %bitcast.62, bf16[256,768]{1,0:T(8,128)(2,1)} %bitcast.57, f32[2,1536]{1,0:T(2,128)} %fusion.11.mod_ref, bf16[768,3072]{1,0:T(8,128)(2,1)} %weight_ref.3, ...), custom_call_target="tpu_custom_call" | custom-call | flops 1509949440 | bytes 6696960 | tf_op jit(solution)/shard_map/pallas_call | solution.py:216
  23.4 2.4 collective-permute-start
  27.1 5.2 %all-to-all-start.1 = ((bf16[16,192,256]{2,1,0:T(8,128)(2,1)}), bf16[16,192,256]{2,1,0:T(8,128)(2,1)}, u32[]{:S(2)}, u32[]{:S(2)}) async-start(bf16[16,192,256]{2,1,0:T(8,128)(2,1)} %get-tuple-element.45), calls=%async_computation.1 | async-start | bytes 3145728 | tf_op jit(solution)/shard_map/all_to_all | solution.py:490
  35.1 11.8 %collective-permute-done.2.refs_2_ = bf16[2,2,528,128]{3,2,1,0:T(8,128)(2,1)S(1)} collective-permute-done((bf16[2,2,528,128]{3,2,1,0:T(8,128)(2,1)S(1)}, bf16[2,2,528,128]{3,2,1,0:T(8,128)(2,1)S(1)}, u32[]{:S(2)}, u32[]{:S(2)}) %collective-permute-start.2) | collective-permute-done | bytes 540704 | tf_op jit(solution)/shard_map/ppermute | solution.py:470
  47.1 2.7 %collective-permute-start.4 = (bf16[2,1,528,128]{3,2,1,0:T(8,128)(2,1)S(1)}, bf16[2,1,528,128]{3,2,1,0:T(8,128)(2,1)}, u32[]{:S(2)}, u32[]{:S(2)}) collective-permute-start(bf16[2,1,528,128]{3,2,1,0:T(8,128)(2,1)S(1)} %slice.36), channel_id=1, source_target_pairs={{0,48},{16,0},{32,16},{48,32},{1,49},{17,1},{33,17},{49,33},{2,50}... | collective-permute-start | bytes 811016 | tf_op jit(solution)/shard_map/ppermute | solution.py:470
  51.2 3.8 %collective-permute-done.3.refs_3_ = bf16[2,1,528,128]{3,2,1,0:T(8,128)(2,1)S(1)} collective-permute-done((bf16[2,1,528,128]{3,2,1,0:T(8,128)(2,1)S(1)}, bf16[2,1,528,128]{3,2,1,0:T(8,128)(2,1)S(1)}, u32[]{:S(2)}, u32[]{:S(2)}) %collective-permute-start.3) | collective-permute-done | bytes 270368 | tf_op jit(solution)/shard_map/ppermute | solution.py:470
  55.0 1.8 all-to-all-done.1.rows_ref
  56.8 22.1 %shard_map.162 = (bf16[16,192,256]{2,1,0:T(8,128)(2,1)}, bf16[2,2,8,64,128]{4,3,2,1,0:T(8,128)(2,1)}, bf16[2,2,8,64,128]{4,3,2,1,0:T(8,128)(2,1)}, bf16[2,2,8,64...) custom-call(s32[16]{0:T(128)} %stack.76.base_ref, f32[1]{0:T(128)} %dynamic_slice.10.cross_ref, ...), custom_call_target="tpu_custom_call" | custom-call | flops 2415919104 | bytes 16777216 | tf_op jit(solution)/shard_map/pallas_call | solution.py:138
  78.9 5.4 %all-to-all-start.2 = ((bf16[16,192,256]{2,1,0:T(8,128)(2,1)}), bf16[16,192,256]{2,1,0:T(8,128)(2,1)}, u32[]{:S(2)}, u32[]{:S(2)}) async-start(bf16[16,192,256]{2,1,0:T(8,128)(2,1)} %get-tuple-element.47), calls=%async_computation.2 | async-start | bytes 3145728 | tf_op jit(solution)/shard_map/all_to_all | solution.py:490
  85.8 2.6 %collective-permute-start.9 = (bf16[2,2,8,64,128]{4,3,2,1,0:T(8,128)(2,1)}, bf16[2,2,8,64,128]{4,3,2,1,0:T(8,128)(2,1)}, u32[]{:S(2)}, u32[]{:S(2)}) collective-permute-start(bf16[2,2,8,64,128]{4,3,2,1,0:T(8,128)(2,1)} %get-tuple-element.56), channel_id=1, source_target_pairs={{0,32},{16,48},{32,0},{48,16},{1,33},{17,49},{33,1},{49,17},{2,34}... | collective-permute-start | bytes 1572872 | tf_op jit(solution)/shard_map/ppermute | solution.py:470
  89.4 16.3 %all-to-all-done.2.back_ref = bf16[16,192,256]{2,1,0:T(8,128)(2,1)} async-done(((bf16[16,192,256]{2,1,0:T(8,128)(2,1)}), bf16[16,192,256]{2,1,0:T(8,128)(2,1)}, u32[]{:S(2)}, u32[]{:S(2)}) %all-to-all-start.2) | async-done | bytes 1572896 | tf_op jit(solution)/shard_map/all_to_all | solution.py:490
  105.8 3.4 %shard_map.163 = (bf16[5,384,256]{2,1,0:T(8,128)(2,1)}, bf16[5,384,256]{2,1,0:T(8,128)(2,1)}) custom-call(s32[1]{0:T(128)} %bitcast.core_ref.place_ref, bf16[16,192,256]{2,1,0:T(8,128)(2,1)} %all-to-all-done.2.back_ref, f32[768,256]{1,0:T(8,128)} %get-tuple-element.48.gate_ref, f32[768,256]{1,0:T(8,128)} %get-tuple-element.49.grad_gated_ref), custom_call_target="tpu_custom_call" | custom-call | bytes 3145732 | tf_op jit(solution)/shard_map/pallas_call | solution.py:216
  109.1 4.4 %collective-permute-start.5 = (bf16[5,384,256]{2,1,0:T(8,128)(2,1)}, bf16[5,384,256]{2,1,0:T(8,128)(2,1)}, u32[]{:S(2)}, u32[]{:S(2)}) collective-permute-start(bf16[5,384,256]{2,1,0:T(8,128)(2,1)} %get-tuple-element.51.send_ref), channel_id=1, source_target_pairs={{0,8},{8,0},{1,9},{9,1},{2,10},{10,2},{3,11},{11,3},{4,12},{12,4},... | collective-permute-start | bytes 2949128 | tf_op jit(solution)/shard_map/ppermute | solution.py:486
  117.6 5.4 %all-to-all-start.4 = ((bf16[16,64,128]{2,1,0:T(8,128)(2,1)}), bf16[16,64,128]{2,1,0:T(8,128)(2,1)S(1)}, u32[]{:S(2)}, u32[]{:S(2)}) async-start(bf16[16,64,128]{2,1,0:T(8,128)(2,1)} %bitcast.27), calls=%async_computation.4 | async-start | bytes 524288 | tf_op jit(solution)/shard_map/all_to_all | solution.py:490
  123.9 5.8 %shard_map.164 = bf16[64,64,384]{2,1,0:T(8,128)(2,1)} custom-call(bf16[5,384,256]{2,1,0:T(8,128)(2,1)} %get-tuple-element.50.keep_ref, bf16[5,384,256]{2,1,0:T(8,128)(2,1)} %collective-permute-done.5.got_ref, bf16[256,768]{1,0:T(8,128)(2,1)} %get-tuple-element.52.own_normed_ref, bf16[256,768]{1,0:T(8,128)(2,1)} %copy-done.9, bf16[256,768]{1,0:T(8,128)(2,1)} %bitcast.58, ...), custom_call_target="tpu_custom_call" | custom-call | flops 1509949440 | bytes 3538944 | tf_op jit(solution)/shard_map/pallas_call | solution.py:216
  131.1 8.4 %all-to-all-start.3 = ((bf16[64,64,384]{2,1,0:T(8,128)(2,1)}), bf16[64,64,384]{2,1,0:T(8,128)(2,1)}, u32[]{:S(2)}, u32[]{:S(2)}) async-start(bf16[64,64,384]{2,1,0:T(8,128)(2,1)} %shard_map.164), calls=%async_computation.3 | async-start | bytes 6291456 | tf_op jit(solution)/shard_map/all_to_all | solution.py:490
  143.1 6.8 %shard_map.165 = (bf16[256,768]{1,0:T(8,128)(2,1)}, bf16[256,768]{1,0:T(8,128)(2,1)}, f32[8,384]{1,0:T(8,128)}) custom-call(s32[1]{0:T(128)} %bitcast.core_ref.place_ref, bf16[5,384,256]{2,1,0:T(8,128)(2,1)} %get-tuple-element.50.keep_ref, bf16[5,384,256]{2,1,0:T(8,128)(2,1)} %get-tuple-element.51.send_ref, bf16[256,768]{1,0:T(8,128)(2,1)} %bitcast.63, ...), custom_call_target="tpu_custom_call" | custom-call | flops 1509949440 | bytes 8663044 | tf_op jit(solution)/shard_map/pallas_call | solution.py:216
  151.7 22.3 %collective-permute-done.12 = f32[2560]{0:T(1024)S(1)} collective-permute-done((f32[2560]{0:T(1024)S(1)}, f32[2560]{0:T(1024)S(1)}, u32[]{:S(2)}, u32[]{:S(2)}) %collective-permute-start.12) | collective-permute-done | bytes 10272 | tf_op jit(solution)/shard_map/ppermute | solution.py:611
  174.7 2.5 all-to-all-done.3.parts_ref
  177.2 4.3 %shard_map.166 = bf16[64,72,384]{2,1,0:T(8,128)(2,1)} custom-call(bf16[64,64,384]{2,1,0:T(8,128)(2,1)} %all-to-all-done.3.parts_ref, f32[8,384]{1,0:T(8,128)} %reshape.77.small_ref), custom_call_target="tpu_custom_call" | custom-call | flops 1572864 | bytes 3158016 | tf_op jit(solution)/shard_map/pallas_call | solution.py:216
  181.5 8.3 %all-to-all-start.5 = ((bf16[64,72,384]{2,1,0:T(8,128)(2,1)}), bf16[64,72,384]{2,1,0:T(8,128)(2,1)S(1)}, u32[]{:S(2)}, u32[]{:S(2)}) async-start(bf16[64,72,384]{2,1,0:T(8,128)(2,1)} %shard_map.166), calls=%async_computation.5 | async-start | bytes 7077888 | tf_op jit(solution)/shard_map/all_to_all | solution.py:490
  189.8 1.7 convert_bitcast_fusion
  191.5 2.7 %copy.40 = bf16[128,64,128]{2,1,0:T(8,128)(2,1)} copy(bf16[128,64,128]{2,0,1:T(8,128)(2,1)S(1)} %convert_bitcast_fusion) | data formatting | bytes 4194304 | tf_op jit(solution)/shard_map/convert_element_type | solution.py:594
  194.2 36.5 %all-to-all-done.5.block_ref = bf16[64,72,384]{2,1,0:T(8,128)(2,1)S(1)} async-done(((bf16[64,72,384]{2,1,0:T(8,128)(2,1)}), bf16[64,72,384]{2,1,0:T(8,128)(2,1)S(1)}, u32[]{:S(2)}, u32[]{:S(2)}) %all-to-all-start.5) | async-done | bytes 3538976 | tf_op jit(solution)/shard_map/all_to_all | solution.py:490
  230.7 4.1 %collective-permute-start.13 = (bf16[64,72,384]{2,1,0:T(8,128)(2,1)S(1)}, bf16[64,72,384]{2,1,0:T(8,128)(2,1)}, u32[]{:S(2)}, u32[]{:S(2)}) collective-permute-start(bf16[64,72,384]{2,1,0:T(8,128)(2,1)S(1)} %all-to-all-done.5.block_ref), channel_id=1, source_target_pairs={{0,8},{8,0},{1,9},{9,1},{2,10},{10,2},{3,11},{11,3},{4,12},{12,4},... | collective-permute-start | bytes 10616840 | tf_op jit(solution)/shard_map/ppermute | solution.py:486
  235.7 1.8 shard_map.169.mine_ref
  238.1 3.9 %shard_map.167 = (f32[768,3072]{1,0:T(8,128)}, f32[2,384,768]{2,1,0:T(8,128)}) custom-call(s32[1]{0:T(128)} %bitcast.core_ref.place_ref, bf16[64,72,384]{2,1,0:T(8,128)(2,1)} %copy-done.2), custom_call_target="tpu_custom_call" | custom-call | bytes 10485760 | tf_op jit(solution)/shard_map/pallas_call | solution.py:386
  242.8 2.8 %shard_map.170 = (f32[200,1536]{1,0:T(8,128)}, f32[16,128]{1,0:T(8,128)}, f32[1,16]{1,0:T(1,128)}) custom-call(f32[8,2,8,384]{3,2,1,0:T(8,128)} %shard_map.169.mine_ref, f32[8,2,8,384]{3,2,1,0:T(8,128)} %copy-done.10), custom_call_target="tpu_custom_call" | custom-call | bytes 393216 | tf_op jit(solution)/shard_map/pallas_call | solution.py:216
  245.6 4.1 %shard_map.168 = (f32[768,3072]{1,0:T(8,128)}, f32[2,384,768]{2,1,0:T(8,128)}) custom-call(s32[1]{0:T(128)S(6)} %sub.21.place_ref, bf16[64,72,384]{2,1,0:T(8,128)(2,1)} %collective-permute-done.13.block_ref, f32[768,3072]{1,0:T(8,128)} %get-tuple-element.65.refs_0_, ...), custom_call_target="tpu_custom_call", output_to_operand_aliasing={{0}: (2, {}), {1}: (3, {})} | custom-call | bytes 10485760 | tf_op jit(solution)/shard_map/pallas_call | solution.py:386
  (94 shorter events, 25.3 us)
Async XLA Ops:
  0.7 12.9 %copy-start.15 = (s32[2]{0:T(128)S(1)}, s32[2]{0:T(128)}, u32[]{:S(2)}) copy-start(s32[2]{0:T(128)} %param.11) | copy-start | bytes 28
  0.7 12.9 %copy-start.5 = (bf16[200,1536]{1,0:T(8,128)(2,1)S(1)}, bf16[200,1536]{1,0:T(8,128)(2,1)}, u32[]{:S(2)}) copy-start(bf16[200,1536]{1,0:T(8,128)(2,1)} %param.12) | copy-start | bytes 1843204
  5.1 16.5 %all-to-all-start = ((bf16[16,80,128]{2,1,0:T(8,128)(2,1)}), bf16[16,80,128]{2,1,0:T(8,128)(2,1)S(1)}, u32[]{:S(2)}, u32[]{:S(2)}) async-start(bf16[16,80,128]{2,1,0:T(8,128)(2,1)} %copy.36), calls=%async_computation | async-start | bytes 655360 | tf_op jit(solution)/shard_map/all_to_all | solution.py:490
  14.4 7.2 %copy-start.14 = (s32[1024]{0:T(1024)S(1)}, s32[1024]{0:T(1024)}, u32[]{:S(2)}) copy-start(s32[1024]{0:T(1024)} %param.18) | copy-start | bytes 12292
  23.4 3.6 %collective-permute-start = (bf16[2,528,128]{2,1,0:T(8,128)(2,1)S(1)}, bf16[2,528,128]{2,1,0:T(8,128)(2,1)S(1)}, u32[]{:S(2)}, u32[]{:S(2)}) collective-permute-start(bf16[2,528,128]{2,1,0:T(8,128)(2,1)S(1)} %get-tuple-element.75), channel_id=1, source_target_pairs={{0,8},{8,0},{1,9},{9,1},{2,10},{10,2},{3,11},{11,3},{4,12},{12,4},... | collective-permute-start | bytes 811016 | tf_op jit(solution)/shard_map/ppermute | solution.py:486
  27.0 20.1 %copy-start.6 = (bf16[2,2,528,128]{3,2,1,0:T(8,128)(2,1)}, bf16[2,2,528,128]{3,2,1,0:T(8,128)(2,1)S(1)}, u32[]{:S(2)}) copy-start(bf16[2,2,528,128]{3,2,1,0:T(8,128)(2,1)S(1)} %pad_maximum_fusion.refs_0_) | copy-start | bytes 1622020
  27.1 22.8 %copy-start.17 = (f32[16]{0:T(128)S(1)}, f32[16]{0:T(128)}, u32[]{:S(2)}) copy-start(f32[16]{0:T(128)} %param.17) | copy-start | bytes 196
  27.1 29.7 %all-to-all-start.1 = ((bf16[16,192,256]{2,1,0:T(8,128)(2,1)}), bf16[16,192,256]{2,1,0:T(8,128)(2,1)}, u32[]{:S(2)}, u32[]{:S(2)}) async-start(bf16[16,192,256]{2,1,0:T(8,128)(2,1)} %get-tuple-element.45), calls=%async_computation.1 | async-start | bytes 3145728 | tf_op jit(solution)/shard_map/all_to_all | solution.py:490
  32.3 14.7 %collective-permute-start.2 = (bf16[2,2,528,128]{3,2,1,0:T(8,128)(2,1)S(1)}, bf16[2,2,528,128]{3,2,1,0:T(8,128)(2,1)S(1)}, u32[]{:S(2)}, u32[]{:S(2)}) collective-permute-start(bf16[2,2,528,128]{3,2,1,0:T(8,128)(2,1)S(1)} %pad_maximum_fusion.refs_0_), channel_id=1, source_target_pairs={{0,16},{16,32},{32,48},{48,0},{1,17},{17,33},{33,49},{49,1},{2,18}... | collective-permute-start | bytes 1622024 | tf_op jit(solution)/shard_map/ppermute | solution.py:470
  33.6 13.4 %collective-permute-start.1 = (bf16[2,2,528,128]{3,2,1,0:T(8,128)(2,1)S(1)}, bf16[2,2,528,128]{3,2,1,0:T(8,128)(2,1)S(1)}, u32[]{:S(2)}, u32[]{:S(2)}) collective-permute-start(bf16[2,2,528,128]{3,2,1,0:T(8,128)(2,1)S(1)} %pad_maximum_fusion.refs_0_), channel_id=1, source_target_pairs={{0,48},{16,0},{32,16},{48,32},{1,49},{17,1},{33,17},{49,33},{2,50}... | collective-permute-start | bytes 1622024 | tf_op jit(solution)/shard_map/ppermute | solution.py:470
  47.0 8.0 %collective-permute-start.3 = (bf16[2,1,528,128]{3,2,1,0:T(8,128)(2,1)S(1)}, bf16[2,1,528,128]{3,2,1,0:T(8,128)(2,1)S(1)}, u32[]{:S(2)}, u32[]{:S(2)}) collective-permute-start(bf16[2,1,528,128]{3,2,1,0:T(8,128)(2,1)S(1)} %slice.35), channel_id=1, source_target_pairs={{0,16},{16,32},{32,48},{48,0},{1,17},{17,33},{33,49},{49,1},{2,18}... | collective-permute-start | bytes 811016 | tf_op jit(solution)/shard_map/ppermute | solution.py:470
  47.1 7.9 %collective-permute-start.4 = (bf16[2,1,528,128]{3,2,1,0:T(8,128)(2,1)S(1)}, bf16[2,1,528,128]{3,2,1,0:T(8,128)(2,1)}, u32[]{:S(2)}, u32[]{:S(2)}) collective-permute-start(bf16[2,1,528,128]{3,2,1,0:T(8,128)(2,1)S(1)} %slice.36), channel_id=1, source_target_pairs={{0,48},{16,0},{32,16},{48,32},{1,49},{17,1},{33,17},{49,33},{2,50}... | collective-permute-start | bytes 811016 | tf_op jit(solution)/shard_map/ppermute | solution.py:470
  78.9 26.9 %all-to-all-start.2 = ((bf16[16,192,256]{2,1,0:T(8,128)(2,1)}), bf16[16,192,256]{2,1,0:T(8,128)(2,1)}, u32[]{:S(2)}, u32[]{:S(2)}) async-start(bf16[16,192,256]{2,1,0:T(8,128)(2,1)} %get-tuple-element.47), calls=%async_computation.2 | async-start | bytes 3145728 | tf_op jit(solution)/shard_map/all_to_all | solution.py:490
  84.3 29.2 %copy-start.7 = (bf16[2,2,8,64,128]{4,3,2,1,0:T(8,128)(2,1)S(1)}, bf16[2,2,8,64,128]{4,3,2,1,0:T(8,128)(2,1)}, u32[]{:S(2)}) copy-start(bf16[2,2,8,64,128]{4,3,2,1,0:T(8,128)(2,1)} %get-tuple-element.54) | copy-start | bytes 1572868
  84.4 29.2 %collective-permute-start.8 = (bf16[2,2,8,64,128]{4,3,2,1,0:T(8,128)(2,1)}, bf16[2,2,8,64,128]{4,3,2,1,0:T(8,128)(2,1)S(1)}, u32[]{:S(2)}, u32[]{:S(2)}) collective-permute-start(bf16[2,2,8,64,128]{4,3,2,1,0:T(8,128)(2,1)} %get-tuple-element.55), channel_id=1, source_target_pairs={{0,16},{16,32},{32,48},{48,0},{1,17},{17,33},{33,49},{49,1},{2,18}... | collective-permute-start | bytes 1572872 | tf_op jit(solution)/shard_map/ppermute | solution.py:470
  85.8 27.8 %collective-permute-start.9 = (bf16[2,2,8,64,128]{4,3,2,1,0:T(8,128)(2,1)}, bf16[2,2,8,64,128]{4,3,2,1,0:T(8,128)(2,1)}, u32[]{:S(2)}, u32[]{:S(2)}) collective-permute-start(bf16[2,2,8,64,128]{4,3,2,1,0:T(8,128)(2,1)} %get-tuple-element.56), channel_id=1, source_target_pairs={{0,32},{16,48},{32,0},{48,16},{1,33},{17,49},{33,1},{49,17},{2,34}... | collective-permute-start | bytes 1572872 | tf_op jit(solution)/shard_map/ppermute | solution.py:470
  88.4 25.2 %collective-permute-start.10 = (bf16[2,2,8,64,128]{4,3,2,1,0:T(8,128)(2,1)}, bf16[2,2,8,64,128]{4,3,2,1,0:T(8,128)(2,1)}, u32[]{:S(2)}, u32[]{:S(2)}) collective-permute-start(bf16[2,2,8,64,128]{4,3,2,1,0:T(8,128)(2,1)} %get-tuple-element.57), channel_id=1, source_target_pairs={{0,48},{16,0},{32,16},{48,32},{1,49},{17,1},{33,17},{49,33},{2,50}... | collective-permute-start | bytes 1572872 | tf_op jit(solution)/shard_map/ppermute | solution.py:470
  109.1 6.2 %copy-start.3 = (bf16[2,128,768]{2,1,0:T(8,128)(2,1)S(1)}, bf16[2,128,768]{2,1,0:T(8,128)(2,1)}, u32[]{:S(2)}) copy-start(bf16[2,128,768]{2,1,0:T(8,128)(2,1)} %param.19) | copy-start | bytes 1179652
  109.1 13.9 %collective-permute-start.5 = (bf16[5,384,256]{2,1,0:T(8,128)(2,1)}, bf16[5,384,256]{2,1,0:T(8,128)(2,1)}, u32[]{:S(2)}, u32[]{:S(2)}) collective-permute-start(bf16[5,384,256]{2,1,0:T(8,128)(2,1)} %get-tuple-element.51.send_ref), channel_id=1, source_target_pairs={{0,8},{8,0},{1,9},{9,1},{2,10},{10,2},{3,11},{11,3},{4,12},{12,4},... | collective-permute-start | bytes 2949128 | tf_op jit(solution)/shard_map/ppermute | solution.py:486
  115.2 1.6 collective-permute-start.11
  115.3 7.7 %collective-permute-start.7 = (bf16[256,768]{1,0:T(8,128)(2,1)S(1)}, bf16[256,768]{1,0:T(8,128)(2,1)S(1)}, u32[]{:S(2)}, u32[]{:S(2)}) collective-permute-start(bf16[256,768]{1,0:T(8,128)(2,1)S(1)} %bitcast.60), channel_id=1, source_target_pairs={{0,8},{8,0},{1,9},{9,1},{2,10},{10,2},{3,11},{11,3},{4,12},{12,4},... | collective-permute-start | bytes 1179656 | tf_op jit(solution)/shard_map/ppermute | solution.py:486
  115.8 7.3 %collective-permute-start.6 = (bf16[256,768]{1,0:T(8,128)(2,1)}, bf16[256,768]{1,0:T(8,128)(2,1)S(1)}, u32[]{:S(2)}, u32[]{:S(2)}) collective-permute-start(bf16[256,768]{1,0:T(8,128)(2,1)} %get-tuple-element.52.own_normed_ref), channel_id=1, source_target_pairs={{0,8},{8,0},{1,9},{9,1},{2,10},{10,2},{3,11},{11,3},{4,12},{12,4},... | collective-permute-start | bytes 1179656 | tf_op jit(solution)/shard_map/ppermute | solution.py:486
  117.6 13.5 %all-to-all-start.4 = ((bf16[16,64,128]{2,1,0:T(8,128)(2,1)}), bf16[16,64,128]{2,1,0:T(8,128)(2,1)S(1)}, u32[]{:S(2)}, u32[]{:S(2)}) async-start(bf16[16,64,128]{2,1,0:T(8,128)(2,1)} %bitcast.27), calls=%async_computation.4 | async-start | bytes 524288 | tf_op jit(solution)/shard_map/all_to_all | solution.py:490
  131.0 18.8 %copy-start.4 = (bf16[16,64,128]{2,1,0:T(8,128)(2,1)}, bf16[16,64,128]{2,1,0:T(8,128)(2,1)S(1)}, u32[]{:S(2)}) copy-start(bf16[16,64,128]{2,1,0:T(8,128)(2,1)S(1)} %all-to-all-done.4) | copy-start | bytes 786436
  131.1 46.1 %all-to-all-start.3 = ((bf16[64,64,384]{2,1,0:T(8,128)(2,1)}), bf16[64,64,384]{2,1,0:T(8,128)(2,1)}, u32[]{:S(2)}, u32[]{:S(2)}) async-start(bf16[64,64,384]{2,1,0:T(8,128)(2,1)} %shard_map.164), calls=%async_computation.3 | async-start | bytes 6291456 | tf_op jit(solution)/shard_map/all_to_all | solution.py:490
  150.7 23.4 %collective-permute-start.12 = (f32[2560]{0:T(1024)S(1)}, f32[2560]{0:T(1024)S(1)}, u32[]{:S(2)}, u32[]{:S(2)}) collective-permute-start(f32[2560]{0:T(1024)S(1)} %get-tuple-element.72), channel_id=1, source_target_pairs={{0,2},{2,0},{4,6},{6,4},{1,3},{3,1},{5,7},{7,5},{8,10},{10,8},{12,... | collective-permute-start | bytes 30728 | tf_op jit(solution)/shard_map/ppermute | solution.py:611
  181.5 8.3 %copy-start.13 = (bf16[128,16]{0,1:T(8,128)(2,1)S(1)}, bf16[128,16]{0,1:T(8,128)(2,1)}, u32[]{:S(2)}) copy-start(bf16[128,16]{0,1:T(8,128)(2,1)} %param.16) | copy-start | bytes 12292
  181.5 49.2 %all-to-all-start.5 = ((bf16[64,72,384]{2,1,0:T(8,128)(2,1)}), bf16[64,72,384]{2,1,0:T(8,128)(2,1)S(1)}, u32[]{:S(2)}, u32[]{:S(2)}) async-start(bf16[64,72,384]{2,1,0:T(8,128)(2,1)} %shard_map.166), calls=%async_computation.5 | async-start | bytes 7077888 | tf_op jit(solution)/shard_map/all_to_all | solution.py:490
  230.7 7.4 %copy-start.2 = (bf16[64,72,384]{2,1,0:T(8,128)(2,1)}, bf16[64,72,384]{2,1,0:T(8,128)(2,1)S(1)}, u32[]{:S(2)}) copy-start(bf16[64,72,384]{2,1,0:T(8,128)(2,1)S(1)} %all-to-all-done.5.block_ref) | copy-start | bytes 10616836
  230.7 14.9 %collective-permute-start.13 = (bf16[64,72,384]{2,1,0:T(8,128)(2,1)S(1)}, bf16[64,72,384]{2,1,0:T(8,128)(2,1)}, u32[]{:S(2)}, u32[]{:S(2)}) collective-permute-start(bf16[64,72,384]{2,1,0:T(8,128)(2,1)S(1)} %all-to-all-done.5.block_ref), channel_id=1, source_target_pairs={{0,8},{8,0},{1,9},{9,1},{2,10},{10,2},{3,11},{11,3},{4,12},{12,4},... | collective-permute-start | bytes 10616840 | tf_op jit(solution)/shard_map/ppermute | solution.py:486
  237.6 4.5 %collective-permute-start.14 = (f32[8,2,8,384]{3,2,1,0:T(8,128)}, f32[8,2,8,384]{3,2,1,0:T(8,128)S(1)}, u32[]{:S(2)}, u32[]{:S(2)}) collective-permute-start(f32[8,2,8,384]{3,2,1,0:T(8,128)} %shard_map.169.mine_ref), channel_id=1, source_target_pairs={{0,8},{8,0},{1,9},{9,1},{2,10},{10,2},{3,11},{11,3},{4,12},{12,4},... | collective-permute-start | bytes 589832 | tf_op jit(solution)/shard_map/ppermute | solution.py:486
  245.6 4.1 %copy-start.1 = (bf16[128,64,128]{2,1,0:T(8,128)(2,1)S(1)}, bf16[128,64,128]{2,1,0:T(8,128)(2,1)}, u32[]{:S(2)}) copy-start(bf16[128,64,128]{2,1,0:T(8,128)(2,1)} %param.15) | copy-start | bytes 6291460
  (7 other events, 11.3 us)

commit v7 on v6

--- a/solution.py
+++ b/solution.py
@@ -318,25 +318,68 @@
                 table_ref[row : row + 1, :] = total[:, k * half : (k + 1) * half]
 
 
-def weights_kernel(keep_ref, got_ref, own_normed_ref, other_normed_ref, own_cots_ref, other_cots_ref, payload_ref):
+def weights_kernel(
+    keep_ref,
+    got_ref,
+    own_normed_ref,
+    other_normed_ref,
+    own_cots_ref,
+    other_cots_ref,
+    payload_ref,
+    stage,
+    stage_out,
+    sems,
+):
     width = own_normed_ref.shape[1]
     half = width // 2
-    depth = 48
+    groups, depth = stage.shape[1:3]
+    gated = jnp.concatenate([keep_ref[0], got_ref[0]], axis=1)
+    cots = jnp.concatenate([own_cots_ref[...], other_cots_ref[...]], axis=0)
+    out_grad = dot(gated, cots, ((1,), (0,))).astype(bf16)
+    for d in range(4 * groups):
+        if d < half // 8:
+            block = out_grad[16 * (d // 2) : 16 * (d // 2 + 1), half * (d % 2) : half * (d % 2 + 1)]
+        else:
+            block = jnp.zeros((16, half), bf16)
+        stage_out[d // 4, d % 4] = block
+    copies = [pltpu.make_async_copy(stage_out, payload_ref.at[:, :, depth:, :], sems.at[4])]
+    copies[0].start()
     normed_t = jnp.concatenate([own_normed_ref[...], other_normed_ref[...]], axis=0).T
     for index in range(4):
         grad = jnp.concatenate([keep_ref[index + 1], got_ref[index + 1]], axis=1).T
         weight_grad = dot(normed_t, grad, ((1,), (0,))).astype(bf16)
-        for a in range(width // depth):
-            payload_ref[4 * a + index, :depth, :] = weight_grad[depth * a : depth * (a + 1)]
-    gated = jnp.concatenate([keep_ref[0], got_ref[0]], axis=1)
-    cots = jnp.concatenate([own_cots_ref[...], other_cots_ref[...]], axis=0)
-    out_grad = dot(gated, cots, ((1,), (0,))).astype(bf16)
-    for d in range(payload_ref.shape[0]):
-        if d < half // 8:
-            block = out_grad[16 * (d // 2) : 16 * (d // 2 + 1), half * (d % 2) : half * (d % 2 + 1)]
-        else:
-            block = jnp.zeros((16, half), bf16)
-        payload_ref[d, depth:, :] = block
+        for a in range(groups):
+            stage[index, a] = weight_grad[depth * a : depth * (a + 1)]
+        copy = pltpu.make_async_copy(
+            stage.at[index], payload_ref.at[:, index, :depth, :], sems.at[index]
+        )
+        copy.start()
+        copies.append(copy)
+    for copy in copies:
+        copy.wait()
+
+
+def weight_payload(*operands):
+    rows, width = operands[2].shape
+    half = width // 2
+    vmem = pl.BlockSpec(memory_space=pltpu.VMEM)
+    return pl.pallas_call(
+        weights_kernel,
+        in_specs=[vmem] * len(operands),
+        out_specs=pl.BlockSpec(memory_space=pl.ANY),
+        out_shape=jax.ShapeDtypeStruct((16, 4, 64, half), bf16),
+        scratch_shapes=[
+            pltpu.VMEM((4, 16, 48, half), bf16),
+            pltpu.VMEM((16, 4, 16, half), bf16),
+            pltpu.SemaphoreType.DMA((5,)),
+        ],
+        compiler_params=pltpu.CompilerParams(vmem_limit_bytes=vmem_bytes),
+        cost_estimate=pl.CostEstimate(
+            flops=10 * rows * width * width,
+            bytes_accessed=8 * 1024 * 1024,
+            transcendentals=0,
+        ),
+    )(*operands)
 
 
 def assemble_kernel(place_ref, block_ref, *refs):
@@ -535,9 +578,7 @@
     count = chains.shape[0]
     chain_col = jnp.broadcast_to(chains[:, None], (count, 128))
     chain_row = jnp.broadcast_to(chains[None, :], (8, count))
-    sent, bias_got, chain_col, chain_row = lax.optimization_barrier(
-        (sent, bias_got, chain_col, chain_row)
-    )
+    sent, bias_got = lax.optimization_barrier((sent, bias_got))
     bias_own = jnp.concatenate(
         [
             bias_got[:, :col_count].reshape(2, blocks * col_count, row_count),
@@ -549,6 +590,7 @@
     near = jnp.stack([bias_own, swap(bias_own)])
     sent, near = lax.optimization_barrier((sent, near))
     biases = spread_bias(near)
+    biases[3], chain_col, chain_row = lax.optimization_barrier((biases[3], chain_col, chain_row))
     head_rows = exchange(sent, head_axes)
     y_at = lax.axis_index("y")
     base = jnp.stack(
@@ -580,12 +622,8 @@
     )
     updated = updated.reshape(activations.shape)
     grad_tokens = grad_tokens.reshape(activations.shape)
-    (payload,) = in_vmem(
-        weights_kernel,
-        [((chip_count, 64, half), bf16)],
-        (keep, got, normed, other_normed, cots, other_cots),
-        10 * acts.size * width,
-    )
+    payload = weight_payload(keep, got, normed, other_normed, cots, other_cots)
+    payload = payload.reshape(chip_count, -1, half)
 
     bias_sum = sum_bias(*grad_biases).astype(bf16)
     grad_bias_half = exchange(bias_sum.reshape(heads, col_count, row_count), head_axes)

time: 251 us -> 248 us (0.988)
    pallas_call x7 -> x6, Pallas kernels: 31.5 us -> 25.7 us  [in_vmem(): pl.pallas_call(kernel, in_specs=scalars + [vmem] * (len(operands) - smem)...]
    pallas_call x0 -> x1, Pallas kernels: none -> 4.9 us  [weight_payload(): pl.pallas_call(weights_kernel, in_specs=[vmem] * len(operands), out_specs...]
  transfers between devices with their start and end apart: 21 -> 21, of which waited for: 11 -> 11; matrix products, arithmetic and copies ran while one was open for 5% -> 6% of each run, Pallas kernels for 12% -> 12%
where the time goes in v7:
time: 248 us; the launch traced here: 247 us
  waiting for transfers between devices  96.7 us (39%)
  starting transfers between devices  65.8 us (27%)
  Pallas kernels  60.8 us (25%)
  local copies, waits for them, and re-layouts  11.8 us (5%)
  matrix products  4.9 us (2%)
  other arithmetic  4.83 us (2%)
  between operations  2.56 us (1%)
    all_to_all x6, waiting for transfers between devices, exchange(): return lax.all_to_all(array, axes, 0, 0, tiled=True)  56.7 us
    all_to_all x6, starting transfers between devices, exchange(): return lax.all_to_all(array, axes, 0, 0, tiled=True)  41.4 us
    pallas_call x6, Pallas kernels, in_vmem(): pl.pallas_call(kernel, in_specs=scalars + [vmem] * (len(operands) - smem)...  25.7 us
    ppermute x1, waiting for transfers between devices, shards(): lax.ppermute(pick(1 - odd), 'x', [(i, i ^ 1) for i in range(4)])  22.3 us
    pallas_call x1, Pallas kernels, attend(): pl.pallas_call(functools.partial(attend_kernel, factor, part), grid=(samp...  22.2 us
    ppermute x7, waiting for transfers between devices, ring(): return lax.ppermute(array, 'y', [(i, (i + shift) % 4) for i in range(4)])  15.6 us
    ppermute x7, starting transfers between devices, swap(): return lax.ppermute(array, 'core', [(0, 1), (1, 0)])  12.8 us
    ppermute x7, starting transfers between devices, ring(): return lax.ppermute(array, 'y', [(i, (i + shift) % 4) for i in range(4)])  10.5 us
  transfers between devices with their start and end apart: 21, of which 11 were waited for; matrix products, arithmetic and copies ran while one was open for 6% of the time, Pallas kernels for 12%

profile of v7, /device:TPU:1, one launch (start us, length us, event | category | flops | bytes accessed | tf_op | source)
XLA Modules:
  0.0 247.4 jit_solution(470298118161108480)
XLA Ops:
  0.7 1.6 copy-done
  2.2 1.9 fusion.16
  5.1 8.4 %all-to-all-start = ((bf16[16,80,128]{2,1,0:T(8,128)(2,1)}), bf16[16,80,128]{2,1,0:T(8,128)(2,1)S(1)}, u32[]{:S(2)}, u32[]{:S(2)}) async-start(bf16[16,80,128]{2,1,0:T(8,128)(2,1)} %copy.36), calls=%async_computation | async-start | bytes 655360 | tf_op jit(solution)/shard_map/all_to_all | solution.py:533
  14.4 6.6 %shard_map.161 = (bf16[16,192,256]{2,1,0:T(8,128)(2,1)}, f32[768,256]{1,0:T(8,128)}, f32[768,256]{1,0:T(8,128)}, bf16[256,768]{1,0:T(8,128)(2,1)}) custom-call(bf16[256,768]{1,0:T(8,128)(2,1)} %bitcast.64, bf16[256,768]{1,0:T(8,128)(2,1)} %bitcast.59, f32[2,1536]{1,0:T(2,128)} %fusion.11.mod_ref, bf16[768,3072]{1,0:T(8,128)(2,1)} %weight_ref.3, ...), custom_call_target="tpu_custom_call" | custom-call | flops 1509949440 | bytes 6696960 | tf_op jit(solution)/shard_map/pallas_call | solution.py:216
  21.8 2.4 collective-permute-start
  25.5 5.2 %all-to-all-start.1 = ((bf16[16,192,256]{2,1,0:T(8,128)(2,1)}), bf16[16,192,256]{2,1,0:T(8,128)(2,1)}, u32[]{:S(2)}, u32[]{:S(2)}) async-start(bf16[16,192,256]{2,1,0:T(8,128)(2,1)} %get-tuple-element.47), calls=%async_computation.1 | async-start | bytes 3145728 | tf_op jit(solution)/shard_map/all_to_all | solution.py:533
  33.5 11.8 %collective-permute-done.1.refs_2_ = bf16[2,2,528,128]{3,2,1,0:T(8,128)(2,1)S(1)} collective-permute-done((bf16[2,2,528,128]{3,2,1,0:T(8,128)(2,1)S(1)}, bf16[2,2,528,128]{3,2,1,0:T(8,128)(2,1)S(1)}, u32[]{:S(2)}, u32[]{:S(2)}) %collective-permute-start.1) | collective-permute-done | bytes 540704 | tf_op jit(solution)/shard_map/ppermute | solution.py:513
  45.5 2.7 %collective-permute-start.4 = (bf16[2,1,528,128]{3,2,1,0:T(8,128)(2,1)S(1)}, bf16[2,1,528,128]{3,2,1,0:T(8,128)(2,1)}, u32[]{:S(2)}, u32[]{:S(2)}) collective-permute-start(bf16[2,1,528,128]{3,2,1,0:T(8,128)(2,1)S(1)} %slice.36), channel_id=1, source_target_pairs={{0,48},{16,0},{32,16},{48,32},{1,49},{17,1},{33,17},{49,33},{2,50}... | collective-permute-start | bytes 811016 | tf_op jit(solution)/shard_map/ppermute | solution.py:513
  49.5 3.8 %collective-permute-done.2.refs_3_ = bf16[2,1,528,128]{3,2,1,0:T(8,128)(2,1)S(1)} collective-permute-done((bf16[2,1,528,128]{3,2,1,0:T(8,128)(2,1)S(1)}, bf16[2,1,528,128]{3,2,1,0:T(8,128)(2,1)S(1)}, u32[]{:S(2)}, u32[]{:S(2)}) %collective-permute-start.2) | collective-permute-done | bytes 270368 | tf_op jit(solution)/shard_map/ppermute | solution.py:513
  55.2 22.2 %shard_map.162 = (bf16[16,192,256]{2,1,0:T(8,128)(2,1)}, bf16[2,2,8,64,128]{4,3,2,1,0:T(8,128)(2,1)}, bf16[2,2,8,64,128]{4,3,2,1,0:T(8,128)(2,1)}, bf16[2,2,8,64...) custom-call(s32[16]{0:T(128)} %stack.76.base_ref, f32[1]{0:T(128)} %dynamic_slice.10.cross_ref, ...), custom_call_target="tpu_custom_call" | custom-call | flops 2415919104 | bytes 16777216 | tf_op jit(solution)/shard_map/pallas_call | solution.py:138
  77.3 5.7 %all-to-all-start.2 = ((bf16[16,192,256]{2,1,0:T(8,128)(2,1)}), bf16[16,192,256]{2,1,0:T(8,128)(2,1)}, u32[]{:S(2)}, u32[]{:S(2)}) async-start(bf16[16,192,256]{2,1,0:T(8,128)(2,1)} %get-tuple-element.49), calls=%async_computation.2 | async-start | bytes 3145728 | tf_op jit(solution)/shard_map/all_to_all | solution.py:533
  84.2 2.6 %collective-permute-start.9 = (bf16[2,2,8,64,128]{4,3,2,1,0:T(8,128)(2,1)}, bf16[2,2,8,64,128]{4,3,2,1,0:T(8,128)(2,1)}, u32[]{:S(2)}, u32[]{:S(2)}) collective-permute-start(bf16[2,2,8,64,128]{4,3,2,1,0:T(8,128)(2,1)} %get-tuple-element.58), channel_id=1, source_target_pairs={{0,32},{16,48},{32,0},{48,16},{1,33},{17,49},{33,1},{49,17},{2,34}... | collective-permute-start | bytes 1572872 | tf_op jit(solution)/shard_map/ppermute | solution.py:513
  87.8 14.9 %all-to-all-done.2.back_ref = bf16[16,192,256]{2,1,0:T(8,128)(2,1)} async-done(((bf16[16,192,256]{2,1,0:T(8,128)(2,1)}), bf16[16,192,256]{2,1,0:T(8,128)(2,1)}, u32[]{:S(2)}, u32[]{:S(2)}) %all-to-all-start.2) | async-done | bytes 1572896 | tf_op jit(solution)/shard_map/all_to_all | solution.py:533
  102.7 3.4 %shard_map.163 = (bf16[5,384,256]{2,1,0:T(8,128)(2,1)}, bf16[5,384,256]{2,1,0:T(8,128)(2,1)}) custom-call(s32[1]{0:T(128)} %bitcast.core_ref.place_ref, bf16[16,192,256]{2,1,0:T(8,128)(2,1)} %all-to-all-done.2.back_ref, f32[768,256]{1,0:T(8,128)} %get-tuple-element.50.gate_ref, f32[768,256]{1,0:T(8,128)} %get-tuple-element.51.grad_gated_ref), custom_call_target="tpu_custom_call" | custom-call | bytes 3145732 | tf_op jit(solution)/shard_map/pallas_call | solution.py:216
  106.1 5.0 %collective-permute-start.5 = (bf16[5,384,256]{2,1,0:T(8,128)(2,1)}, bf16[5,384,256]{2,1,0:T(8,128)(2,1)}, u32[]{:S(2)}, u32[]{:S(2)}) collective-permute-start(bf16[5,384,256]{2,1,0:T(8,128)(2,1)} %get-tuple-element.53.send_ref), channel_id=1, source_target_pairs={{0,8},{8,0},{1,9},{9,1},{2,10},{10,2},{3,11},{11,3},{4,12},{12,4},... | collective-permute-start | bytes 2949128 | tf_op jit(solution)/shard_map/ppermute | solution.py:529
  115.1 6.3 %all-to-all-start.4 = ((bf16[16,64,128]{2,1,0:T(8,128)(2,1)}), bf16[16,64,128]{2,1,0:T(8,128)(2,1)S(1)}, u32[]{:S(2)}, u32[]{:S(2)}) async-start(bf16[16,64,128]{2,1,0:T(8,128)(2,1)} %bitcast.28), calls=%async_computation.4 | async-start | bytes 524288 | tf_op jit(solution)/shard_map/all_to_all | solution.py:533
  122.3 4.9 %shard_map.164 = bf16[16,4,64,384]{3,2,1,0:T(8,128)(2,1)} custom-call(bf16[5,384,256]{2,1,0:T(8,128)(2,1)} %get-tuple-element.52.keep_ref, bf16[5,384,256]{2,1,0:T(8,128)(2,1)} %collective-permute-done.5.got_ref, bf16[256,768]{1,0:T(8,128)(2,1)} %get-tuple-element.54.own_normed_ref, bf16[256,768]{1,0:T(8,128)(2,1)} %copy-done.9, bf16[256,768]{1,0:T(8,128)(2,1)} %bitcast.60, ...), custom_call_target="tpu_custom_call" | custom-call | flops 1509949440 | bytes 8388608 | tf_op jit(solution)/shard_map/pallas_call | solution.py:366
  127.2 2.2 all-to-all-done.4
  129.4 7.6 %all-to-all-start.3 = ((bf16[64,64,384]{2,1,0:T(8,128)(2,1)}), bf16[64,64,384]{2,1,0:T(8,128)(2,1)}, u32[]{:S(2)}, u32[]{:S(2)}) async-start(bf16[64,64,384]{2,1,0:T(8,128)(2,1)} %bitcast.58), calls=%async_computation.3 | async-start | bytes 6291456 | tf_op jit(solution)/shard_map/all_to_all | solution.py:533
  140.7 6.8 %shard_map.165 = (bf16[256,768]{1,0:T(8,128)(2,1)}, bf16[256,768]{1,0:T(8,128)(2,1)}, f32[8,384]{1,0:T(8,128)}) custom-call(s32[1]{0:T(128)} %bitcast.core_ref.place_ref, bf16[5,384,256]{2,1,0:T(8,128)(2,1)} %get-tuple-element.52.keep_ref, bf16[5,384,256]{2,1,0:T(8,128)(2,1)} %get-tuple-element.53.send_ref, bf16[256,768]{1,0:T(8,128)(2,1)} %bitcast.65, ...), custom_call_target="tpu_custom_call" | custom-call | flops 1509949440 | bytes 8663044 | tf_op jit(solution)/shard_map/pallas_call | solution.py:216
  149.3 22.3 %collective-permute-done.12 = f32[2560]{0:T(1024)S(1)} collective-permute-done((f32[2560]{0:T(1024)S(1)}, f32[2560]{0:T(1024)S(1)}, u32[]{:S(2)}, u32[]{:S(2)}) %collective-permute-start.12) | collective-permute-done | bytes 10272 | tf_op jit(solution)/shard_map/ppermute | solution.py:649
  172.3 2.5 all-to-all-done.3.parts_ref
  174.8 4.3 %shard_map.166 = bf16[64,72,384]{2,1,0:T(8,128)(2,1)} custom-call(bf16[64,64,384]{2,1,0:T(8,128)(2,1)} %all-to-all-done.3.parts_ref, f32[8,384]{1,0:T(8,128)} %reshape.81.small_ref), custom_call_target="tpu_custom_call" | custom-call | flops 1572864 | bytes 3158016 | tf_op jit(solution)/shard_map/pallas_call | solution.py:216
  179.1 8.3 %all-to-all-start.5 = ((bf16[64,72,384]{2,1,0:T(8,128)(2,1)}), bf16[64,72,384]{2,1,0:T(8,128)(2,1)S(1)}, u32[]{:S(2)}, u32[]{:S(2)}) async-start(bf16[64,72,384]{2,1,0:T(8,128)(2,1)} %shard_map.166), calls=%async_computation.5 | async-start | bytes 7077888 | tf_op jit(solution)/shard_map/all_to_all | solution.py:533
  187.4 1.7 convert_bitcast_fusion
  189.1 2.7 %copy.40 = bf16[128,64,128]{2,1,0:T(8,128)(2,1)} copy(bf16[128,64,128]{2,0,1:T(8,128)(2,1)S(1)} %convert_bitcast_fusion) | data formatting | bytes 4194304 | tf_op jit(solution)/shard_map/convert_element_type | solution.py:632
  191.8 36.5 %all-to-all-done.5.block_ref = bf16[64,72,384]{2,1,0:T(8,128)(2,1)S(1)} async-done(((bf16[64,72,384]{2,1,0:T(8,128)(2,1)}), bf16[64,72,384]{2,1,0:T(8,128)(2,1)S(1)}, u32[]{:S(2)}, u32[]{:S(2)}) %all-to-all-start.5) | async-done | bytes 3538976 | tf_op jit(solution)/shard_map/all_to_all | solution.py:533
  228.3 4.1 %collective-permute-start.13 = (bf16[64,72,384]{2,1,0:T(8,128)(2,1)S(1)}, bf16[64,72,384]{2,1,0:T(8,128)(2,1)}, u32[]{:S(2)}, u32[]{:S(2)}) collective-permute-start(bf16[64,72,384]{2,1,0:T(8,128)(2,1)S(1)} %all-to-all-done.5.block_ref), channel_id=1, source_target_pairs={{0,8},{8,0},{1,9},{9,1},{2,10},{10,2},{3,11},{11,3},{4,12},{12,4},... | collective-permute-start | bytes 10616840 | tf_op jit(solution)/shard_map/ppermute | solution.py:529
  233.3 1.8 shard_map.169.mine_ref
  235.7 3.9 %shard_map.167 = (f32[768,3072]{1,0:T(8,128)}, f32[2,384,768]{2,1,0:T(8,128)}) custom-call(s32[1]{0:T(128)} %bitcast.core_ref.place_ref, bf16[64,72,384]{2,1,0:T(8,128)(2,1)} %copy-done.2), custom_call_target="tpu_custom_call" | custom-call | bytes 10485760 | tf_op jit(solution)/shard_map/pallas_call | solution.py:429
  240.3 2.8 %shard_map.170 = (f32[200,1536]{1,0:T(8,128)}, f32[16,128]{1,0:T(8,128)}, f32[1,16]{1,0:T(1,128)}) custom-call(f32[8,2,8,384]{3,2,1,0:T(8,128)} %shard_map.169.mine_ref, f32[8,2,8,384]{3,2,1,0:T(8,128)} %copy-done.10), custom_call_target="tpu_custom_call" | custom-call | bytes 393216 | tf_op jit(solution)/shard_map/pallas_call | solution.py:216
  243.1 4.1 %shard_map.168 = (f32[768,3072]{1,0:T(8,128)}, f32[2,384,768]{2,1,0:T(8,128)}) custom-call(s32[1]{0:T(128)S(6)} %sub.21.place_ref, bf16[64,72,384]{2,1,0:T(8,128)(2,1)} %collective-permute-done.13.block_ref, f32[768,3072]{1,0:T(8,128)} %get-tuple-element.67.refs_0_, ...), custom_call_target="tpu_custom_call", output_to_operand_aliasing={{0}: (2, {}), {1}: (3, {})} | custom-call | bytes 10485760 | tf_op jit(solution)/shard_map/pallas_call | solution.py:429
  (94 shorter events, 23.9 us)
Async XLA Ops:
  0.7 12.9 %copy-start.15 = (s32[2]{0:T(128)S(1)}, s32[2]{0:T(128)}, u32[]{:S(2)}) copy-start(s32[2]{0:T(128)} %param.11) | copy-start | bytes 28
  0.7 12.9 %copy-start.5 = (bf16[200,1536]{1,0:T(8,128)(2,1)S(1)}, bf16[200,1536]{1,0:T(8,128)(2,1)}, u32[]{:S(2)}) copy-start(bf16[200,1536]{1,0:T(8,128)(2,1)} %param.12) | copy-start | bytes 1843204
  5.1 16.5 %all-to-all-start = ((bf16[16,80,128]{2,1,0:T(8,128)(2,1)}), bf16[16,80,128]{2,1,0:T(8,128)(2,1)S(1)}, u32[]{:S(2)}, u32[]{:S(2)}) async-start(bf16[16,80,128]{2,1,0:T(8,128)(2,1)} %copy.36), calls=%async_computation | async-start | bytes 655360 | tf_op jit(solution)/shard_map/all_to_all | solution.py:533
  21.8 3.6 %collective-permute-start = (bf16[2,528,128]{2,1,0:T(8,128)(2,1)S(1)}, bf16[2,528,128]{2,1,0:T(8,128)(2,1)S(1)}, u32[]{:S(2)}, u32[]{:S(2)}) collective-permute-start(bf16[2,528,128]{2,1,0:T(8,128)(2,1)S(1)} %get-tuple-element.77), channel_id=1, source_target_pairs={{0,8},{8,0},{1,9},{9,1},{2,10},{10,2},{3,11},{11,3},{4,12},{12,4},... | collective-permute-start | bytes 811016 | tf_op jit(solution)/shard_map/ppermute | solution.py:529
  25.4 20.1 %copy-start.6 = (bf16[2,2,528,128]{3,2,1,0:T(8,128)(2,1)}, bf16[2,2,528,128]{3,2,1,0:T(8,128)(2,1)S(1)}, u32[]{:S(2)}) copy-start(bf16[2,2,528,128]{3,2,1,0:T(8,128)(2,1)S(1)} %pad_maximum_fusion.refs_0_) | copy-start | bytes 1622020
  25.4 22.8 %copy-start.17 = (f32[16]{0:T(128)S(1)}, f32[16]{0:T(128)}, u32[]{:S(2)}) copy-start(f32[16]{0:T(128)} %param.17) | copy-start | bytes 196
  25.5 27.9 %copy-start.14 = (s32[1024]{0:T(1024)S(1)}, s32[1024]{0:T(1024)}, u32[]{:S(2)}) copy-start(s32[1024]{0:T(1024)} %param.18) | copy-start | bytes 12292
  25.5 29.7 %all-to-all-start.1 = ((bf16[16,192,256]{2,1,0:T(8,128)(2,1)}), bf16[16,192,256]{2,1,0:T(8,128)(2,1)}, u32[]{:S(2)}, u32[]{:S(2)}) async-start(bf16[16,192,256]{2,1,0:T(8,128)(2,1)} %get-tuple-element.47), calls=%async_computation.1 | async-start | bytes 3145728 | tf_op jit(solution)/shard_map/all_to_all | solution.py:533
  30.6 14.7 %collective-permute-start.1 = (bf16[2,2,528,128]{3,2,1,0:T(8,128)(2,1)S(1)}, bf16[2,2,528,128]{3,2,1,0:T(8,128)(2,1)S(1)}, u32[]{:S(2)}, u32[]{:S(2)}) collective-permute-start(bf16[2,2,528,128]{3,2,1,0:T(8,128)(2,1)S(1)} %pad_maximum_fusion.refs_0_), channel_id=1, source_target_pairs={{0,16},{16,32},{32,48},{48,0},{1,17},{17,33},{33,49},{49,1},{2,18}... | collective-permute-start | bytes 1622024 | tf_op jit(solution)/shard_map/ppermute | solution.py:513
  32.0 13.4 %collective-permute-start.3 = (bf16[2,2,528,128]{3,2,1,0:T(8,128)(2,1)S(1)}, bf16[2,2,528,128]{3,2,1,0:T(8,128)(2,1)S(1)}, u32[]{:S(2)}, u32[]{:S(2)}) collective-permute-start(bf16[2,2,528,128]{3,2,1,0:T(8,128)(2,1)S(1)} %pad_maximum_fusion.refs_0_), channel_id=1, source_target_pairs={{0,48},{16,0},{32,16},{48,32},{1,49},{17,1},{33,17},{49,33},{2,50}... | collective-permute-start | bytes 1622024 | tf_op jit(solution)/shard_map/ppermute | solution.py:513
  45.4 8.0 %collective-permute-start.2 = (bf16[2,1,528,128]{3,2,1,0:T(8,128)(2,1)S(1)}, bf16[2,1,528,128]{3,2,1,0:T(8,128)(2,1)S(1)}, u32[]{:S(2)}, u32[]{:S(2)}) collective-permute-start(bf16[2,1,528,128]{3,2,1,0:T(8,128)(2,1)S(1)} %slice.35), channel_id=1, source_target_pairs={{0,16},{16,32},{32,48},{48,0},{1,17},{17,33},{33,49},{49,1},{2,18}... | collective-permute-start | bytes 811016 | tf_op jit(solution)/shard_map/ppermute | solution.py:513
  45.5 9.6 %collective-permute-start.4 = (bf16[2,1,528,128]{3,2,1,0:T(8,128)(2,1)S(1)}, bf16[2,1,528,128]{3,2,1,0:T(8,128)(2,1)}, u32[]{:S(2)}, u32[]{:S(2)}) collective-permute-start(bf16[2,1,528,128]{3,2,1,0:T(8,128)(2,1)S(1)} %slice.36), channel_id=1, source_target_pairs={{0,48},{16,0},{32,16},{48,32},{1,49},{17,1},{33,17},{49,33},{2,50}... | collective-permute-start | bytes 811016 | tf_op jit(solution)/shard_map/ppermute | solution.py:513
  77.3 25.4 %all-to-all-start.2 = ((bf16[16,192,256]{2,1,0:T(8,128)(2,1)}), bf16[16,192,256]{2,1,0:T(8,128)(2,1)}, u32[]{:S(2)}, u32[]{:S(2)}) async-start(bf16[16,192,256]{2,1,0:T(8,128)(2,1)} %get-tuple-element.49), calls=%async_computation.2 | async-start | bytes 3145728 | tf_op jit(solution)/shard_map/all_to_all | solution.py:533
  83.0 28.1 %copy-start.7 = (bf16[2,2,8,64,128]{4,3,2,1,0:T(8,128)(2,1)S(1)}, bf16[2,2,8,64,128]{4,3,2,1,0:T(8,128)(2,1)}, u32[]{:S(2)}) copy-start(bf16[2,2,8,64,128]{4,3,2,1,0:T(8,128)(2,1)} %get-tuple-element.56) | copy-start | bytes 1572868
  83.0 28.1 %collective-permute-start.8 = (bf16[2,2,8,64,128]{4,3,2,1,0:T(8,128)(2,1)}, bf16[2,2,8,64,128]{4,3,2,1,0:T(8,128)(2,1)S(1)}, u32[]{:S(2)}, u32[]{:S(2)}) collective-permute-start(bf16[2,2,8,64,128]{4,3,2,1,0:T(8,128)(2,1)} %get-tuple-element.57), channel_id=1, source_target_pairs={{0,16},{16,32},{32,48},{48,0},{1,17},{17,33},{33,49},{49,1},{2,18}... | collective-permute-start | bytes 1572872 | tf_op jit(solution)/shard_map/ppermute | solution.py:513
  84.2 27.0 %collective-permute-start.9 = (bf16[2,2,8,64,128]{4,3,2,1,0:T(8,128)(2,1)}, bf16[2,2,8,64,128]{4,3,2,1,0:T(8,128)(2,1)}, u32[]{:S(2)}, u32[]{:S(2)}) collective-permute-start(bf16[2,2,8,64,128]{4,3,2,1,0:T(8,128)(2,1)} %get-tuple-element.58), channel_id=1, source_target_pairs={{0,32},{16,48},{32,0},{48,16},{1,33},{17,49},{33,1},{49,17},{2,34}... | collective-permute-start | bytes 1572872 | tf_op jit(solution)/shard_map/ppermute | solution.py:513
  86.8 24.3 %collective-permute-start.10 = (bf16[2,2,8,64,128]{4,3,2,1,0:T(8,128)(2,1)}, bf16[2,2,8,64,128]{4,3,2,1,0:T(8,128)(2,1)}, u32[]{:S(2)}, u32[]{:S(2)}) collective-permute-start(bf16[2,2,8,64,128]{4,3,2,1,0:T(8,128)(2,1)} %get-tuple-element.59), channel_id=1, source_target_pairs={{0,48},{16,0},{32,16},{48,32},{1,49},{17,1},{33,17},{49,33},{2,50}... | collective-permute-start | bytes 1572872 | tf_op jit(solution)/shard_map/ppermute | solution.py:513
  106.1 6.8 %copy-start.3 = (bf16[2,128,768]{2,1,0:T(8,128)(2,1)S(1)}, bf16[2,128,768]{2,1,0:T(8,128)(2,1)}, u32[]{:S(2)}) copy-start(bf16[2,128,768]{2,1,0:T(8,128)(2,1)} %param.19) | copy-start | bytes 1179652
  106.1 15.4 %collective-permute-start.5 = (bf16[5,384,256]{2,1,0:T(8,128)(2,1)}, bf16[5,384,256]{2,1,0:T(8,128)(2,1)}, u32[]{:S(2)}, u32[]{:S(2)}) collective-permute-start(bf16[5,384,256]{2,1,0:T(8,128)(2,1)} %get-tuple-element.53.send_ref), channel_id=1, source_target_pairs={{0,8},{8,0},{1,9},{9,1},{2,10},{10,2},{3,11},{11,3},{4,12},{12,4},... | collective-permute-start | bytes 2949128 | tf_op jit(solution)/shard_map/ppermute | solution.py:529
  112.7 1.6 collective-permute-start.11
  112.9 8.5 %collective-permute-start.7 = (bf16[256,768]{1,0:T(8,128)(2,1)S(1)}, bf16[256,768]{1,0:T(8,128)(2,1)S(1)}, u32[]{:S(2)}, u32[]{:S(2)}) collective-permute-start(bf16[256,768]{1,0:T(8,128)(2,1)S(1)} %bitcast.62), channel_id=1, source_target_pairs={{0,8},{8,0},{1,9},{9,1},{2,10},{10,2},{3,11},{11,3},{4,12},{12,4},... | collective-permute-start | bytes 1179656 | tf_op jit(solution)/shard_map/ppermute | solution.py:529
  113.3 8.1 %collective-permute-start.6 = (bf16[256,768]{1,0:T(8,128)(2,1)}, bf16[256,768]{1,0:T(8,128)(2,1)S(1)}, u32[]{:S(2)}, u32[]{:S(2)}) collective-permute-start(bf16[256,768]{1,0:T(8,128)(2,1)} %get-tuple-element.54.own_normed_ref), channel_id=1, source_target_pairs={{0,8},{8,0},{1,9},{9,1},{2,10},{10,2},{3,11},{11,3},{4,12},{12,4},... | collective-permute-start | bytes 1179656 | tf_op jit(solution)/shard_map/ppermute | solution.py:529
  115.1 14.3 %all-to-all-start.4 = ((bf16[16,64,128]{2,1,0:T(8,128)(2,1)}), bf16[16,64,128]{2,1,0:T(8,128)(2,1)S(1)}, u32[]{:S(2)}, u32[]{:S(2)}) async-start(bf16[16,64,128]{2,1,0:T(8,128)(2,1)} %bitcast.28), calls=%async_computation.4 | async-start | bytes 524288 | tf_op jit(solution)/shard_map/all_to_all | solution.py:533
  129.4 18.0 %copy-start.4 = (bf16[16,64,128]{2,1,0:T(8,128)(2,1)}, bf16[16,64,128]{2,1,0:T(8,128)(2,1)S(1)}, u32[]{:S(2)}) copy-start(bf16[16,64,128]{2,1,0:T(8,128)(2,1)S(1)} %all-to-all-done.4) | copy-start | bytes 786436
  129.4 45.3 %all-to-all-start.3 = ((bf16[64,64,384]{2,1,0:T(8,128)(2,1)}), bf16[64,64,384]{2,1,0:T(8,128)(2,1)}, u32[]{:S(2)}, u32[]{:S(2)}) async-start(bf16[64,64,384]{2,1,0:T(8,128)(2,1)} %bitcast.58), calls=%async_computation.3 | async-start | bytes 6291456 | tf_op jit(solution)/shard_map/all_to_all | solution.py:533
  148.2 23.4 %collective-permute-start.12 = (f32[2560]{0:T(1024)S(1)}, f32[2560]{0:T(1024)S(1)}, u32[]{:S(2)}, u32[]{:S(2)}) collective-permute-start(f32[2560]{0:T(1024)S(1)} %get-tuple-element.74), channel_id=1, source_target_pairs={{0,2},{2,0},{4,6},{6,4},{1,3},{3,1},{5,7},{7,5},{8,10},{10,8},{12,... | collective-permute-start | bytes 30728 | tf_op jit(solution)/shard_map/ppermute | solution.py:649
  179.1 8.3 %copy-start.13 = (bf16[128,16]{0,1:T(8,128)(2,1)S(1)}, bf16[128,16]{0,1:T(8,128)(2,1)}, u32[]{:S(2)}) copy-start(bf16[128,16]{0,1:T(8,128)(2,1)} %param.16) | copy-start | bytes 12292
  179.1 49.2 %all-to-all-start.5 = ((bf16[64,72,384]{2,1,0:T(8,128)(2,1)}), bf16[64,72,384]{2,1,0:T(8,128)(2,1)S(1)}, u32[]{:S(2)}, u32[]{:S(2)}) async-start(bf16[64,72,384]{2,1,0:T(8,128)(2,1)} %shard_map.166), calls=%async_computation.5 | async-start | bytes 7077888 | tf_op jit(solution)/shard_map/all_to_all | solution.py:533
  228.2 7.5 %copy-start.2 = (bf16[64,72,384]{2,1,0:T(8,128)(2,1)}, bf16[64,72,384]{2,1,0:T(8,128)(2,1)S(1)}, u32[]{:S(2)}) copy-start(bf16[64,72,384]{2,1,0:T(8,128)(2,1)S(1)} %all-to-all-done.5.block_ref) | copy-start | bytes 10616836
  228.3 14.9 %collective-permute-start.13 = (bf16[64,72,384]{2,1,0:T(8,128)(2,1)S(1)}, bf16[64,72,384]{2,1,0:T(8,128)(2,1)}, u32[]{:S(2)}, u32[]{:S(2)}) collective-permute-start(bf16[64,72,384]{2,1,0:T(8,128)(2,1)S(1)} %all-to-all-done.5.block_ref), channel_id=1, source_target_pairs={{0,8},{8,0},{1,9},{9,1},{2,10},{10,2},{3,11},{11,3},{4,12},{12,4},... | collective-permute-start | bytes 10616840 | tf_op jit(solution)/shard_map/ppermute | solution.py:529
  235.1 4.5 %collective-permute-start.14 = (f32[8,2,8,384]{3,2,1,0:T(8,128)}, f32[8,2,8,384]{3,2,1,0:T(8,128)S(1)}, u32[]{:S(2)}, u32[]{:S(2)}) collective-permute-start(f32[8,2,8,384]{3,2,1,0:T(8,128)} %shard_map.169.mine_ref), channel_id=1, source_target_pairs={{0,8},{8,0},{1,9},{9,1},{2,10},{10,2},{3,11},{11,3},{4,12},{12,4},... | collective-permute-start | bytes 589832 | tf_op jit(solution)/shard_map/ppermute | solution.py:529
  243.1 4.1 %copy-start.1 = (bf16[128,64,128]{2,1,0:T(8,128)(2,1)S(1)}, bf16[128,64,128]{2,1,0:T(8,128)(2,1)}, u32[]{:S(2)}) copy-start(bf16[128,64,128]{2,1,0:T(8,128)(2,1)} %param.15) | copy-start | bytes 6291460
  (7 other events, 11.3 us)

commit v8 on v7

--- a/solution.py
+++ b/solution.py
@@ -590,7 +590,7 @@
     near = jnp.stack([bias_own, swap(bias_own)])
     sent, near = lax.optimization_barrier((sent, near))
     biases = spread_bias(near)
-    biases[3], chain_col, chain_row = lax.optimization_barrier((biases[3], chain_col, chain_row))
+    biases[1], chain_col, chain_row = lax.optimization_barrier((biases[1], chain_col, chain_row))
     head_rows = exchange(sent, head_axes)
     y_at = lax.axis_index("y")
     base = jnp.stack(

time: 248 us -> 248 us (level)
    all_to_all x6, waiting for transfers between devices: 56.7 us -> 59.9 us  [exchange(): return lax.all_to_all(array, axes, 0, 0, tiled=True)]
where the time goes in v8:
time: 248 us; the launch traced here: 247 us
  waiting for transfers between devices  98.3 us (40%)
  starting transfers between devices  64.3 us (26%)
  Pallas kernels  60.8 us (25%)
  local copies, waits for them, and re-layouts  11.7 us (5%)
  matrix products  4.9 us (2%)
  other arithmetic  4.83 us (2%)
  between operations  2.56 us (1%)
    all_to_all x6, waiting for transfers between devices, exchange(): return lax.all_to_all(array, axes, 0, 0, tiled=True)  59.9 us
    all_to_all x6, starting transfers between devices, exchange(): return lax.all_to_all(array, axes, 0, 0, tiled=True)  40.3 us
    pallas_call x6, Pallas kernels, in_vmem(): pl.pallas_call(kernel, in_specs=scalars + [vmem] * (len(operands) - smem)...  25.7 us
    ppermute x1, waiting for transfers between devices, shards(): lax.ppermute(pick(1 - odd), 'x', [(i, i ^ 1) for i in range(4)])  22.3 us
    pallas_call x1, Pallas kernels, attend(): pl.pallas_call(functools.partial(attend_kernel, factor, part), grid=(samp...  22.2 us
    ppermute x7, waiting for transfers between devices, ring(): return lax.ppermute(array, 'y', [(i, (i + shift) % 4) for i in range(4)])  14 us
    ppermute x7, starting transfers between devices, swap(): return lax.ppermute(array, 'core', [(0, 1), (1, 0)])  12.2 us
    ppermute x7, starting transfers between devices, ring(): return lax.ppermute(array, 'y', [(i, (i + shift) % 4) for i in range(4)])  10.7 us
  transfers between devices with their start and end apart: 21, of which 11 were waited for; matrix products, arithmetic and copies ran while one was open for 6% of the time, Pallas kernels for 12%

profile of v8, /device:TPU:1, one launch (start us, length us, event | category | flops | bytes accessed | tf_op | source)
XLA Modules:
  0.0 247.4 jit_solution(2693993626182937045)
XLA Ops:
  2.2 1.9 fusion.16
  5.1 8.4 %all-to-all-start = ((bf16[16,80,128]{2,1,0:T(8,128)(2,1)}), bf16[16,80,128]{2,1,0:T(8,128)(2,1)S(1)}, u32[]{:S(2)}, u32[]{:S(2)}) async-start(bf16[16,80,128]{2,1,0:T(8,128)(2,1)} %copy.36), calls=%async_computation | async-start | bytes 655360 | tf_op jit(solution)/shard_map/all_to_all | solution.py:533
  14.4 6.6 %shard_map.161 = (bf16[16,192,256]{2,1,0:T(8,128)(2,1)}, f32[768,256]{1,0:T(8,128)}, f32[768,256]{1,0:T(8,128)}, bf16[256,768]{1,0:T(8,128)(2,1)}) custom-call(bf16[256,768]{1,0:T(8,128)(2,1)} %bitcast.64, bf16[256,768]{1,0:T(8,128)(2,1)} %bitcast.59, f32[2,1536]{1,0:T(2,128)} %fusion.11.mod_ref, bf16[768,3072]{1,0:T(8,128)(2,1)} %weight_ref.3, ...), custom_call_target="tpu_custom_call" | custom-call | flops 1509949440 | bytes 6696960 | tf_op jit(solution)/shard_map/pallas_call | solution.py:216
  21.8 2.4 collective-permute-start
  25.5 5.2 %all-to-all-start.1 = ((bf16[16,192,256]{2,1,0:T(8,128)(2,1)}), bf16[16,192,256]{2,1,0:T(8,128)(2,1)}, u32[]{:S(2)}, u32[]{:S(2)}) async-start(bf16[16,192,256]{2,1,0:T(8,128)(2,1)} %get-tuple-element.47), calls=%async_computation.1 | async-start | bytes 3145728 | tf_op jit(solution)/shard_map/all_to_all | solution.py:533
  33.5 11.8 %collective-permute-done.2.refs_2_ = bf16[2,2,528,128]{3,2,1,0:T(8,128)(2,1)S(1)} collective-permute-done((bf16[2,2,528,128]{3,2,1,0:T(8,128)(2,1)S(1)}, bf16[2,2,528,128]{3,2,1,0:T(8,128)(2,1)S(1)}, u32[]{:S(2)}, u32[]{:S(2)}) %collective-permute-start.2) | collective-permute-done | bytes 540704 | tf_op jit(solution)/shard_map/ppermute | solution.py:513
  45.5 2.7 %collective-permute-start.4 = (bf16[2,1,528,128]{3,2,1,0:T(8,128)(2,1)S(1)}, bf16[2,1,528,128]{3,2,1,0:T(8,128)(2,1)}, u32[]{:S(2)}, u32[]{:S(2)}) collective-permute-start(bf16[2,1,528,128]{3,2,1,0:T(8,128)(2,1)S(1)} %slice.36), channel_id=1, source_target_pairs={{0,48},{16,0},{32,16},{48,32},{1,49},{17,1},{33,17},{49,33},{2,50}... | collective-permute-start | bytes 811016 | tf_op jit(solution)/shard_map/ppermute | solution.py:513
  51.2 2.2 collective-permute-done.3.refs_3_
  53.4 1.8 all-to-all-done.1.rows_ref
  55.2 22.2 %shard_map.162 = (bf16[16,192,256]{2,1,0:T(8,128)(2,1)}, bf16[2,2,8,64,128]{4,3,2,1,0:T(8,128)(2,1)}, bf16[2,2,8,64,128]{4,3,2,1,0:T(8,128)(2,1)}, bf16[2,2,8,64...) custom-call(s32[16]{0:T(128)} %stack.76.base_ref, f32[1]{0:T(128)} %dynamic_slice.10.cross_ref, ...), custom_call_target="tpu_custom_call" | custom-call | flops 2415919104 | bytes 16777216 | tf_op jit(solution)/shard_map/pallas_call | solution.py:138
  77.3 5.4 %all-to-all-start.2 = ((bf16[16,192,256]{2,1,0:T(8,128)(2,1)}), bf16[16,192,256]{2,1,0:T(8,128)(2,1)}, u32[]{:S(2)}, u32[]{:S(2)}) async-start(bf16[16,192,256]{2,1,0:T(8,128)(2,1)} %get-tuple-element.49), calls=%async_computation.2 | async-start | bytes 3145728 | tf_op jit(solution)/shard_map/all_to_all | solution.py:533
  84.2 2.6 %collective-permute-start.9 = (bf16[2,2,8,64,128]{4,3,2,1,0:T(8,128)(2,1)}, bf16[2,2,8,64,128]{4,3,2,1,0:T(8,128)(2,1)}, u32[]{:S(2)}, u32[]{:S(2)}) collective-permute-start(bf16[2,2,8,64,128]{4,3,2,1,0:T(8,128)(2,1)} %get-tuple-element.58), channel_id=1, source_target_pairs={{0,32},{16,48},{32,0},{48,16},{1,33},{17,49},{33,1},{49,17},{2,34}... | collective-permute-start | bytes 1572872 | tf_op jit(solution)/shard_map/ppermute | solution.py:513
  87.8 16.4 %all-to-all-done.2.back_ref = bf16[16,192,256]{2,1,0:T(8,128)(2,1)} async-done(((bf16[16,192,256]{2,1,0:T(8,128)(2,1)}), bf16[16,192,256]{2,1,0:T(8,128)(2,1)}, u32[]{:S(2)}, u32[]{:S(2)}) %all-to-all-start.2) | async-done | bytes 1572896 | tf_op jit(solution)/shard_map/all_to_all | solution.py:533
  104.2 3.4 %shard_map.163 = (bf16[5,384,256]{2,1,0:T(8,128)(2,1)}, bf16[5,384,256]{2,1,0:T(8,128)(2,1)}) custom-call(s32[1]{0:T(128)} %bitcast.core_ref.place_ref, bf16[16,192,256]{2,1,0:T(8,128)(2,1)} %all-to-all-done.2.back_ref, f32[768,256]{1,0:T(8,128)} %get-tuple-element.50.gate_ref, f32[768,256]{1,0:T(8,128)} %get-tuple-element.51.grad_gated_ref), custom_call_target="tpu_custom_call" | custom-call | bytes 3145732 | tf_op jit(solution)/shard_map/pallas_call | solution.py:216
  107.6 4.4 %collective-permute-start.5 = (bf16[5,384,256]{2,1,0:T(8,128)(2,1)}, bf16[5,384,256]{2,1,0:T(8,128)(2,1)}, u32[]{:S(2)}, u32[]{:S(2)}) collective-permute-start(bf16[5,384,256]{2,1,0:T(8,128)(2,1)} %get-tuple-element.53.send_ref), channel_id=1, source_target_pairs={{0,8},{8,0},{1,9},{9,1},{2,10},{10,2},{3,11},{11,3},{4,12},{12,4},... | collective-permute-start | bytes 2949128 | tf_op jit(solution)/shard_map/ppermute | solution.py:529
  116.0 5.4 %all-to-all-start.4 = ((bf16[16,64,128]{2,1,0:T(8,128)(2,1)}), bf16[16,64,128]{2,1,0:T(8,128)(2,1)S(1)}, u32[]{:S(2)}, u32[]{:S(2)}) async-start(bf16[16,64,128]{2,1,0:T(8,128)(2,1)} %bitcast.28), calls=%async_computation.4 | async-start | bytes 524288 | tf_op jit(solution)/shard_map/all_to_all | solution.py:533
  122.3 4.9 %shard_map.164 = bf16[16,4,64,384]{3,2,1,0:T(8,128)(2,1)} custom-call(bf16[5,384,256]{2,1,0:T(8,128)(2,1)} %get-tuple-element.52.keep_ref, bf16[5,384,256]{2,1,0:T(8,128)(2,1)} %collective-permute-done.5.got_ref, bf16[256,768]{1,0:T(8,128)(2,1)} %get-tuple-element.54.own_normed_ref, bf16[256,768]{1,0:T(8,128)(2,1)} %copy-done.9, bf16[256,768]{1,0:T(8,128)(2,1)} %bitcast.60, ...), custom_call_target="tpu_custom_call" | custom-call | flops 1509949440 | bytes 8388608 | tf_op jit(solution)/shard_map/pallas_call | solution.py:366
  127.2 2.2 all-to-all-done.4
  129.4 7.6 %all-to-all-start.3 = ((bf16[64,64,384]{2,1,0:T(8,128)(2,1)}), bf16[64,64,384]{2,1,0:T(8,128)(2,1)}, u32[]{:S(2)}, u32[]{:S(2)}) async-start(bf16[64,64,384]{2,1,0:T(8,128)(2,1)} %bitcast.58), calls=%async_computation.3 | async-start | bytes 6291456 | tf_op jit(solution)/shard_map/all_to_all | solution.py:533
  140.7 6.8 %shard_map.165 = (bf16[256,768]{1,0:T(8,128)(2,1)}, bf16[256,768]{1,0:T(8,128)(2,1)}, f32[8,384]{1,0:T(8,128)}) custom-call(s32[1]{0:T(128)} %bitcast.core_ref.place_ref, bf16[5,384,256]{2,1,0:T(8,128)(2,1)} %get-tuple-element.52.keep_ref, bf16[5,384,256]{2,1,0:T(8,128)(2,1)} %get-tuple-element.53.send_ref, bf16[256,768]{1,0:T(8,128)(2,1)} %bitcast.65, ...), custom_call_target="tpu_custom_call" | custom-call | flops 1509949440 | bytes 8663044 | tf_op jit(solution)/shard_map/pallas_call | solution.py:216
  149.3 22.3 %collective-permute-done.12 = f32[2560]{0:T(1024)S(1)} collective-permute-done((f32[2560]{0:T(1024)S(1)}, f32[2560]{0:T(1024)S(1)}, u32[]{:S(2)}, u32[]{:S(2)}) %collective-permute-start.12) | collective-permute-done | bytes 10272 | tf_op jit(solution)/shard_map/ppermute | solution.py:649
  172.3 2.5 all-to-all-done.3.parts_ref
  174.8 4.3 %shard_map.166 = bf16[64,72,384]{2,1,0:T(8,128)(2,1)} custom-call(bf16[64,64,384]{2,1,0:T(8,128)(2,1)} %all-to-all-done.3.parts_ref, f32[8,384]{1,0:T(8,128)} %reshape.81.small_ref), custom_call_target="tpu_custom_call" | custom-call | flops 1572864 | bytes 3158016 | tf_op jit(solution)/shard_map/pallas_call | solution.py:216
  179.1 8.3 %all-to-all-start.5 = ((bf16[64,72,384]{2,1,0:T(8,128)(2,1)}), bf16[64,72,384]{2,1,0:T(8,128)(2,1)S(1)}, u32[]{:S(2)}, u32[]{:S(2)}) async-start(bf16[64,72,384]{2,1,0:T(8,128)(2,1)} %shard_map.166), calls=%async_computation.5 | async-start | bytes 7077888 | tf_op jit(solution)/shard_map/all_to_all | solution.py:533
  187.4 1.7 convert_bitcast_fusion
  189.1 2.7 %copy.40 = bf16[128,64,128]{2,1,0:T(8,128)(2,1)} copy(bf16[128,64,128]{2,0,1:T(8,128)(2,1)S(1)} %convert_bitcast_fusion) | data formatting | bytes 4194304 | tf_op jit(solution)/shard_map/convert_element_type | solution.py:632
  191.8 36.5 %all-to-all-done.5.block_ref = bf16[64,72,384]{2,1,0:T(8,128)(2,1)S(1)} async-done(((bf16[64,72,384]{2,1,0:T(8,128)(2,1)}), bf16[64,72,384]{2,1,0:T(8,128)(2,1)S(1)}, u32[]{:S(2)}, u32[]{:S(2)}) %all-to-all-start.5) | async-done | bytes 3538976 | tf_op jit(solution)/shard_map/all_to_all | solution.py:533
  228.3 4.1 %collective-permute-start.13 = (bf16[64,72,384]{2,1,0:T(8,128)(2,1)S(1)}, bf16[64,72,384]{2,1,0:T(8,128)(2,1)}, u32[]{:S(2)}, u32[]{:S(2)}) collective-permute-start(bf16[64,72,384]{2,1,0:T(8,128)(2,1)S(1)} %all-to-all-done.5.block_ref), channel_id=1, source_target_pairs={{0,8},{8,0},{1,9},{9,1},{2,10},{10,2},{3,11},{11,3},{4,12},{12,4},... | collective-permute-start | bytes 10616840 | tf_op jit(solution)/shard_map/ppermute | solution.py:529
  233.3 1.8 shard_map.169.mine_ref
  235.7 3.9 %shard_map.167 = (f32[768,3072]{1,0:T(8,128)}, f32[2,384,768]{2,1,0:T(8,128)}) custom-call(s32[1]{0:T(128)} %bitcast.core_ref.place_ref, bf16[64,72,384]{2,1,0:T(8,128)(2,1)} %copy-done.2), custom_call_target="tpu_custom_call" | custom-call | bytes 10485760 | tf_op jit(solution)/shard_map/pallas_call | solution.py:429
  240.3 2.8 %shard_map.170 = (f32[200,1536]{1,0:T(8,128)}, f32[16,128]{1,0:T(8,128)}, f32[1,16]{1,0:T(1,128)}) custom-call(f32[8,2,8,384]{3,2,1,0:T(8,128)} %shard_map.169.mine_ref, f32[8,2,8,384]{3,2,1,0:T(8,128)} %copy-done.10), custom_call_target="tpu_custom_call" | custom-call | bytes 393216 | tf_op jit(solution)/shard_map/pallas_call | solution.py:216
  243.1 4.1 %shard_map.168 = (f32[768,3072]{1,0:T(8,128)}, f32[2,384,768]{2,1,0:T(8,128)}) custom-call(s32[1]{0:T(128)S(6)} %sub.21.place_ref, bf16[64,72,384]{2,1,0:T(8,128)(2,1)} %collective-permute-done.13.block_ref, f32[768,3072]{1,0:T(8,128)} %get-tuple-element.67.refs_0_, ...), custom_call_target="tpu_custom_call", output_to_operand_aliasing={{0}: (2, {}), {1}: (3, {})} | custom-call | bytes 10485760 | tf_op jit(solution)/shard_map/pallas_call | solution.py:429
  (94 shorter events, 25.5 us)
Async XLA Ops:
  0.7 12.9 %copy-start.15 = (s32[2]{0:T(128)S(1)}, s32[2]{0:T(128)}, u32[]{:S(2)}) copy-start(s32[2]{0:T(128)} %param.11) | copy-start | bytes 28
  0.7 12.9 %copy-start.5 = (bf16[200,1536]{1,0:T(8,128)(2,1)S(1)}, bf16[200,1536]{1,0:T(8,128)(2,1)}, u32[]{:S(2)}) copy-start(bf16[200,1536]{1,0:T(8,128)(2,1)} %param.12) | copy-start | bytes 1843204
  5.1 16.5 %all-to-all-start = ((bf16[16,80,128]{2,1,0:T(8,128)(2,1)}), bf16[16,80,128]{2,1,0:T(8,128)(2,1)S(1)}, u32[]{:S(2)}, u32[]{:S(2)}) async-start(bf16[16,80,128]{2,1,0:T(8,128)(2,1)} %copy.36), calls=%async_computation | async-start | bytes 655360 | tf_op jit(solution)/shard_map/all_to_all | solution.py:533
  21.8 3.6 %collective-permute-start = (bf16[2,528,128]{2,1,0:T(8,128)(2,1)S(1)}, bf16[2,528,128]{2,1,0:T(8,128)(2,1)S(1)}, u32[]{:S(2)}, u32[]{:S(2)}) collective-permute-start(bf16[2,528,128]{2,1,0:T(8,128)(2,1)S(1)} %get-tuple-element.77), channel_id=1, source_target_pairs={{0,8},{8,0},{1,9},{9,1},{2,10},{10,2},{3,11},{11,3},{4,12},{12,4},... | collective-permute-start | bytes 811016 | tf_op jit(solution)/shard_map/ppermute | solution.py:529
  25.4 20.1 %copy-start.6 = (bf16[2,2,528,128]{3,2,1,0:T(8,128)(2,1)}, bf16[2,2,528,128]{3,2,1,0:T(8,128)(2,1)S(1)}, u32[]{:S(2)}) copy-start(bf16[2,2,528,128]{3,2,1,0:T(8,128)(2,1)S(1)} %pad_maximum_fusion.refs_0_) | copy-start | bytes 1622020
  25.4 22.8 %copy-start.17 = (f32[16]{0:T(128)S(1)}, f32[16]{0:T(128)}, u32[]{:S(2)}) copy-start(f32[16]{0:T(128)} %param.17) | copy-start | bytes 196
  25.5 24.1 %copy-start.14 = (s32[1024]{0:T(1024)S(1)}, s32[1024]{0:T(1024)}, u32[]{:S(2)}) copy-start(s32[1024]{0:T(1024)} %param.18) | copy-start | bytes 12292
  25.5 29.7 %all-to-all-start.1 = ((bf16[16,192,256]{2,1,0:T(8,128)(2,1)}), bf16[16,192,256]{2,1,0:T(8,128)(2,1)}, u32[]{:S(2)}, u32[]{:S(2)}) async-start(bf16[16,192,256]{2,1,0:T(8,128)(2,1)} %get-tuple-element.47), calls=%async_computation.1 | async-start | bytes 3145728 | tf_op jit(solution)/shard_map/all_to_all | solution.py:533
  30.6 14.7 %collective-permute-start.2 = (bf16[2,2,528,128]{3,2,1,0:T(8,128)(2,1)S(1)}, bf16[2,2,528,128]{3,2,1,0:T(8,128)(2,1)S(1)}, u32[]{:S(2)}, u32[]{:S(2)}) collective-permute-start(bf16[2,2,528,128]{3,2,1,0:T(8,128)(2,1)S(1)} %pad_maximum_fusion.refs_0_), channel_id=1, source_target_pairs={{0,16},{16,32},{32,48},{48,0},{1,17},{17,33},{33,49},{49,1},{2,18}... | collective-permute-start | bytes 1622024 | tf_op jit(solution)/shard_map/ppermute | solution.py:513
  32.0 13.4 %collective-permute-start.1 = (bf16[2,2,528,128]{3,2,1,0:T(8,128)(2,1)S(1)}, bf16[2,2,528,128]{3,2,1,0:T(8,128)(2,1)S(1)}, u32[]{:S(2)}, u32[]{:S(2)}) collective-permute-start(bf16[2,2,528,128]{3,2,1,0:T(8,128)(2,1)S(1)} %pad_maximum_fusion.refs_0_), channel_id=1, source_target_pairs={{0,48},{16,0},{32,16},{48,32},{1,49},{17,1},{33,17},{49,33},{2,50}... | collective-permute-start | bytes 1622024 | tf_op jit(solution)/shard_map/ppermute | solution.py:513
  45.4 8.0 %collective-permute-start.3 = (bf16[2,1,528,128]{3,2,1,0:T(8,128)(2,1)S(1)}, bf16[2,1,528,128]{3,2,1,0:T(8,128)(2,1)S(1)}, u32[]{:S(2)}, u32[]{:S(2)}) collective-permute-start(bf16[2,1,528,128]{3,2,1,0:T(8,128)(2,1)S(1)} %slice.35), channel_id=1, source_target_pairs={{0,16},{16,32},{32,48},{48,0},{1,17},{17,33},{33,49},{49,1},{2,18}... | collective-permute-start | bytes 811016 | tf_op jit(solution)/shard_map/ppermute | solution.py:513
  45.5 7.9 %collective-permute-start.4 = (bf16[2,1,528,128]{3,2,1,0:T(8,128)(2,1)S(1)}, bf16[2,1,528,128]{3,2,1,0:T(8,128)(2,1)}, u32[]{:S(2)}, u32[]{:S(2)}) collective-permute-start(bf16[2,1,528,128]{3,2,1,0:T(8,128)(2,1)S(1)} %slice.36), channel_id=1, source_target_pairs={{0,48},{16,0},{32,16},{48,32},{1,49},{17,1},{33,17},{49,33},{2,50}... | collective-permute-start | bytes 811016 | tf_op jit(solution)/shard_map/ppermute | solution.py:513
  77.3 26.9 %all-to-all-start.2 = ((bf16[16,192,256]{2,1,0:T(8,128)(2,1)}), bf16[16,192,256]{2,1,0:T(8,128)(2,1)}, u32[]{:S(2)}, u32[]{:S(2)}) async-start(bf16[16,192,256]{2,1,0:T(8,128)(2,1)} %get-tuple-element.49), calls=%async_computation.2 | async-start | bytes 3145728 | tf_op jit(solution)/shard_map/all_to_all | solution.py:533
  82.8 29.3 %copy-start.7 = (bf16[2,2,8,64,128]{4,3,2,1,0:T(8,128)(2,1)S(1)}, bf16[2,2,8,64,128]{4,3,2,1,0:T(8,128)(2,1)}, u32[]{:S(2)}) copy-start(bf16[2,2,8,64,128]{4,3,2,1,0:T(8,128)(2,1)} %get-tuple-element.56) | copy-start | bytes 1572868
  82.8 29.3 %collective-permute-start.8 = (bf16[2,2,8,64,128]{4,3,2,1,0:T(8,128)(2,1)}, bf16[2,2,8,64,128]{4,3,2,1,0:T(8,128)(2,1)S(1)}, u32[]{:S(2)}, u32[]{:S(2)}) collective-permute-start(bf16[2,2,8,64,128]{4,3,2,1,0:T(8,128)(2,1)} %get-tuple-element.57), channel_id=1, source_target_pairs={{0,16},{16,32},{32,48},{48,0},{1,17},{17,33},{33,49},{49,1},{2,18}... | collective-permute-start | bytes 1572872 | tf_op jit(solution)/shard_map/ppermute | solution.py:513
  84.2 27.9 %collective-permute-start.9 = (bf16[2,2,8,64,128]{4,3,2,1,0:T(8,128)(2,1)}, bf16[2,2,8,64,128]{4,3,2,1,0:T(8,128)(2,1)}, u32[]{:S(2)}, u32[]{:S(2)}) collective-permute-start(bf16[2,2,8,64,128]{4,3,2,1,0:T(8,128)(2,1)} %get-tuple-element.58), channel_id=1, source_target_pairs={{0,32},{16,48},{32,0},{48,16},{1,33},{17,49},{33,1},{49,17},{2,34}... | collective-permute-start | bytes 1572872 | tf_op jit(solution)/shard_map/ppermute | solution.py:513
  86.8 25.3 %collective-permute-start.10 = (bf16[2,2,8,64,128]{4,3,2,1,0:T(8,128)(2,1)}, bf16[2,2,8,64,128]{4,3,2,1,0:T(8,128)(2,1)}, u32[]{:S(2)}, u32[]{:S(2)}) collective-permute-start(bf16[2,2,8,64,128]{4,3,2,1,0:T(8,128)(2,1)} %get-tuple-element.59), channel_id=1, source_target_pairs={{0,48},{16,0},{32,16},{48,32},{1,49},{17,1},{33,17},{49,33},{2,50}... | collective-permute-start | bytes 1572872 | tf_op jit(solution)/shard_map/ppermute | solution.py:513
  107.6 6.2 %copy-start.3 = (bf16[2,128,768]{2,1,0:T(8,128)(2,1)S(1)}, bf16[2,128,768]{2,1,0:T(8,128)(2,1)}, u32[]{:S(2)}) copy-start(bf16[2,128,768]{2,1,0:T(8,128)(2,1)} %param.19) | copy-start | bytes 1179652
  107.6 13.9 %collective-permute-start.5 = (bf16[5,384,256]{2,1,0:T(8,128)(2,1)}, bf16[5,384,256]{2,1,0:T(8,128)(2,1)}, u32[]{:S(2)}, u32[]{:S(2)}) collective-permute-start(bf16[5,384,256]{2,1,0:T(8,128)(2,1)} %get-tuple-element.53.send_ref), channel_id=1, source_target_pairs={{0,8},{8,0},{1,9},{9,1},{2,10},{10,2},{3,11},{11,3},{4,12},{12,4},... | collective-permute-start | bytes 2949128 | tf_op jit(solution)/shard_map/ppermute | solution.py:529
  113.6 1.6 collective-permute-start.11
  113.8 7.6 %collective-permute-start.7 = (bf16[256,768]{1,0:T(8,128)(2,1)S(1)}, bf16[256,768]{1,0:T(8,128)(2,1)S(1)}, u32[]{:S(2)}, u32[]{:S(2)}) collective-permute-start(bf16[256,768]{1,0:T(8,128)(2,1)S(1)} %bitcast.62), channel_id=1, source_target_pairs={{0,8},{8,0},{1,9},{9,1},{2,10},{10,2},{3,11},{11,3},{4,12},{12,4},... | collective-permute-start | bytes 1179656 | tf_op jit(solution)/shard_map/ppermute | solution.py:529
  114.2 7.2 %collective-permute-start.6 = (bf16[256,768]{1,0:T(8,128)(2,1)}, bf16[256,768]{1,0:T(8,128)(2,1)S(1)}, u32[]{:S(2)}, u32[]{:S(2)}) collective-permute-start(bf16[256,768]{1,0:T(8,128)(2,1)} %get-tuple-element.54.own_normed_ref), channel_id=1, source_target_pairs={{0,8},{8,0},{1,9},{9,1},{2,10},{10,2},{3,11},{11,3},{4,12},{12,4},... | collective-permute-start | bytes 1179656 | tf_op jit(solution)/shard_map/ppermute | solution.py:529
  116.0 13.4 %all-to-all-start.4 = ((bf16[16,64,128]{2,1,0:T(8,128)(2,1)}), bf16[16,64,128]{2,1,0:T(8,128)(2,1)S(1)}, u32[]{:S(2)}, u32[]{:S(2)}) async-start(bf16[16,64,128]{2,1,0:T(8,128)(2,1)} %bitcast.28), calls=%async_computation.4 | async-start | bytes 524288 | tf_op jit(solution)/shard_map/all_to_all | solution.py:533
  129.4 18.0 %copy-start.4 = (bf16[16,64,128]{2,1,0:T(8,128)(2,1)}, bf16[16,64,128]{2,1,0:T(8,128)(2,1)S(1)}, u32[]{:S(2)}) copy-start(bf16[16,64,128]{2,1,0:T(8,128)(2,1)S(1)} %all-to-all-done.4) | copy-start | bytes 786436
  129.4 45.3 %all-to-all-start.3 = ((bf16[64,64,384]{2,1,0:T(8,128)(2,1)}), bf16[64,64,384]{2,1,0:T(8,128)(2,1)}, u32[]{:S(2)}, u32[]{:S(2)}) async-start(bf16[64,64,384]{2,1,0:T(8,128)(2,1)} %bitcast.58), calls=%async_computation.3 | async-start | bytes 6291456 | tf_op jit(solution)/shard_map/all_to_all | solution.py:533
  148.2 23.4 %collective-permute-start.12 = (f32[2560]{0:T(1024)S(1)}, f32[2560]{0:T(1024)S(1)}, u32[]{:S(2)}, u32[]{:S(2)}) collective-permute-start(f32[2560]{0:T(1024)S(1)} %get-tuple-element.74), channel_id=1, source_target_pairs={{0,2},{2,0},{4,6},{6,4},{1,3},{3,1},{5,7},{7,5},{8,10},{10,8},{12,... | collective-permute-start | bytes 30728 | tf_op jit(solution)/shard_map/ppermute | solution.py:649
  179.1 8.3 %copy-start.13 = (bf16[128,16]{0,1:T(8,128)(2,1)S(1)}, bf16[128,16]{0,1:T(8,128)(2,1)}, u32[]{:S(2)}) copy-start(bf16[128,16]{0,1:T(8,128)(2,1)} %param.16) | copy-start | bytes 12292
  179.1 49.2 %all-to-all-start.5 = ((bf16[64,72,384]{2,1,0:T(8,128)(2,1)}), bf16[64,72,384]{2,1,0:T(8,128)(2,1)S(1)}, u32[]{:S(2)}, u32[]{:S(2)}) async-start(bf16[64,72,384]{2,1,0:T(8,128)(2,1)} %shard_map.166), calls=%async_computation.5 | async-start | bytes 7077888 | tf_op jit(solution)/shard_map/all_to_all | solution.py:533
  228.3 7.5 %copy-start.2 = (bf16[64,72,384]{2,1,0:T(8,128)(2,1)}, bf16[64,72,384]{2,1,0:T(8,128)(2,1)S(1)}, u32[]{:S(2)}) copy-start(bf16[64,72,384]{2,1,0:T(8,128)(2,1)S(1)} %all-to-all-done.5.block_ref) | copy-start | bytes 10616836
  228.3 14.9 %collective-permute-start.13 = (bf16[64,72,384]{2,1,0:T(8,128)(2,1)S(1)}, bf16[64,72,384]{2,1,0:T(8,128)(2,1)}, u32[]{:S(2)}, u32[]{:S(2)}) collective-permute-start(bf16[64,72,384]{2,1,0:T(8,128)(2,1)S(1)} %all-to-all-done.5.block_ref), channel_id=1, source_target_pairs={{0,8},{8,0},{1,9},{9,1},{2,10},{10,2},{3,11},{11,3},{4,12},{12,4},... | collective-permute-start | bytes 10616840 | tf_op jit(solution)/shard_map/ppermute | solution.py:529
  235.1 4.5 %collective-permute-start.14 = (f32[8,2,8,384]{3,2,1,0:T(8,128)}, f32[8,2,8,384]{3,2,1,0:T(8,128)S(1)}, u32[]{:S(2)}, u32[]{:S(2)}) collective-permute-start(f32[8,2,8,384]{3,2,1,0:T(8,128)} %shard_map.169.mine_ref), channel_id=1, source_target_pairs={{0,8},{8,0},{1,9},{9,1},{2,10},{10,2},{3,11},{11,3},{4,12},{12,4},... | collective-permute-start | bytes 589832 | tf_op jit(solution)/shard_map/ppermute | solution.py:529
  243.1 4.1 %copy-start.1 = (bf16[128,64,128]{2,1,0:T(8,128)(2,1)S(1)}, bf16[128,64,128]{2,1,0:T(8,128)(2,1)}, u32[]{:S(2)}) copy-start(bf16[128,64,128]{2,1,0:T(8,128)(2,1)} %param.15) | copy-start | bytes 6291460
  (7 other events, 11.3 us)
